TPU v7x, 32 devices: a whole 2x2x4 slice. The times are simulated.
32 devices in a mesh: area: 2 (over x), row: 4 (over z), col: 4 (over y, core).
Axes of the slice: x: 2, y: 2, z: 4, core: 2. Of those that a mesh axis runs over, the one named last changes fastest.
Arguments:
- area_xy: float32 [2, 4096], P(None, 'area'), as said below
- sampling_var: float32 [4096], P('area'), may hold values from 8 to 128
- inducer_xy: float32 [2, 8192], replicated, as said below
- order: int32 [8192], replicated, may hold values from 0 to 8191, each once
- prior: float32 [8192], P(('row', 'col')), may hold values from 1 to 10
Outputs:
- panel_rows: float32 [512, 8192], P(None, ('row', 'col'))
- schur: float32 [8192, 8192], P('area', ('row', 'col'))
Inputs may be any that keep to these rules, and one draw needn't show every extreme that they name: order names each Gram index's inducing point, each of 0 to 8191 once. `area_xy`: each area's coordinates lie between 0 and 12 / sqrt(8192). `inducer_xy`: each inducing point's coordinates lie between 0 and 12 / sqrt(8192).
All inputs are finite; a program needn't handle non-finite values.
Results may differ from a plain program's by a relative error of at most 0.00068.
Values sent between devices are 32-bit elements; how exact they have to be, the bound alone decides.
No kernel may reach another device: no remote copies, remote signals or barrier semaphores. Data moves between devices by JAX's collectives and lax.ppermute only.
A program may use at most 128 MiB of HBM per device.

v0:
```python
import math

import jax
import jax.numpy as jnp
from jax import lax
from jax.sharding import PartitionSpec as P

NB = 512


def from_root(array, axis, root):
    mine = lax.axis_index(axis) == root
    return lax.psum(jnp.where(mine, array, jnp.zeros_like(array)), axis)


def kernel_rows(coords, weights_root, points, length_scale):
    delta_x = coords[0][:, None] - points[0][None, :]
    delta_y = coords[1][:, None] - points[1][None, :]
    distance = jnp.sqrt(delta_x * delta_x + delta_y * delta_y)
    return (weights_root[:, None] * jnp.exp(-distance / length_scale)).astype(jnp.bfloat16)


def area_gram(coords, weights_root, left_points, right_points, length_scale):
    total_areas = coords.shape[1]
    block = max(min(256, total_areas), total_areas // 16)

    def accumulate(step_index, running):
        first_area = step_index * block
        coords_part = lax.dynamic_slice_in_dim(coords, first_area, block, 1)
        weights_part = lax.dynamic_slice_in_dim(weights_root, first_area, block, 0)
        left_rows = kernel_rows(coords_part, weights_part, left_points, length_scale)
        right_rows = kernel_rows(coords_part, weights_part, right_points, length_scale)
        return running + lax.dot_general(
            left_rows, right_rows, (((0,), (0,)), ((), ())), preferred_element_type=jnp.float32
        )

    initial = jnp.zeros((left_points.shape[1], right_points.shape[1]), jnp.float32)
    return lax.fori_loop(0, total_areas // block, accumulate, initial)


def per_device(area_xy, sampling_var, inducer_xy, order, prior):
    size_total = order.shape[0]
    length_scale = 2.0 / math.sqrt(size_total)
    col_width = prior.shape[0]
    row_height = size_total // lax.axis_size("area")
    area_index = lax.axis_index("area")
    block_index = lax.axis_index("row") * lax.axis_size("col") + lax.axis_index("col")
    column_ids = lax.dynamic_slice_in_dim(order, block_index * col_width, col_width, 0)
    column_points = jnp.take(inducer_xy, column_ids, axis=1)
    weights_root = jnp.sqrt(1.0 / (0.5 + sampling_var))
    areas_total = area_xy.shape[1] * lax.axis_size("area")
    scale_factor = size_total / areas_total
    row_points = jnp.take(inducer_xy, order, axis=1)
    gram = lax.psum_scatter(
        area_gram(area_xy, weights_root, row_points, column_points, length_scale),
        "area",
        scatter_dimension=0,
        tiled=True,
    )
    global_rows = area_index * row_height + lax.broadcasted_iota(
        jnp.int32, (row_height, col_width), 0
    )
    global_cols = block_index * col_width + lax.broadcasted_iota(
        jnp.int32, (row_height, col_width), 1
    )
    precision = gram * scale_factor + jnp.where(global_rows == global_cols, prior[None, :], 0.0)
    top_block = from_root(precision[:NB, :], "area", 0)
    joined_cols = lax.all_gather(top_block, "col", axis=1, tiled=True)
    diagonal = from_root(joined_cols[:, :NB], "row", 0)
    lower = jnp.linalg.cholesky(diagonal)
    inverse = jax.scipy.linalg.solve_triangular(lower, jnp.eye(NB, dtype=jnp.float32), lower=True)
    panel_rows = jnp.dot(
        inverse, top_block, precision=lax.Precision.HIGHEST, preferred_element_type=jnp.float32
    )
    whole_panel = lax.all_gather(panel_rows, ("row", "col"), axis=1, tiled=True)
    own_panel = lax.dynamic_slice_in_dim(whole_panel, area_index * row_height, row_height, 1)
    update = lax.dot_general(
        own_panel,
        panel_rows,
        (((0,), (0,)), ((), ())),
        precision=lax.Precision.HIGHEST,
        preferred_element_type=jnp.float32,
    )
    return (panel_rows, precision - update)


def solution(mesh):
    in_specs = (P(None, "area"), P("area"), P(), P(), P(("row", "col")))
    out_specs = (P(None, ("row", "col")), P("area", ("row", "col")))
    return jax.shard_map(
        per_device, mesh=mesh, in_specs=in_specs, out_specs=out_specs, check_vma=False
    )
```

profile of v0, /device:TPU:0, one launch (start us, length us, event | category | flops | bytes accessed | tf_op | source)
XLA Modules:
  0.0 842.3 jit_solution(11432866185492326781)
XLA Ops:
  9.6 3.4 copy.7
  13.0 3.2 gather_fusion.1
  16.5 29.9 %gather_fusion = f32[8192,2]{1,0:T(8,128)} fusion(f32[2,8192]{0,1:T(8,128)} %copy.7, s32[8192]{0:T(1024)S(1)} %fusion.55), kind=kCustom, calls=%fused_computation | custom fusion | bytes 163840 | tf_op jit(solution)/shard_map/jit(_take)/gather | solution.py:53
  46.3 7.4 select_bitcast_fusion
  53.8 2.8 copy.9
  56.6 112.6 %while.16 = (s32[]{:T(128)}, f32[8192,512]{1,0:T(8,128)}, f32[2048]{0:T(1024)S(1)}, f32[2,2048]{1,0:T(2,128)}, f32[2,8192]{1,0:T(2,128)S(1)}, /*index=5*/f32[2,5...) while((s32[]{:T(128)}, f32[8192,512]{1,0:T(8,128)}, ...), condition=%wide.region_1.2_spmd.clone, body=%wide.region_0.1_spmd.clone.sunk | while | flops 2175926272 | bytes 33772732 | solution.py:38
  57.6 10.2 %select_add_fusion.3 = f32[8192,512]{1,0:T(8,128)} fusion(f32[8192,512]{1,0:T(8,128)} %get-tuple-element.281, pred[]{:T(512)S(6)} %compare.46, f32[8192]{0:T(1024)S(1)} %bitcast.71, f32[256]{0:T(256)S(1)} %bitcast.75, f32[8192]{0:T(1024)S(1)} %bitcast.70, f32[256]{0:T(256)S(1)} %bitcast.74, f32[256]{0:T(256)S(1)} %dynamic_slice.31, ...), kind=kOutput, calls=%fused_computation.4.clone.1 | convolution fusion | flops 2175926272 | bytes 33627136 | tf_op jit(solution)/shard_map/while/body/eval_jaxpr/dot_general | solution.py:33
  68.8 13.5 %select_add_fusion.3 = f32[8192,512]{1,0:T(8,128)} fusion(f32[8192,512]{1,0:T(8,128)} %get-tuple-element.281, pred[]{:T(512)S(6)} %compare.46, f32[8192]{0:T(1024)S(1)} %bitcast.71, f32[256]{0:T(256)S(1)} %bitcast.75, f32[8192]{0:T(1024)S(1)} %bitcast.70, f32[256]{0:T(256)S(1)} %bitcast.74, f32[256]{0:T(256)S(1)} %dynamic_slice.31, ...), kind=kOutput, calls=%fused_computation.4.clone.1 | convolution fusion | flops 2175926272 | bytes 33627136 | tf_op jit(solution)/shard_map/while/body/eval_jaxpr/dot_general | solution.py:33
  83.3 13.5 %select_add_fusion.3 = f32[8192,512]{1,0:T(8,128)} fusion(f32[8192,512]{1,0:T(8,128)} %get-tuple-element.281, pred[]{:T(512)S(6)} %compare.46, f32[8192]{0:T(1024)S(1)} %bitcast.71, f32[256]{0:T(256)S(1)} %bitcast.75, f32[8192]{0:T(1024)S(1)} %bitcast.70, f32[256]{0:T(256)S(1)} %bitcast.74, f32[256]{0:T(256)S(1)} %dynamic_slice.31, ...), kind=kOutput, calls=%fused_computation.4.clone.1 | convolution fusion | flops 2175926272 | bytes 33627136 | tf_op jit(solution)/shard_map/while/body/eval_jaxpr/dot_general | solution.py:33
  97.8 13.5 %select_add_fusion.3 = f32[8192,512]{1,0:T(8,128)} fusion(f32[8192,512]{1,0:T(8,128)} %get-tuple-element.281, pred[]{:T(512)S(6)} %compare.46, f32[8192]{0:T(1024)S(1)} %bitcast.71, f32[256]{0:T(256)S(1)} %bitcast.75, f32[8192]{0:T(1024)S(1)} %bitcast.70, f32[256]{0:T(256)S(1)} %bitcast.74, f32[256]{0:T(256)S(1)} %dynamic_slice.31, ...), kind=kOutput, calls=%fused_computation.4.clone.1 | convolution fusion | flops 2175926272 | bytes 33627136 | tf_op jit(solution)/shard_map/while/body/eval_jaxpr/dot_general | solution.py:33
  112.3 13.5 %select_add_fusion.3 = f32[8192,512]{1,0:T(8,128)} fusion(f32[8192,512]{1,0:T(8,128)} %get-tuple-element.281, pred[]{:T(512)S(6)} %compare.46, f32[8192]{0:T(1024)S(1)} %bitcast.71, f32[256]{0:T(256)S(1)} %bitcast.75, f32[8192]{0:T(1024)S(1)} %bitcast.70, f32[256]{0:T(256)S(1)} %bitcast.74, f32[256]{0:T(256)S(1)} %dynamic_slice.31, ...), kind=kOutput, calls=%fused_computation.4.clone.1 | convolution fusion | flops 2175926272 | bytes 33627136 | tf_op jit(solution)/shard_map/while/body/eval_jaxpr/dot_general | solution.py:33
  126.8 13.5 %select_add_fusion.3 = f32[8192,512]{1,0:T(8,128)} fusion(f32[8192,512]{1,0:T(8,128)} %get-tuple-element.281, pred[]{:T(512)S(6)} %compare.46, f32[8192]{0:T(1024)S(1)} %bitcast.71, f32[256]{0:T(256)S(1)} %bitcast.75, f32[8192]{0:T(1024)S(1)} %bitcast.70, f32[256]{0:T(256)S(1)} %bitcast.74, f32[256]{0:T(256)S(1)} %dynamic_slice.31, ...), kind=kOutput, calls=%fused_computation.4.clone.1 | convolution fusion | flops 2175926272 | bytes 33627136 | tf_op jit(solution)/shard_map/while/body/eval_jaxpr/dot_general | solution.py:33
  141.3 13.5 %select_add_fusion.3 = f32[8192,512]{1,0:T(8,128)} fusion(f32[8192,512]{1,0:T(8,128)} %get-tuple-element.281, pred[]{:T(512)S(6)} %compare.46, f32[8192]{0:T(1024)S(1)} %bitcast.71, f32[256]{0:T(256)S(1)} %bitcast.75, f32[8192]{0:T(1024)S(1)} %bitcast.70, f32[256]{0:T(256)S(1)} %bitcast.74, f32[256]{0:T(256)S(1)} %dynamic_slice.31, ...), kind=kOutput, calls=%fused_computation.4.clone.1 | convolution fusion | flops 2175926272 | bytes 33627136 | tf_op jit(solution)/shard_map/while/body/eval_jaxpr/dot_general | solution.py:33
  155.8 13.5 %select_add_fusion.3 = f32[8192,512]{1,0:T(8,128)} fusion(f32[8192,512]{1,0:T(8,128)} %get-tuple-element.281, pred[]{:T(512)S(6)} %compare.46, f32[8192]{0:T(1024)S(1)} %bitcast.71, f32[256]{0:T(256)S(1)} %bitcast.75, f32[8192]{0:T(1024)S(1)} %bitcast.70, f32[256]{0:T(256)S(1)} %bitcast.74, f32[256]{0:T(256)S(1)} %dynamic_slice.31, ...), kind=kOutput, calls=%fused_computation.4.clone.1 | convolution fusion | flops 2175926272 | bytes 33627136 | tf_op jit(solution)/shard_map/while/body/eval_jaxpr/dot_general | solution.py:33
  169.3 17.5 %copy.11 = f32[8192,512]{0,1:T(8,128)} copy(f32[8192,512]{1,0:T(8,128)} %get-tuple-element.111) | data formatting | bytes 33554432 | tf_op jit(solution)/shard_map/while | solution.py:38
  186.9 191.9 %reduce-scatter.2.cloned.1.call-done = f32[4096,512]{0,1:T(8,128)} async-done(((f32[8192,512]{0,1:T(8,128)}), f32[4096,512]{0,1:T(8,128)}) %reduce-scatter.2.cloned.1.call-update) | async-done | bytes 8388624 | tf_op jit(solution)/shard_map/reduce_scatter | solution.py:54
  378.8 4.3 select_add_fusion.1
  383.1 3.4 copy-done
  387.6 40.1 %all-reduce.4.cloned.1.call-done = f32[512,512]{0,1:T(8,128)} async-done(((f32[512,512]{0,1:T(8,128)}), f32[512,512]{0,1:T(8,128)}) %all-reduce.4.cloned.1.call-update) | async-done | bytes 1048592 | tf_op jit(solution)/shard_map/psum | solution.py:13
  427.8 36.0 %all-gather.3.cloned.1.call-done = f32[512,2048]{0,1:T(8,128)} async-done(((f32[512,512]{0,1:T(8,128)}), f32[512,2048]{0,1:T(8,128)}) %all-gather.3.cloned.1.call-update) | async-done | bytes 4194320 | tf_op jit(solution)/shard_map/all_gather | solution.py:68
  463.9 2.3 slice_select_fusion
  467.3 51.2 %all-reduce.6.cloned.1.call-done = f32[512,512]{0,1:T(8,128)} async-done(((f32[512,512]{0,1:T(8,128)}), f32[512,512]{0,1:T(8,128)}) %all-reduce.6.cloned.1.call-update) | async-done | bytes 1048592 | tf_op jit(solution)/shard_map/psum | solution.py:13
  518.5 1.6 copy.12
  520.1 1.4 fusion.26
  522.5 11.7 %cholesky.103 = f32[128,128]{1,0:T(8,128)S(1)} custom-call(f32[128,128]{1,0:T(8,128)S(1)} %cholesky.263), custom_call_target="Cholesky" | custom-call | tf_op jit(solution)/shard_map/jit(cholesky)/cholesky | solution.py:70
  534.2 9.8 %custom-call.31 = f32[1,128,128]{1,2,0:T(8,128)S(1)} custom-call(f32[1,128,128]{2,1,0:T(8,128)S(1)} %get-tuple-element.188), custom_call_target="InvertDiagBlocksLowerTriangular" | custom-call | tf_op jit(solution)/shard_map/jit(cholesky)/cholesky | solution.py:70
  544.1 1.2 fusion.41
  545.3 1.3 convolution_subtract_fusion.3
  546.6 11.7 %cholesky.215 = f32[128,128]{1,0:T(8,128)S(1)} custom-call(f32[128,128]{1,0:T(8,128)S(1)} %cholesky.267), custom_call_target="Cholesky" | custom-call | tf_op jit(solution)/shard_map/jit(cholesky)/cholesky | solution.py:70
  559.9 10.6 %custom-call.32 = f32[1,128,128]{1,2,0:T(8,128)} custom-call(f32[1,128,128]{2,1,0:T(8,128)S(1)} %get-tuple-element.186), custom_call_target="InvertDiagBlocksLowerTriangular" | custom-call | tf_op jit(solution)/shard_map/jit(cholesky)/cholesky | solution.py:70
  573.5 1.5 convolution_subtract_fusion.4
  575.0 11.7 %cholesky.236 = f32[128,128]{1,0:T(8,128)S(1)} custom-call(f32[128,128]{1,0:T(8,128)S(1)} %cholesky.272), custom_call_target="Cholesky" | custom-call | tf_op jit(solution)/shard_map/jit(cholesky)/cholesky | solution.py:70
  586.9 9.8 %custom-call.33 = f32[1,128,128]{1,2,0:T(8,128)S(1)} custom-call(f32[1,128,128]{2,1,0:T(8,128)S(1)} %get-tuple-element.184), custom_call_target="InvertDiagBlocksLowerTriangular" | custom-call | tf_op jit(solution)/shard_map/jit(cholesky)/cholesky | solution.py:70
  597.0 1.3 convolution_subtract_fusion.5
  598.4 12.1 %cholesky.253 = f32[128,128]{1,0:T(8,128)S(1)} custom-call(f32[128,128]{1,0:T(8,128)S(1)} %convolution_subtract_fusion.5), custom_call_target="Cholesky" | custom-call | tf_op jit(solution)/shard_map/jit(cholesky)/cholesky | solution.py:70
  616.3 14.5 %while.15 = (s32[]{:T(128)}, f32[512,512]{0,1:T(8,128)}, s32[4,2]{0,1:T(2,128)S(1)}, f32[4,128,128]{2,1,0:T(8,128)}, s32[]{:T(128)}) while((s32[]{:T(128)}, f32[512,512]{0,1:T(8,128)}, s32[4,2]{0,1:T(2,128)S(1)}, f32[4,128,128]{2,1,0:T(8,128)}, s32[]{:T(128)}) %tuple.70), condition=%wide.while_cond, body=%wide.while_body.sunk | while | flops 2 | bytes 393829 | solution.py:71
  616.9 2.2 dynamic-slice.13
  620.6 2.2 dynamic-slice.13
  624.2 2.2 dynamic-slice.13
  627.9 2.2 dynamic-slice.13
  630.8 40.1 %custom-call.34 = f32[4,128,128]{1,2,0:T(8,128)S(1)} custom-call(f32[4,128,128]{2,1,0:T(8,128)} %get-tuple-element.119), custom_call_target="InvertDiagBlocksLowerTriangular" | custom-call | tf_op jit(solution)/shard_map/jit(_solve_triangular)/triangular_solve | solution.py:71
  672.0 1.3 convolution_subtract_fusion.1
  673.7 1.4 convolution_subtract_fusion
  675.5 1.6 convolution_subtract_fusion.2
  677.6 2.8 fusion.18
  680.4 126.5 %all-gather.5.cloned.1.call-done = f32[512,8192]{1,0:T(8,128)} async-done(((f32[512,512]{1,0:T(8,128)}), f32[512,8192]{1,0:T(8,128)}) %all-gather.5.cloned.1.call-update) | async-done | bytes 16777232 | tf_op jit(solution)/shard_map/all_gather | solution.py:75
  806.9 19.8 %fusion.15 = f32[4096,512]{0,1:T(8,128)} fusion(f32[4096,512]{0,1:T(8,128)} %copy-done, f32[512,512]{1,0:T(8,128)} %fusion.18, f32[512,8192]{1,0:T(8,128)} %all-gather.5.cloned.1.call-done, s32[]{:T(128)S(6)} %select_n.65), kind=kOutput, calls=%fused_computation.24 | convolution fusion | flops 12886999040 | bytes 26214404 | tf_op jit(solution)/shard_map/dot_general | solution.py:77
  826.7 8.9 %copy.22 = f32[4096,512]{1,0:T(8,128)} copy(f32[4096,512]{0,1:T(8,128)} %fusion.15) | data formatting | bytes 16777216
  (110 shorter events, 30.0 us)
Async XLA Ops:
  7.2 371.6 %reduce-scatter.2.cloned.1.call-start = ((), (), s32[]{:S(2)}) async-start(), calls=%async_computation.1 | async-start | bytes 25165824 | tf_op jit(solution)/shard_map/reduce_scatter | solution.py:54
  9.6 47.1 %copy-start.3 = (f32[2048]{0:T(1024)S(1)}, f32[2048]{0:T(1024)}, u32[]{:S(2)}) copy-start(f32[2048]{0:T(1024)} %param.8) | copy-start | bytes 24580
  186.8 192.0 %copy-start.4 = (f32[512]{0:T(512)S(1)}, f32[512]{0:T(512)}, u32[]{:S(2)}) copy-start(f32[512]{0:T(512)} %param.11) | copy-start | bytes 6148
  186.8 241.0 %all-reduce.4.cloned.1.call-start = ((), (), s32[]{:S(2)}) async-start(), calls=%async_computation.2 | async-start | bytes 2097152 | tf_op jit(solution)/shard_map/psum | solution.py:13
  383.1 3.4 copy-start
  387.6 76.3 %all-gather.3.cloned.1.call-start = ((), (), s32[]{:S(2)}) async-start(), calls=%async_computation.3 | async-start | bytes 5242880 | tf_op jit(solution)/shard_map/all_gather | solution.py:68
  427.8 90.7 %all-reduce.6.cloned.1.call-start = ((), (), s32[]{:S(2)}) async-start(), calls=%async_computation.4 | async-start | bytes 2097152 | tf_op jit(solution)/shard_map/psum | solution.py:13
  466.2 340.7 %all-gather.5.cloned.1.call-start = ((), (), s32[]{:S(2)}) async-start(), calls=%async_computation.5 | async-start | bytes 17825792 | tf_op jit(solution)/shard_map/all_gather | solution.py:75
  521.5 1.0 copy-start.2
  522.5 155.1 %copy-start.1 = (f32[512,512]{0,1:T(8,128)S(1)}, f32[512,512]{0,1:T(8,128)}, u32[]{:S(2)}) copy-start(f32[512,512]{0,1:T(8,128)} %all-reduce.4.cloned.1.call-done) | copy-start | bytes 3145732
Sparse Core Ops, SparseCore 0:
  186.9 191.8 reduce-scatter.1
  387.7 40.0 all-reduce.3
  429.3 34.4 all-gather.2
  466.6 51.8 all-reduce.5
  680.5 126.2 all-gather.4
where the time goes:
time: 850 us; the launch traced here: 842 us
  waiting for transfers between devices  446 us (52%)
  other arithmetic  141 us (17%)
  matrix products  141 us (17%)
  local copies, waits for them, and re-layouts  97.6 us (11%)
  between operations  16.8 us (2%)
    reduce_scatter x1, waiting for transfers between devices, per_device(): lax.psum_scatter(area_gram(area_xy, weights_root, row_points, column_poin...  192 us
    all_gather x1, waiting for transfers between devices, per_device(): whole_panel = lax.all_gather(panel_rows, ('row', 'col'), axis=1, tiled=True)  126 us
    dot_general x8, matrix products, accumulate(): lax.dot_general(left_rows, right_rows, (((0,), (0,)), ((), ())), preferre...  105 us
    psum x2, waiting for transfers between devices, from_root(): return lax.psum(jnp.where(mine, array, jnp.zeros_like(array)), axis)  91.3 us
    another operation x14, other arithmetic, per_device(): lower = jnp.linalg.cholesky(diagonal)  79.6 us
    another operation x3, other arithmetic, per_device(): jax.scipy.linalg.solve_triangular(lower, jnp.eye(NB, dtype=jnp.float32),...  41.2 us
    all_gather x1, waiting for transfers between devices, per_device(): joined_cols = lax.all_gather(top_block, 'col', axis=1, tiled=True)  36 us
    gather x1, local copies, waits for them, and re-layouts, per_device(): row_points = jnp.take(inducer_xy, order, axis=1)  29.9 us
  transfers between devices with their start and end apart: 5, of which 5 were waited for; matrix products, arithmetic and copies ran while one was open for 0% of the time, Pallas kernels for 0%

commit v1 on v0

v1 whole, which is shorter than its diff:
```python
import functools
import math

import jax
import jax.numpy as jnp
from jax import lax
from jax.experimental import pallas as pl
from jax.experimental.pallas import tpu as pltpu
from jax.sharding import PartitionSpec as P

NB = 512
LANES = 128
STRIP = 8
BLK = 128
CHUNK = 512
VMEM_BYTES = 60 * 1024 * 1024
HIGH = lax.Precision.HIGHEST
F32 = jnp.float32
BF16 = jnp.bfloat16


def split_pieces(value):
    first = value.astype(BF16)
    rest = value - first.astype(F32)
    second = rest.astype(BF16)
    third = (rest - second.astype(F32)).astype(BF16)
    return first, second, third


def nt_dot(left, right, precision=None):
    return lax.dot_general(
        left, right, (((1,), (1,)), ((), ())), precision=precision, preferred_element_type=F32
    )


def tn_dot(left, right, precision=None):
    return lax.dot_general(
        left, right, (((0,), (0,)), ((), ())), precision=precision, preferred_element_type=F32
    )


def block_position():
    return lax.axis_index("row") * lax.axis_size("col") + lax.axis_index("col")


def points_kernel(scale, starts_ref, order_ref, table_ref, x_ref, y_ref, columns_ref):
    tables = table_ref[...]
    quotients = tables.shape[1]
    pieces_x = split_pieces(tables[0] * scale)
    pieces_y = split_pieces(tables[1] * scale)
    columns_ref[...] = jnp.concatenate(
        [jnp.concatenate(pieces_x, axis=0), jnp.concatenate(pieces_y, axis=0)], axis=1
    ).T
    quotient_ids = lax.broadcasted_iota(jnp.int32, (quotients, LANES), 0)
    lane_ids = lax.broadcasted_iota(jnp.int32, (LANES, LANES), 0)
    on_diagonal = lane_ids == lax.broadcasted_iota(jnp.int32, (LANES, LANES), 1)
    ones = jnp.ones((3 * LANES, LANES), BF16)

    def spread(row):
        diagonals = [
            jnp.where(on_diagonal, jnp.broadcast_to(piece.astype(F32), (LANES, LANES)), 0.0)
            for piece in split_pieces(row)
        ]
        return jnp.dot(
            jnp.concatenate(diagonals, axis=1).astype(BF16), ones, preferred_element_type=F32
        )

    def one_block(step, carry):
        row = jnp.where(
            step < starts_ref[0],
            step,
            jnp.where(
                step < starts_ref[1], starts_ref[2] + step - starts_ref[0], starts_ref[3] + step - starts_ref[1]
            ),
        )
        ids = order_ref[pl.ds(row, 1), :]
        hit = jnp.where(quotient_ids == lax.shift_right_logical(ids, 7), 1.0, 0.0).astype(BF16)
        values = jnp.dot(
            columns_ref[...], jnp.concatenate([hit, hit, hit], axis=0), preferred_element_type=F32
        )
        mine = lane_ids == lax.bitwise_and(ids, LANES - 1)
        rows = pl.ds(pl.multiple_of(step * LANES, LANES), LANES)
        x_ref[rows, :] = spread(jnp.sum(jnp.where(mine, values[:LANES], 0.0), axis=0, keepdims=True))
        y_ref[rows, :] = spread(jnp.sum(jnp.where(mine, values[LANES:], 0.0), axis=0, keepdims=True))
        return carry

    lax.fori_loop(0, x_ref.shape[0] // LANES, one_block, 0)


def gram_points(order, inducer_xy, scale, col_width, row_height):
    quotients = order.shape[0] // LANES
    starts = jnp.stack(
        [
            jnp.int32(NB // LANES),
            jnp.int32((NB + col_width) // LANES),
            block_position() * (col_width // LANES),
            lax.axis_index("area") * (row_height // LANES),
        ]
    ).astype(jnp.int32)
    count = NB + col_width + row_height
    shape = jax.ShapeDtypeStruct((count, LANES), F32)
    return pl.pallas_call(
        functools.partial(points_kernel, scale),
        out_shape=(shape, shape),
        in_specs=[
            pl.BlockSpec(memory_space=pltpu.SMEM),
            pl.BlockSpec(memory_space=pltpu.VMEM),
            pl.BlockSpec(memory_space=pltpu.VMEM),
        ],
        out_specs=[pl.BlockSpec(memory_space=pltpu.VMEM)] * 2,
        scratch_shapes=[pltpu.VMEM((2 * LANES, 3 * quotients), BF16)],
        compiler_params=pltpu.CompilerParams(vmem_limit_bytes=VMEM_BYTES),
        name="points",
    )(starts, order.reshape(quotients, LANES), inducer_xy.reshape(2, quotients, LANES))


def fill_kernel(dest, dest_area, x_ref, y_ref, first_row, row_count, area_ref, first_area, area_count):
    for pair in range(area_count // 256):
        areas = []
        for half in range(2):
            lanes = pl.ds(first_area + pair * 256 + half * LANES, LANES)
            areas.append(
                [jnp.broadcast_to(area_ref[k : k + 1, lanes], (16, LANES)) for k in range(3)]
            )
        for group in range(row_count // 16):
            rows = pl.ds(first_row + group * 16, 16)
            point_x, point_y = x_ref[rows, :], y_ref[rows, :]
            for half in range(2):
                area_x, area_y, log_weight = areas[half]
                delta_x, delta_y = area_x - point_x, area_y - point_y
                square = jnp.maximum(delta_x * delta_x + delta_y * delta_y, 1e-30)
                value = jnp.exp2(log_weight - square * lax.rsqrt(square))
                dest[
                    pl.ds(group * 16, 16), pl.ds(dest_area + pair * 256 + half * LANES, LANES)
                ] = value.astype(BF16)


def head_kernel(
    factor, offset_ref, x_ref, y_ref, area_ref, first_prior_ref, prior_ref, head_ref, cols_ref, system_ref
):
    col_width = cols_ref.shape[0]
    total = area_ref.shape[1]
    system_ref[...] = jnp.zeros_like(system_ref)

    def step(index, carry):
        first = pl.multiple_of(index * CHUNK, CHUNK)
        here = pl.ds(first, CHUNK)
        fill_kernel(head_ref, first, x_ref, y_ref, 0, NB, area_ref, first, CHUNK)
        fill_kernel(cols_ref, first, x_ref, y_ref, NB, col_width, area_ref, first, CHUNK)
        left = head_ref[:, here]
        system_ref[:, :NB] += nt_dot(left, left)
        system_ref[:, NB:] += nt_dot(left, cols_ref[:, here])
        return carry

    lax.fori_loop(0, total // CHUNK, step, 0)
    rows = lax.broadcasted_iota(jnp.int32, (NB, NB), 0)
    cols = lax.broadcasted_iota(jnp.int32, (NB, NB), 1)
    system_ref[:, :NB] = system_ref[:, :NB] * factor + jnp.where(
        rows == cols, first_prior_ref[...], 0.0
    )
    rows = lax.broadcasted_iota(jnp.int32, (NB, col_width), 0)
    cols = lax.broadcasted_iota(jnp.int32, (NB, col_width), 1) + offset_ref[0]
    system_ref[:, NB:] = system_ref[:, NB:] * factor + jnp.where(rows == cols, prior_ref[...], 0.0)


def whole_row(value, index):
    return jnp.broadcast_to(value[index : index + 1, :], (STRIP, LANES))


def whole_lane(value, index):
    return jnp.broadcast_to(value[:, index : index + 1], (STRIP, LANES))


def inverse_factor(block_ref, inverse_ref):
    count = BLK // STRIP
    row_ids = lax.broadcasted_iota(jnp.int32, (STRIP, LANES), 0)
    lane_ids = lax.broadcasted_iota(jnp.int32, (STRIP, LANES), 1)
    tops = [block_ref[i * STRIP : (i + 1) * STRIP, :] for i in range(count)]
    units = [jnp.where(lane_ids == row_ids + i * STRIP, 1.0, 0.0).astype(F32) for i in range(count)]
    for p in range(count):
        diag_cols = [whole_lane(tops[p], p * STRIP + j) for j in range(STRIP)]
        entry = {
            (i, j): whole_row(diag_cols[j], i) for j in range(STRIP) for i in range(j, STRIP)
        }
        top_rows = [whole_row(tops[p], j) for j in range(STRIP)]
        unit_rows = [whole_row(units[p], j) for j in range(STRIP)]
        roots = []
        for j in range(STRIP):
            root = lax.rsqrt(entry[j, j])
            roots.append(root)
            for i in range(j + 1, STRIP):
                entry[i, j] = entry[i, j] * root
            for k in range(j + 1, STRIP):
                for i in range(k, STRIP):
                    entry[i, k] = entry[i, k] - entry[i, j] * entry[k, j]
        for j in range(STRIP):
            for k in range(j):
                top_rows[j] = top_rows[j] - entry[j, k] * top_rows[k]
                unit_rows[j] = unit_rows[j] - entry[j, k] * unit_rows[k]
            top_rows[j] = top_rows[j] * roots[j]
            unit_rows[j] = unit_rows[j] * roots[j]
        for i in range(p + 1, count):
            cols = [whole_lane(tops[i], p * STRIP + j) for j in range(STRIP)]
            top, unit = tops[i], units[i]
            for j in range(STRIP):
                for k in range(j):
                    cols[j] = cols[j] - cols[k] * entry[j, k]
                cols[j] = cols[j] * roots[j]
                top = top - cols[j] * top_rows[j]
                unit = unit - cols[j] * unit_rows[j]
            tops[i], units[i] = top, unit
        final = unit_rows[STRIP - 1]
        for j in range(STRIP - 1):
            final = jnp.where(row_ids == j, unit_rows[j], final)
        inverse_ref[p * STRIP : (p + 1) * STRIP, :] = final


def factor_kernel(system_ref, first_prior_ref, panel_ref, solved_ref, weighted_ref, work, block, inverses):
    count = NB // BLK
    work[...] = system_ref[...].reshape(work.shape)

    def eliminate(k, carry):
        block[...] = work[k, :, pl.ds(pl.multiple_of(k * BLK, BLK), BLK)]
        inverse_factor(block, inverses.at[k])
        row = jnp.dot(inverses[k], work[k], precision=HIGH, preferred_element_type=F32)
        work[k] = row
        for i in range(1, count):

            @pl.when(i > k)
            def _():
                work[i] -= tn_dot(row[:, i * BLK : (i + 1) * BLK], row, HIGH)

        return carry

    lax.fori_loop(0, count, eliminate, 0)
    for k in range(count - 1, -1, -1):
        mine = pl.ds(k * BLK, BLK)
        panel = work[k, :, NB:]
        panel_ref[mine, :] = panel
        if k < count - 1:
            panel = panel - jnp.dot(
                work[k, :, (k + 1) * BLK : NB],
                solved_ref[(k + 1) * BLK :, :],
                precision=HIGH,
                preferred_element_type=F32,
            )
        solved_ref[mine, :] = tn_dot(inverses[k], panel, HIGH)
    rows = lax.broadcasted_iota(jnp.int32, (NB, NB), 0)
    cols = lax.broadcasted_iota(jnp.int32, (NB, NB), 1)
    column = jnp.sum(jnp.where(rows == cols, first_prior_ref[...], 0.0), axis=1, keepdims=True)
    weighted_ref[...] = solved_ref[...] * column


def schur_kernel(
    factor,
    offset_ref,
    x_ref,
    y_ref,
    area_ref,
    prior_ref,
    head_ref,
    cols_ref,
    solved_ref,
    weighted_ref,
    out_ref,
    left_even,
    left_odd,
    residual,
):
    tile = pl.program_id(0)
    tiles = pl.num_programs(0)
    col_width = cols_ref.shape[0]
    total = area_ref.shape[1]
    steps = total // CHUNK
    first_points = NB + col_width
    tile_rows = out_ref.shape[0]

    @pl.when(tile == 0)
    def _():
        high = solved_ref[...].astype(BF16)
        low = (solved_ref[...] - high.astype(F32)).astype(BF16)

        def step(index, carry):
            first = pl.multiple_of(index * CHUNK, CHUNK)
            here = pl.ds(first, CHUNK)
            right = head_ref[:, here]
            removed = tn_dot(high, right) + tn_dot(low, right)
            residual[:, here] = (cols_ref[:, here].astype(F32) - removed).astype(BF16)
            fill_kernel(left_even, first, x_ref, y_ref, first_points, tile_rows, area_ref, first, CHUNK)
            return carry

        lax.fori_loop(0, steps, step, 0)

    def run(source, dest):
        out_ref[...] = jnp.zeros_like(out_ref)

        def step(index, carry):
            first = pl.multiple_of(index * CHUNK, CHUNK)
            here = pl.ds(first, CHUNK)
            out_ref[...] += nt_dot(source[:, here], residual[:, here])
            if dest is not None:
                next_row = pl.multiple_of(first_points + (tile + 1) * tile_rows, 16)
                fill_kernel(dest, first, x_ref, y_ref, next_row, tile_rows, area_ref, first, CHUNK)
            return carry

        lax.fori_loop(0, steps, step, 0)

    parity = lax.rem(tile, 2)
    more = tile < tiles - 1
    pl.when(jnp.logical_and(more, parity == 0))(lambda: run(left_even, left_odd))
    pl.when(jnp.logical_and(more, parity == 1))(lambda: run(left_odd, left_even))
    pl.when(jnp.logical_and(jnp.logical_not(more), parity == 0))(lambda: run(left_even, None))
    pl.when(jnp.logical_and(jnp.logical_not(more), parity == 1))(lambda: run(left_odd, None))

    rows = lax.broadcasted_iota(jnp.int32, (tile_rows, col_width), 0) + (offset_ref[1] + tile * tile_rows)
    cols = lax.broadcasted_iota(jnp.int32, (tile_rows, col_width), 1) + offset_ref[0]
    out_ref[...] = out_ref[...] * factor + jnp.where(rows == cols, prior_ref[...], 0.0)

    first_row = offset_ref[1] + tile * tile_rows

    @pl.when(first_row < NB)
    def _():
        out_ref[...] -= weighted_ref[pl.ds(pl.multiple_of(first_row, tile_rows), tile_rows), :]


def all_areas(array):
    axis = array.ndim - 1
    if lax.axis_size("area") == 2:
        other = lax.ppermute(array, "area", [(0, 1), (1, 0)])
        first = lax.axis_index("area") == 0
        return jnp.concatenate(
            [jnp.where(first, array, other), jnp.where(first, other, array)], axis=axis
        )
    return lax.all_gather(array, "area", axis=axis, tiled=True)


def per_device(area_xy, sampling_var, inducer_xy, order, prior):
    size_total = order.shape[0]
    length_scale = 2.0 / math.sqrt(size_total)
    scale = math.log2(math.e) / length_scale
    col_width = prior.shape[0]
    row_height = size_total // lax.axis_size("area")
    areas_total = area_xy.shape[1] * lax.axis_size("area")
    factor = size_total / areas_total

    own = jnp.concatenate([area_xy * scale, -0.5 * jnp.log2(0.5 + sampling_var)[None, :]], axis=0)
    areas = all_areas(own)
    first_prior = lax.all_gather(prior, ("row", "col"), axis=0, tiled=True)[:NB].reshape(1, NB)
    own_prior = prior.reshape(1, col_width)
    point_x, point_y = gram_points(order, inducer_xy, scale, col_width, row_height)
    offsets = jnp.stack(
        [block_position() * col_width, lax.axis_index("area") * row_height]
    ).astype(jnp.int32)

    tile_rows = min(row_height, 512 if areas_total <= 8192 else 256)
    smem = pl.BlockSpec(memory_space=pltpu.SMEM)
    vmem = pl.BlockSpec(memory_space=pltpu.VMEM)
    params = pltpu.CompilerParams(vmem_limit_bytes=VMEM_BYTES)
    head, cols, system = pl.pallas_call(
        functools.partial(head_kernel, factor),
        out_shape=(
            jax.ShapeDtypeStruct((NB, areas_total), BF16),
            jax.ShapeDtypeStruct((col_width, areas_total), BF16),
            jax.ShapeDtypeStruct((NB, NB + col_width), F32),
        ),
        in_specs=[smem] + [vmem] * 5,
        out_specs=[vmem] * 3,
        compiler_params=params,
        name="head",
    )(offsets, point_x, point_y, areas, first_prior, own_prior)
    panel_rows, solved, weighted = pl.pallas_call(
        factor_kernel,
        out_shape=(jax.ShapeDtypeStruct((NB, col_width), F32),) * 3,
        in_specs=[vmem] * 2,
        out_specs=[vmem] * 3,
        scratch_shapes=[
            pltpu.VMEM((NB // BLK, BLK, NB + col_width), F32),
            pltpu.VMEM((BLK, BLK), F32),
            pltpu.VMEM((NB // BLK, BLK, BLK), F32),
        ],
        compiler_params=params,
        name="factor",
    )(system, first_prior)
    schur = pl.pallas_call(
        functools.partial(schur_kernel, factor),
        grid=(row_height // tile_rows,),
        out_shape=jax.ShapeDtypeStruct((row_height, col_width), F32),
        in_specs=[smem] + [vmem] * 8,
        out_specs=pl.BlockSpec((tile_rows, col_width), lambda i: (i, 0)),
        scratch_shapes=[
            pltpu.VMEM((tile_rows, areas_total), BF16),
            pltpu.VMEM((tile_rows, areas_total), BF16),
            pltpu.VMEM((col_width, areas_total), BF16),
        ],
        compiler_params=params,
        name="schur",
    )(offsets, point_x, point_y, areas, own_prior, head, cols, solved, weighted)
    return (panel_rows, schur)


def solution(mesh):
    in_specs = (P(None, "area"), P("area"), P(), P(), P(("row", "col")))
    out_specs = (P(None, ("row", "col")), P("area", ("row", "col")))
    return jax.shard_map(
        per_device, mesh=mesh, in_specs=in_specs, out_specs=out_specs, check_vma=False
    )
```

time: 850 us -> 167 us (0.20)
  waiting for transfers between devices: 446 us -> 0.01 us
  matrix products: 141 us -> 0 us
  other arithmetic: 141 us -> 3.31 us
  Pallas kernels: 0 us -> 136 us
  local copies, waits for them, and re-layouts: 97.6 us -> 2.01 us
  blocking collectives: 0 us -> 22 us
  between operations: 16.8 us -> 0.65 us
    reduce_scatter x1 -> x0, waiting for transfers between devices: 192 us -> none  [per_device(): lax.psum_scatter(area_gram(area_xy, weights_root, row_points, column_poin...]
    all_gather x2 -> x0, waiting for transfers between devices: 162 us -> none  [the longest x1 126 us: per_device(): whole_panel = lax.all_gather(panel_rows, ('row', 'col'), axis=1, tiled=True)]
    pallas_call x0 -> x4, Pallas kernels: none -> 136 us  [the longest x1 69 us: per_device(): pl.pallas_call(functools.partial(schur_kernel, factor), grid=(row_height...]
    dot_general x10 -> x0, matrix products: 127 us -> none  [the longest x8 105 us: accumulate(): lax.dot_general(left_rows, right_rows, (((0,), (0,)), ((), ())), preferre...]
    another operation x17 -> x2, other arithmetic: 121 us -> 1.2 us  [the longest x1 0.61 us: per_device(): jnp.stack([block_position() * col_width, lax.axis_index('area') * row_hei...]
    psum x2 -> x0, waiting for transfers between devices: 91.3 us -> none  [from_root(): return lax.psum(jnp.where(mine, array, jnp.zeros_like(array)), axis)]
    gather x2 -> x0, local copies, waits for them, and re-layouts: 33.1 us -> none  [the longest x1 29.9 us: per_device(): row_points = jnp.take(inducer_xy, order, axis=1)]
    all_gather x0 -> x1, blocking collectives: none -> 22 us  [per_device(): lax.all_gather(prior, ('row', 'col'), axis=0, tiled=True)[:NB]]
  transfers between devices with their start and end apart: 5 -> 1, of which waited for: 5 -> 0; matrix products, arithmetic and copies ran while one was open for 0% -> 2% of each run, Pallas kernels for 0% -> 11%
where the time goes in v1:
time: 167 us
  Pallas kernels  136 us (81%)
  blocking collectives  22 us (13%)
  other arithmetic  3.31 us (2%)
  starting transfers between devices  3 us (2%)
  local copies, waits for them, and re-layouts  2.01 us (1%)
    pallas_call x1, Pallas kernels, per_device(): pl.pallas_call(functools.partial(schur_kernel, factor), grid=(row_height...  69 us
    pallas_call x1, Pallas kernels, per_device(): pl.pallas_call(factor_kernel, out_shape=(jax.ShapeDtypeStruct((NB, col_wi...  30.8 us
    all_gather x1, blocking collectives, per_device(): lax.all_gather(prior, ('row', 'col'), axis=0, tiled=True)[:NB]  22 us
    pallas_call x1, Pallas kernels, gram_points(): pl.pallas_call(functools.partial(points_kernel, scale), out_shape=(shape,...  19.1 us
    pallas_call x1, Pallas kernels, per_device(): pl.pallas_call(functools.partial(head_kernel, factor), out_shape=(jax.Sha...  17 us
  transfers between devices with their start and end apart: 1, of which 0 were waited for; matrix products, arithmetic and copies ran while one was open for 2% of the time, Pallas kernels for 11%

profile of v1, /device:TPU:0, one launch (start us, length us, event | category | flops | bytes accessed | tf_op | source)
XLA Modules:
  0.0 166.9 jit_solution(310878584250106498)
XLA Ops:
  0.6 0.7 log_multiply_fusion
  1.3 0.7 broadcast_multiply_fusion
  2.1 3.0 %collective-permute-start = (f32[3,2048]{1,0:T(4,128)S(1)}, f32[3,2048]{1,0:T(4,128)S(1)}, u32[]{:S(2)}, u32[]{:S(2)}) collective-permute-start(f32[3,2048]{1,0:T(4,128)S(1)} %pad_maximum_fusion.1), channel_id=1, source_target_pairs={{0,16},{16,0},{1,17},{17,1},{2,18},{18,2},{3,19},{19,3},{4,20},{20... | collective-permute-start | bytes 73736 | tf_op jit(solution)/shard_map/ppermute | solution.py:329
  5.1 22.0 %all-gather = f32[16,1,512]{2,1,0:T(1,128)S(1)} all-gather(f32[1,1,512]{2,1,0:T(1,128)} %bitcast.19), channel_id=1, replica_groups=mesh['area'=2,'row'=4,'col'=4] {'row','col'}, dimensions={0}, use_global_device_ids=true | all-gather | bytes 34816 | tf_op jit(solution)/shard_map/all_gather | solution.py:348
  27.0 0.5 slice_bitcast_fusion.first_prior_ref
  27.6 0.6 pad_add_fusion.offset_ref
  28.2 0.6 pad_add_fusion.1.starts_ref
  28.8 1.5 copy.9
  30.3 19.1 %points.1 = (f32[5120,128]{1,0:T(8,128)}, f32[5120,128]{1,0:T(8,128)}) custom-call(s32[4]{0:T(128)} %pad_add_fusion.1.starts_ref, s32[64,128]{1,0:T(8,128)} %bitcast.18, f32[2,64,128]{2,1,0:T(8,128)} %bitcast.14), custom_call_target="tpu_custom_call" | custom-call | tf_op jit(solution)/shard_map/points/pallas_call | solution.py:102
  49.4 0.0 collective-permute-done
  49.4 0.6 pad_maximum_fusion.area_ref
  50.1 17.0 %head.1 = (bf16[512,4096]{1,0:T(8,128)(2,1)}, bf16[512,4096]{1,0:T(8,128)(2,1)}, f32[512,1024]{1,0:T(8,128)}) custom-call(s32[2]{0:T(128)} %pad_add_fusion.offset_ref, f32[5120,128]{1,0:T(8,128)} %get-tuple-element.10.x_ref, f32[5120,128]{1,0:T(8,128)} %get-tuple-element.11.y_ref, f32[3,4096]{1,0:T(4,128)} %pad_maximum_fusion.area_ref, ...), custom_call_target="tpu_custom_call" | custom-call | tf_op jit(solution)/shard_map/head/pallas_call | solution.py:359
  67.1 30.8 %factor.1 = (f32[512,512]{1,0:T(8,128)}, f32[512,512]{1,0:T(8,128)}, f32[512,512]{1,0:T(8,128)}) custom-call(f32[512,1024]{1,0:T(8,128)} %get-tuple-element.12.system_ref, f32[1,512]{1,0:T(1,128)} %slice_bitcast_fusion.first_prior_ref), custom_call_target="tpu_custom_call" | custom-call | tf_op jit(solution)/shard_map/factor/pallas_call | solution.py:371
  97.9 69.0 %schur.1 = f32[4096,512]{1,0:T(8,128)} custom-call(s32[2]{0:T(128)} %pad_add_fusion.offset_ref, f32[5120,128]{1,0:T(8,128)} %get-tuple-element.10.x_ref, f32[5120,128]{1,0:T(8,128)} %get-tuple-element.11.y_ref, f32[3,4096]{1,0:T(4,128)} %pad_maximum_fusion.area_ref, f32[1,512]{1,0:T(1,128)} %bitcast.21, bf16[512,4096]{1,0:T(8,128)(2,1)} %get-tuple-element.14.head_ref, ...), custom_call_target="tpu_custom_call" | custom-call | tf_op jit(solution)/shard_map/schur/pallas_call | solution.py:384
  (2 shorter events, 0.0 us)
Async XLA Ops:
  2.1 47.3 %collective-permute-start = (f32[3,2048]{1,0:T(4,128)S(1)}, f32[3,2048]{1,0:T(4,128)S(1)}, u32[]{:S(2)}, u32[]{:S(2)}) collective-permute-start(f32[3,2048]{1,0:T(4,128)S(1)} %pad_maximum_fusion.1), channel_id=1, source_target_pairs={{0,16},{16,0},{1,17},{17,1},{2,18},{18,2},{3,19},{19,3},{4,20},{20... | collective-permute-start | bytes 73736 | tf_op jit(solution)/shard_map/ppermute | solution.py:329

commit v2 on v1

--- a/solution.py
+++ b/solution.py
@@ -12,7 +12,8 @@
 LANES = 128
 STRIP = 8
 BLK = 128
-CHUNK = 512
+CHUNK = 1024
+SPAN = 2048
 VMEM_BYTES = 60 * 1024 * 1024
 HIGH = lax.Precision.HIGHEST
 F32 = jnp.float32
@@ -65,7 +66,7 @@
             jnp.concatenate(diagonals, axis=1).astype(BF16), ones, preferred_element_type=F32
         )
 
-    def one_block(step, carry):
+    def one_block(step):
         row = jnp.where(
             step < starts_ref[0],
             step,
@@ -79,12 +80,22 @@
             columns_ref[...], jnp.concatenate([hit, hit, hit], axis=0), preferred_element_type=F32
         )
         mine = lane_ids == lax.bitwise_and(ids, LANES - 1)
-        rows = pl.ds(pl.multiple_of(step * LANES, LANES), LANES)
-        x_ref[rows, :] = spread(jnp.sum(jnp.where(mine, values[:LANES], 0.0), axis=0, keepdims=True))
-        y_ref[rows, :] = spread(jnp.sum(jnp.where(mine, values[LANES:], 0.0), axis=0, keepdims=True))
+        x_row = jnp.sum(jnp.where(mine, values[:LANES], 0.0), axis=0, keepdims=True)
+        y_row = jnp.sum(jnp.where(mine, values[LANES:], 0.0), axis=0, keepdims=True)
+        return spread(x_row), spread(y_row)
+
+    blocks = x_ref.shape[0] // LANES
+    unroll = next(count for count in (8, 7, 5, 4, 3, 2, 1) if blocks % count == 0)
+
+    def several(group, carry):
+        done = [one_block(group * unroll + i) for i in range(unroll)]
+        for i, (x_block, y_block) in enumerate(done):
+            rows = pl.ds(pl.multiple_of((group * unroll + i) * LANES, LANES), LANES)
+            x_ref[rows, :] = x_block
+            y_ref[rows, :] = y_block
         return carry
 
-    lax.fori_loop(0, x_ref.shape[0] // LANES, one_block, 0)
+    lax.fori_loop(0, blocks // unroll, several, 0)
 
 
 def gram_points(order, inducer_xy, scale, col_width, row_height):
@@ -129,14 +140,14 @@
                 area_x, area_y, log_weight = areas[half]
                 delta_x, delta_y = area_x - point_x, area_y - point_y
                 square = jnp.maximum(delta_x * delta_x + delta_y * delta_y, 1e-30)
-                value = jnp.exp2(log_weight - square * lax.rsqrt(square))
+                value = jnp.exp(log_weight - square * lax.rsqrt(square))
                 dest[
                     pl.ds(group * 16, 16), pl.ds(dest_area + pair * 256 + half * LANES, LANES)
                 ] = value.astype(BF16)
 
 
 def head_kernel(
-    factor, offset_ref, x_ref, y_ref, area_ref, first_prior_ref, prior_ref, head_ref, cols_ref, system_ref
+    factor, offset_ref, x_ref, y_ref, area_ref, prior_ref, head_ref, cols_ref, system_ref
 ):
     col_width = cols_ref.shape[0]
     total = area_ref.shape[1]
@@ -153,11 +164,7 @@
         return carry
 
     lax.fori_loop(0, total // CHUNK, step, 0)
-    rows = lax.broadcasted_iota(jnp.int32, (NB, NB), 0)
-    cols = lax.broadcasted_iota(jnp.int32, (NB, NB), 1)
-    system_ref[:, :NB] = system_ref[:, :NB] * factor + jnp.where(
-        rows == cols, first_prior_ref[...], 0.0
-    )
+    system_ref[:, :NB] = system_ref[:, :NB] * factor
     rows = lax.broadcasted_iota(jnp.int32, (NB, col_width), 0)
     cols = lax.broadcasted_iota(jnp.int32, (NB, col_width), 1) + offset_ref[0]
     system_ref[:, NB:] = system_ref[:, NB:] * factor + jnp.where(rows == cols, prior_ref[...], 0.0)
@@ -217,7 +224,11 @@
 
 def factor_kernel(system_ref, first_prior_ref, panel_ref, solved_ref, weighted_ref, work, block, inverses):
     count = NB // BLK
-    work[...] = system_ref[...].reshape(work.shape)
+    rows = lax.broadcasted_iota(jnp.int32, (NB, NB), 0)
+    cols = lax.broadcasted_iota(jnp.int32, (NB, NB), 1)
+    diagonal = jnp.where(rows == cols, first_prior_ref[...], 0.0)
+    work[:, :, :NB] = (system_ref[:, :NB] + diagonal).reshape(count, BLK, NB)
+    work[:, :, NB:] = system_ref[:, NB:].reshape(count, BLK, panel_ref.shape[1])
 
     def eliminate(k, carry):
         block[...] = work[k, :, pl.ds(pl.multiple_of(k * BLK, BLK), BLK)]
@@ -245,9 +256,7 @@
                 preferred_element_type=F32,
             )
         solved_ref[mine, :] = tn_dot(inverses[k], panel, HIGH)
-    rows = lax.broadcasted_iota(jnp.int32, (NB, NB), 0)
-    cols = lax.broadcasted_iota(jnp.int32, (NB, NB), 1)
-    column = jnp.sum(jnp.where(rows == cols, first_prior_ref[...], 0.0), axis=1, keepdims=True)
+    column = jnp.sum(diagonal, axis=1, keepdims=True)
     weighted_ref[...] = solved_ref[...] * column
 
 
@@ -285,25 +294,20 @@
             here = pl.ds(first, CHUNK)
             right = head_ref[:, here]
             removed = tn_dot(high, right) + tn_dot(low, right)
-            residual[:, here] = (cols_ref[:, here].astype(F32) - removed).astype(BF16)
+            residual[here, :] = (cols_ref[:, here].astype(F32) - removed).astype(BF16).T
             fill_kernel(left_even, first, x_ref, y_ref, first_points, tile_rows, area_ref, first, CHUNK)
             return carry
 
         lax.fori_loop(0, steps, step, 0)
 
     def run(source, dest):
-        out_ref[...] = jnp.zeros_like(out_ref)
-
-        def step(index, carry):
-            first = pl.multiple_of(index * CHUNK, CHUNK)
-            here = pl.ds(first, CHUNK)
-            out_ref[...] += nt_dot(source[:, here], residual[:, here])
+        for first in range(0, total, SPAN):
+            here = slice(first, first + SPAN)
+            part = jnp.dot(source[:, here], residual[here, :], preferred_element_type=F32)
+            out_ref[...] = part if first == 0 else out_ref[...] + part
             if dest is not None:
                 next_row = pl.multiple_of(first_points + (tile + 1) * tile_rows, 16)
-                fill_kernel(dest, first, x_ref, y_ref, next_row, tile_rows, area_ref, first, CHUNK)
-            return carry
-
-        lax.fori_loop(0, steps, step, 0)
+                fill_kernel(dest, first, x_ref, y_ref, next_row, tile_rows, area_ref, first, SPAN)
 
     parity = lax.rem(tile, 2)
     more = tile < tiles - 1
@@ -334,18 +338,31 @@
     return lax.all_gather(array, "area", axis=axis, tiled=True)
 
 
+def from_first(array, axis):
+    total = jnp.where(lax.axis_index(axis) == 0, array, 0.0)
+    for target in range(1, lax.axis_size(axis)):
+        total = total + lax.ppermute(array, axis, [(0, target)])
+    return total
+
+
+def first_block_prior(prior):
+    if prior.shape[0] == NB:
+        return from_first(from_first(prior.reshape(1, NB), "col"), "row")
+    return lax.all_gather(prior, ("row", "col"), axis=0, tiled=True)[:NB].reshape(1, NB)
+
+
 def per_device(area_xy, sampling_var, inducer_xy, order, prior):
     size_total = order.shape[0]
     length_scale = 2.0 / math.sqrt(size_total)
-    scale = math.log2(math.e) / length_scale
+    scale = 1.0 / length_scale
     col_width = prior.shape[0]
     row_height = size_total // lax.axis_size("area")
     areas_total = area_xy.shape[1] * lax.axis_size("area")
     factor = size_total / areas_total
 
-    own = jnp.concatenate([area_xy * scale, -0.5 * jnp.log2(0.5 + sampling_var)[None, :]], axis=0)
+    own = jnp.concatenate([area_xy * scale, -0.5 * jnp.log(0.5 + sampling_var)[None, :]], axis=0)
     areas = all_areas(own)
-    first_prior = lax.all_gather(prior, ("row", "col"), axis=0, tiled=True)[:NB].reshape(1, NB)
+    first_prior = first_block_prior(prior)
     own_prior = prior.reshape(1, col_width)
     point_x, point_y = gram_points(order, inducer_xy, scale, col_width, row_height)
     offsets = jnp.stack(
@@ -363,11 +380,11 @@
             jax.ShapeDtypeStruct((col_width, areas_total), BF16),
             jax.ShapeDtypeStruct((NB, NB + col_width), F32),
         ),
-        in_specs=[smem] + [vmem] * 5,
+        in_specs=[smem] + [vmem] * 4,
         out_specs=[vmem] * 3,
         compiler_params=params,
         name="head",
-    )(offsets, point_x, point_y, areas, first_prior, own_prior)
+    )(offsets, point_x, point_y, areas, own_prior)
     panel_rows, solved, weighted = pl.pallas_call(
         factor_kernel,
         out_shape=(jax.ShapeDtypeStruct((NB, col_width), F32),) * 3,
@@ -390,7 +407,7 @@
         scratch_shapes=[
             pltpu.VMEM((tile_rows, areas_total), BF16),
             pltpu.VMEM((tile_rows, areas_total), BF16),
-            pltpu.VMEM((col_width, areas_total), BF16),
+            pltpu.VMEM((areas_total, col_width), BF16),
         ],
         compiler_params=params,
         name="schur",

time: 167 us -> 143 us (0.86)
  blocking collectives: 22 us -> 0 us
  Pallas kernels: 136 us -> 119 us
  starting transfers between devices: 3 us -> 16.5 us
    all_gather x1 -> x0, blocking collectives: 22 us -> none  [per_device(): lax.all_gather(prior, ('row', 'col'), axis=0, tiled=True)[:NB]]
    ppermute x0 -> x6, starting transfers between devices: none -> 15 us  [from_first(): total = total + lax.ppermute(array, axis, [(0, target)])]
    pallas_call x1, Pallas kernels: 69 us -> 57.5 us  [per_device(): pl.pallas_call(functools.partial(schur_kernel, factor), grid=(row_height...]
    pallas_call x1, Pallas kernels: 19.1 us -> 14.1 us  [gram_points(): pl.pallas_call(functools.partial(points_kernel, scale), out_shape=(shape,...]
  transfers between devices with their start and end apart: 1 -> 7, of which waited for: 0 -> 0; matrix products, arithmetic and copies ran while one was open for 2% -> 4% of each run, Pallas kernels for 11% -> 10%
where the time goes in v2:
time: 143 us
  Pallas kernels  119 us (83%)
  starting transfers between devices  16.5 us (12%)
  other arithmetic  4.58 us (3%)
  local copies, waits for them, and re-layouts  1.47 us (1%)
    pallas_call x1, Pallas kernels, per_device(): pl.pallas_call(functools.partial(schur_kernel, factor), grid=(row_height...  57.5 us
    pallas_call x1, Pallas kernels, per_device(): pl.pallas_call(factor_kernel, out_shape=(jax.ShapeDtypeStruct((NB, col_wi...  30.8 us
    pallas_call x1, Pallas kernels, per_device(): pl.pallas_call(functools.partial(head_kernel, factor), out_shape=(jax.Sha...  17 us
    ppermute x6, starting transfers between devices, from_first(): total = total + lax.ppermute(array, axis, [(0, target)])  15 us
    pallas_call x1, Pallas kernels, gram_points(): pl.pallas_call(functools.partial(points_kernel, scale), out_shape=(shape,...  14.1 us
  transfers between devices with their start and end apart: 7, of which 0 were waited for; matrix products, arithmetic and copies ran while one was open for 4% of the time, Pallas kernels for 10%

profile of v2, /device:TPU:0, one launch (start us, length us, event | category | flops | bytes accessed | tf_op | source)
XLA Modules:
  0.0 142.8 jit_solution(7266964853500174356)
XLA Ops:
  0.6 4.3 %collective-permute-start.3 = (f32[1,512]{1,0:T(1,128)}, f32[1,512]{1,0:T(1,128)S(1)}, u32[]{:S(2)}, u32[]{:S(2)}) collective-permute-start(f32[1,512]{1,0:T(1,128)} %bitcast.17), channel_id=1, source_target_pairs={{0,3},{4,7},{8,11},{12,15},{16,19},{20,23},{24,27},{28,31}} | collective-permute-start | bytes 6152 | tf_op jit(solution)/shard_map/ppermute | solution.py:344
  4.9 1.3 collective-permute-start.2
  6.2 1.3 collective-permute-start.1
  7.5 0.7 log_multiply_fusion
  8.3 0.7 broadcast_multiply_fusion
  9.0 1.6 %collective-permute-start = (f32[3,2048]{1,0:T(4,128)S(1)}, f32[3,2048]{1,0:T(4,128)S(1)}, u32[]{:S(2)}, u32[]{:S(2)}) collective-permute-start(f32[3,2048]{1,0:T(4,128)S(1)} %pad_maximum_fusion.1), channel_id=1, source_target_pairs={{0,16},{16,0},{1,17},{17,1},{2,18},{18,2},{3,19},{19,3},{4,20},{20... | collective-permute-start | bytes 73736 | tf_op jit(solution)/shard_map/ppermute | solution.py:333
  10.6 0.7 broadcast_select_fusion.3
  11.3 0.6 pad_add_fusion.offset_ref
  11.9 0.0 collective-permute-done.3
  11.9 0.0 collective-permute-done.2
  11.9 0.0 collective-permute-done.1
  11.9 5.5 %collective-permute-start.6 = (f32[1,512]{1,0:T(1,128)S(1)}, f32[1,512]{1,0:T(1,128)S(1)}, u32[]{:S(2)}, u32[]{:S(2)}) collective-permute-start(f32[1,512]{1,0:T(1,128)S(1)} %add_add_fusion), channel_id=1, source_target_pairs={{0,12},{1,13},{2,14},{3,15},{16,28},{17,29},{18,30},{19,31}} | collective-permute-start | bytes 6152 | tf_op jit(solution)/shard_map/ppermute | solution.py:344
  17.4 1.3 collective-permute-start.5
  18.7 1.3 collective-permute-start.4
  20.0 0.6 pad_add_fusion.1.starts_ref
  20.6 1.5 %copy.9 = f32[1,2,64,128]{3,2,1,0:T(8,128)} copy(f32[1,2,64,128]{3,1,2,0:T(2,128)} %bitcast.15) | data formatting | bytes 131072
  22.1 14.1 %points.1 = (f32[5120,128]{1,0:T(8,128)}, f32[5120,128]{1,0:T(8,128)}) custom-call(s32[4]{0:T(128)} %pad_add_fusion.1.starts_ref, s32[64,128]{1,0:T(8,128)} %bitcast.16, f32[2,64,128]{2,1,0:T(8,128)} %bitcast.12), custom_call_target="tpu_custom_call" | custom-call | tf_op jit(solution)/shard_map/points/pallas_call | solution.py:113
  36.2 0.0 collective-permute-done.6
  36.2 0.0 collective-permute-done.5
  36.2 0.0 collective-permute-done.4
  36.2 0.5 fusion.2.first_prior_ref
  36.7 0.0 collective-permute-done
  36.8 0.6 pad_maximum_fusion.area_ref
  37.4 17.0 %head.1 = (bf16[512,4096]{1,0:T(8,128)(2,1)}, bf16[512,4096]{1,0:T(8,128)(2,1)}, f32[512,1024]{1,0:T(8,128)}) custom-call(s32[2]{0:T(128)} %pad_add_fusion.offset_ref, f32[5120,128]{1,0:T(8,128)} %get-tuple-element.10.x_ref, f32[5120,128]{1,0:T(8,128)} %get-tuple-element.11.y_ref, f32[3,4096]{1,0:T(4,128)} %pad_maximum_fusion.area_ref, f32[1,512]{1,0:T(1,128)} %bitcast.20), custom_call_target="tpu_custom_call" | custom-call | tf_op jit(solution)/shard_map/head/pallas_call | solution.py:376
  54.5 30.8 %factor.1 = (f32[512,512]{1,0:T(8,128)}, f32[512,512]{1,0:T(8,128)}, f32[512,512]{1,0:T(8,128)}) custom-call(f32[512,1024]{1,0:T(8,128)} %get-tuple-element.12.system_ref, f32[1,512]{1,0:T(1,128)} %fusion.2.first_prior_ref), custom_call_target="tpu_custom_call" | custom-call | tf_op jit(solution)/shard_map/factor/pallas_call | solution.py:388
  85.3 57.5 %schur.1 = f32[4096,512]{1,0:T(8,128)} custom-call(s32[2]{0:T(128)} %pad_add_fusion.offset_ref, f32[5120,128]{1,0:T(8,128)} %get-tuple-element.10.x_ref, f32[5120,128]{1,0:T(8,128)} %get-tuple-element.11.y_ref, f32[3,4096]{1,0:T(4,128)} %pad_maximum_fusion.area_ref, f32[1,512]{1,0:T(1,128)} %bitcast.21, bf16[512,4096]{1,0:T(8,128)(2,1)} %get-tuple-element.14.head_ref, ...), custom_call_target="tpu_custom_call" | custom-call | tf_op jit(solution)/shard_map/schur/pallas_call | solution.py:401
  (3 shorter events, 0.1 us)
Async XLA Ops:
  0.6 11.2 %collective-permute-start.3 = (f32[1,512]{1,0:T(1,128)}, f32[1,512]{1,0:T(1,128)S(1)}, u32[]{:S(2)}, u32[]{:S(2)}) collective-permute-start(f32[1,512]{1,0:T(1,128)} %bitcast.17), channel_id=1, source_target_pairs={{0,3},{4,7},{8,11},{12,15},{16,19},{20,23},{24,27},{28,31}} | collective-permute-start | bytes 6152 | tf_op jit(solution)/shard_map/ppermute | solution.py:344
  4.9 6.9 %collective-permute-start.2 = (f32[1,512]{1,0:T(1,128)}, f32[1,512]{1,0:T(1,128)S(1)}, u32[]{:S(2)}, u32[]{:S(2)}) collective-permute-start(f32[1,512]{1,0:T(1,128)} %bitcast.18), channel_id=1, source_target_pairs={{0,2},{4,6},{8,10},{12,14},{16,18},{20,22},{24,26},{28,30}} | collective-permute-start | bytes 6152 | tf_op jit(solution)/shard_map/ppermute | solution.py:344
  6.2 5.6 %collective-permute-start.1 = (f32[1,512]{1,0:T(1,128)}, f32[1,512]{1,0:T(1,128)S(1)}, u32[]{:S(2)}, u32[]{:S(2)}) collective-permute-start(f32[1,512]{1,0:T(1,128)} %bitcast.19), channel_id=1, source_target_pairs={{0,1},{4,5},{8,9},{12,13},{16,17},{20,21},{24,25},{28,29}} | collective-permute-start | bytes 6152 | tf_op jit(solution)/shard_map/ppermute | solution.py:344
  9.0 27.7 %collective-permute-start = (f32[3,2048]{1,0:T(4,128)S(1)}, f32[3,2048]{1,0:T(4,128)S(1)}, u32[]{:S(2)}, u32[]{:S(2)}) collective-permute-start(f32[3,2048]{1,0:T(4,128)S(1)} %pad_maximum_fusion.1), channel_id=1, source_target_pairs={{0,16},{16,0},{1,17},{17,1},{2,18},{18,2},{3,19},{19,3},{4,20},{20... | collective-permute-start | bytes 73736 | tf_op jit(solution)/shard_map/ppermute | solution.py:333
  11.9 24.3 %collective-permute-start.6 = (f32[1,512]{1,0:T(1,128)S(1)}, f32[1,512]{1,0:T(1,128)S(1)}, u32[]{:S(2)}, u32[]{:S(2)}) collective-permute-start(f32[1,512]{1,0:T(1,128)S(1)} %add_add_fusion), channel_id=1, source_target_pairs={{0,12},{1,13},{2,14},{3,15},{16,28},{17,29},{18,30},{19,31}} | collective-permute-start | bytes 6152 | tf_op jit(solution)/shard_map/ppermute | solution.py:344
  17.4 18.8 %collective-permute-start.5 = (f32[1,512]{1,0:T(1,128)S(1)}, f32[1,512]{1,0:T(1,128)S(1)}, u32[]{:S(2)}, u32[]{:S(2)}) collective-permute-start(f32[1,512]{1,0:T(1,128)S(1)} %add_add_fusion), channel_id=1, source_target_pairs={{0,8},{1,9},{2,10},{3,11},{16,24},{17,25},{18,26},{19,27}} | collective-permute-start | bytes 6152 | tf_op jit(solution)/shard_map/ppermute | solution.py:344
  18.7 17.5 %collective-permute-start.4 = (f32[1,512]{1,0:T(1,128)S(1)}, f32[1,512]{1,0:T(1,128)S(1)}, u32[]{:S(2)}, u32[]{:S(2)}) collective-permute-start(f32[1,512]{1,0:T(1,128)S(1)} %add_add_fusion), channel_id=1, source_target_pairs={{0,4},{1,5},{2,6},{3,7},{16,20},{17,21},{18,22},{19,23}} | collective-permute-start | bytes 6152 | tf_op jit(solution)/shard_map/ppermute | solution.py:344

commit v3 on v2

--- a/solution.py
+++ b/solution.py
@@ -13,7 +13,7 @@
 STRIP = 8
 BLK = 128
 CHUNK = 1024
-SPAN = 2048
+SPAN = 512
 VMEM_BYTES = 60 * 1024 * 1024
 HIGH = lax.Precision.HIGHEST
 F32 = jnp.float32
@@ -44,27 +44,32 @@
     return lax.axis_index("row") * lax.axis_size("col") + lax.axis_index("col")
 
 
-def points_kernel(scale, starts_ref, order_ref, table_ref, x_ref, y_ref, columns_ref):
+FEATURES = 32
+PIECE_PAIRS = ((0, 0), (0, 1), (1, 0), (1, 1), (0, 2), (2, 0))
+
+
+def write_features(dest, x_row, y_row, left):
+    one = jnp.ones_like(x_row)
+    norm = [piece.astype(F32) for piece in split_pieces(x_row * x_row + y_row * y_row)]
+    rows = norm + [one] * 3 if left else [one] * 3 + norm
+    for coordinate in (x_row, y_row):
+        factor = 1.0 if left else -2.0
+        pieces = [piece.astype(F32) * factor for piece in split_pieces(coordinate)]
+        rows += [pieces[pair[0 if left else 1]] for pair in PIECE_PAIRS]
+    for index, row in enumerate(rows):
+        dest[index : index + 1, :] = row
+
+
+def points_kernel(scale, center, starts_ref, order_ref, table_ref, features_ref, columns_ref, places, features):
     tables = table_ref[...]
     quotients = tables.shape[1]
-    pieces_x = split_pieces(tables[0] * scale)
-    pieces_y = split_pieces(tables[1] * scale)
+    pieces_x = split_pieces(tables[0] * scale - center)
+    pieces_y = split_pieces(tables[1] * scale - center)
     columns_ref[...] = jnp.concatenate(
         [jnp.concatenate(pieces_x, axis=0), jnp.concatenate(pieces_y, axis=0)], axis=1
     ).T
     quotient_ids = lax.broadcasted_iota(jnp.int32, (quotients, LANES), 0)
     lane_ids = lax.broadcasted_iota(jnp.int32, (LANES, LANES), 0)
-    on_diagonal = lane_ids == lax.broadcasted_iota(jnp.int32, (LANES, LANES), 1)
-    ones = jnp.ones((3 * LANES, LANES), BF16)
-
-    def spread(row):
-        diagonals = [
-            jnp.where(on_diagonal, jnp.broadcast_to(piece.astype(F32), (LANES, LANES)), 0.0)
-            for piece in split_pieces(row)
-        ]
-        return jnp.dot(
-            jnp.concatenate(diagonals, axis=1).astype(BF16), ones, preferred_element_type=F32
-        )
 
     def one_block(step):
         row = jnp.where(
@@ -80,25 +85,24 @@
             columns_ref[...], jnp.concatenate([hit, hit, hit], axis=0), preferred_element_type=F32
         )
         mine = lane_ids == lax.bitwise_and(ids, LANES - 1)
-        x_row = jnp.sum(jnp.where(mine, values[:LANES], 0.0), axis=0, keepdims=True)
-        y_row = jnp.sum(jnp.where(mine, values[LANES:], 0.0), axis=0, keepdims=True)
-        return spread(x_row), spread(y_row)
-
-    blocks = x_ref.shape[0] // LANES
-    unroll = next(count for count in (8, 7, 5, 4, 3, 2, 1) if blocks % count == 0)
-
-    def several(group, carry):
-        done = [one_block(group * unroll + i) for i in range(unroll)]
-        for i, (x_block, y_block) in enumerate(done):
-            rows = pl.ds(pl.multiple_of((group * unroll + i) * LANES, LANES), LANES)
-            x_ref[rows, :] = x_block
-            y_ref[rows, :] = y_block
-        return carry
-
-    lax.fori_loop(0, blocks // unroll, several, 0)
-
-
-def gram_points(order, inducer_xy, scale, col_width, row_height):
+        return [
+            jnp.sum(jnp.where(mine, values[k * LANES : (k + 1) * LANES], 0.0), axis=0, keepdims=True)
+            for k in range(2)
+        ]
+
+    blocks = features_ref.shape[0] // LANES
+    for step in range(blocks):
+        x_row, y_row = one_block(step)
+        places[0:1, step * LANES : (step + 1) * LANES] = x_row
+        places[1:2, step * LANES : (step + 1) * LANES] = y_row
+    features[...] = jnp.zeros_like(features)
+    write_features(features, places[0:1, :], places[1:2, :], True)
+    for step in range(blocks):
+        mine = slice(step * LANES, (step + 1) * LANES)
+        features_ref[mine, :] = features[:, mine].T.astype(BF16)
+
+
+def gram_points(order, inducer_xy, scale, center, col_width, row_height):
     quotients = order.shape[0] // LANES
     starts = jnp.stack(
         [
@@ -109,55 +113,60 @@
         ]
     ).astype(jnp.int32)
     count = NB + col_width + row_height
-    shape = jax.ShapeDtypeStruct((count, LANES), F32)
     return pl.pallas_call(
-        functools.partial(points_kernel, scale),
-        out_shape=(shape, shape),
+        functools.partial(points_kernel, scale, center),
+        out_shape=jax.ShapeDtypeStruct((count, FEATURES), BF16),
         in_specs=[
             pl.BlockSpec(memory_space=pltpu.SMEM),
             pl.BlockSpec(memory_space=pltpu.VMEM),
             pl.BlockSpec(memory_space=pltpu.VMEM),
         ],
-        out_specs=[pl.BlockSpec(memory_space=pltpu.VMEM)] * 2,
-        scratch_shapes=[pltpu.VMEM((2 * LANES, 3 * quotients), BF16)],
+        out_specs=pl.BlockSpec(memory_space=pltpu.VMEM),
+        scratch_shapes=[
+            pltpu.VMEM((2 * LANES, 3 * quotients), BF16),
+            pltpu.VMEM((2, count), F32),
+            pltpu.VMEM((FEATURES, count), F32),
+        ],
         compiler_params=pltpu.CompilerParams(vmem_limit_bytes=VMEM_BYTES),
         name="points",
     )(starts, order.reshape(quotients, LANES), inducer_xy.reshape(2, quotients, LANES))
 
 
-def fill_kernel(dest, dest_area, x_ref, y_ref, first_row, row_count, area_ref, first_area, area_count):
-    for pair in range(area_count // 256):
-        areas = []
-        for half in range(2):
-            lanes = pl.ds(first_area + pair * 256 + half * LANES, LANES)
-            areas.append(
-                [jnp.broadcast_to(area_ref[k : k + 1, lanes], (16, LANES)) for k in range(3)]
-            )
-        for group in range(row_count // 16):
-            rows = pl.ds(first_row + group * 16, 16)
-            point_x, point_y = x_ref[rows, :], y_ref[rows, :]
+def fill_kernel(dest, points, area_features, log_weights, first, count):
+    for start in range(0, count, 256):
+        lanes = pl.ds(first + start, 256)
+        squares = jnp.dot(points, area_features[:, lanes], preferred_element_type=F32)
+        weights = [
+            jnp.broadcast_to(log_weights[2:3, pl.ds(first + start + half, LANES)], (16, LANES))
+            for half in (0, LANES)
+        ]
+        for row in range(0, points.shape[0], 16):
             for half in range(2):
-                area_x, area_y, log_weight = areas[half]
-                delta_x, delta_y = area_x - point_x, area_y - point_y
-                square = jnp.maximum(delta_x * delta_x + delta_y * delta_y, 1e-30)
-                value = jnp.exp(log_weight - square * lax.rsqrt(square))
-                dest[
-                    pl.ds(group * 16, 16), pl.ds(dest_area + pair * 256 + half * LANES, LANES)
-                ] = value.astype(BF16)
+                square = jnp.maximum(
+                    squares[row : row + 16, half * LANES : (half + 1) * LANES], 1e-30
+                )
+                value = jnp.exp2(weights[half] - square * lax.rsqrt(square))
+                dest[row : row + 16, pl.ds(first + start + half * LANES, LANES)] = value.astype(BF16)
 
 
 def head_kernel(
-    factor, offset_ref, x_ref, y_ref, area_ref, prior_ref, head_ref, cols_ref, system_ref
+    factor, offset_ref, points_ref, area_ref, prior_ref, head_ref, cols_ref, system_ref, area_features_ref, features
 ):
     col_width = cols_ref.shape[0]
     total = area_ref.shape[1]
+    features[...] = jnp.zeros_like(features)
+    write_features(features, area_ref[0:1, :], area_ref[1:2, :], False)
+    area_features_ref[...] = features[...].astype(BF16)
+    log_weights = area_ref
     system_ref[...] = jnp.zeros_like(system_ref)
 
     def step(index, carry):
         first = pl.multiple_of(index * CHUNK, CHUNK)
         here = pl.ds(first, CHUNK)
-        fill_kernel(head_ref, first, x_ref, y_ref, 0, NB, area_ref, first, CHUNK)
-        fill_kernel(cols_ref, first, x_ref, y_ref, NB, col_width, area_ref, first, CHUNK)
+        fill_kernel(head_ref, points_ref[:NB, :], area_features_ref, log_weights, first, CHUNK)
+        fill_kernel(
+            cols_ref, points_ref[NB : NB + col_width, :], area_features_ref, log_weights, first, CHUNK
+        )
         left = head_ref[:, here]
         system_ref[:, :NB] += nt_dot(left, left)
         system_ref[:, NB:] += nt_dot(left, cols_ref[:, here])
@@ -263,9 +272,9 @@
 def schur_kernel(
     factor,
     offset_ref,
-    x_ref,
-    y_ref,
+    points_ref,
     area_ref,
+    area_features_ref,
     prior_ref,
     head_ref,
     cols_ref,
@@ -283,9 +292,11 @@
     steps = total // CHUNK
     first_points = NB + col_width
     tile_rows = out_ref.shape[0]
+    log_weights = area_ref
 
     @pl.when(tile == 0)
     def _():
+        points = points_ref[first_points : first_points + tile_rows, :]
         high = solved_ref[...].astype(BF16)
         low = (solved_ref[...] - high.astype(F32)).astype(BF16)
 
@@ -295,19 +306,21 @@
             right = head_ref[:, here]
             removed = tn_dot(high, right) + tn_dot(low, right)
             residual[here, :] = (cols_ref[:, here].astype(F32) - removed).astype(BF16).T
-            fill_kernel(left_even, first, x_ref, y_ref, first_points, tile_rows, area_ref, first, CHUNK)
+            fill_kernel(left_even, points, area_features_ref, log_weights, first, CHUNK)
             return carry
 
         lax.fori_loop(0, steps, step, 0)
 
     def run(source, dest):
+        if dest is not None:
+            next_row = pl.multiple_of(first_points + (tile + 1) * tile_rows, 16)
+            points = points_ref[pl.ds(next_row, tile_rows), :]
         for first in range(0, total, SPAN):
             here = slice(first, first + SPAN)
             part = jnp.dot(source[:, here], residual[here, :], preferred_element_type=F32)
             out_ref[...] = part if first == 0 else out_ref[...] + part
             if dest is not None:
-                next_row = pl.multiple_of(first_points + (tile + 1) * tile_rows, 16)
-                fill_kernel(dest, first, x_ref, y_ref, next_row, tile_rows, area_ref, first, SPAN)
+                fill_kernel(dest, points, area_features_ref, log_weights, first, SPAN)
 
     parity = lax.rem(tile, 2)
     more = tile < tiles - 1
@@ -354,17 +367,18 @@
 def per_device(area_xy, sampling_var, inducer_xy, order, prior):
     size_total = order.shape[0]
     length_scale = 2.0 / math.sqrt(size_total)
-    scale = 1.0 / length_scale
+    scale = math.log2(math.e) / length_scale
+    center = 6.0 / math.sqrt(size_total) * scale
     col_width = prior.shape[0]
     row_height = size_total // lax.axis_size("area")
     areas_total = area_xy.shape[1] * lax.axis_size("area")
     factor = size_total / areas_total
 
-    own = jnp.concatenate([area_xy * scale, -0.5 * jnp.log(0.5 + sampling_var)[None, :]], axis=0)
+    own = jnp.concatenate([area_xy * scale - center, -0.5 * jnp.log2(0.5 + sampling_var)[None, :]], axis=0)
     areas = all_areas(own)
     first_prior = first_block_prior(prior)
     own_prior = prior.reshape(1, col_width)
-    point_x, point_y = gram_points(order, inducer_xy, scale, col_width, row_height)
+    points = gram_points(order, inducer_xy, scale, center, col_width, row_height)
     offsets = jnp.stack(
         [block_position() * col_width, lax.axis_index("area") * row_height]
     ).astype(jnp.int32)
@@ -373,18 +387,20 @@
     smem = pl.BlockSpec(memory_space=pltpu.SMEM)
     vmem = pl.BlockSpec(memory_space=pltpu.VMEM)
     params = pltpu.CompilerParams(vmem_limit_bytes=VMEM_BYTES)
-    head, cols, system = pl.pallas_call(
+    head, cols, system, area_features = pl.pallas_call(
         functools.partial(head_kernel, factor),
         out_shape=(
             jax.ShapeDtypeStruct((NB, areas_total), BF16),
             jax.ShapeDtypeStruct((col_width, areas_total), BF16),
             jax.ShapeDtypeStruct((NB, NB + col_width), F32),
+            jax.ShapeDtypeStruct((FEATURES, areas_total), BF16),
         ),
-        in_specs=[smem] + [vmem] * 4,
-        out_specs=[vmem] * 3,
+        in_specs=[smem] + [vmem] * 3,
+        out_specs=[vmem] * 4,
+        scratch_shapes=[pltpu.VMEM((FEATURES, areas_total), F32)],
         compiler_params=params,
         name="head",
-    )(offsets, point_x, point_y, areas, own_prior)
+    )(offsets, points, areas, own_prior)
     panel_rows, solved, weighted = pl.pallas_call(
         factor_kernel,
         out_shape=(jax.ShapeDtypeStruct((NB, col_width), F32),) * 3,
@@ -411,7 +427,7 @@
         ],
         compiler_params=params,
         name="schur",
-    )(offsets, point_x, point_y, areas, own_prior, head, cols, solved, weighted)
+    )(offsets, points, areas, area_features, own_prior, head, cols, solved, weighted)
     return (panel_rows, schur)
 
 

time: 143 us -> 120 us (0.84)
  Pallas kernels: 119 us -> 96.1 us
    pallas_call x1, Pallas kernels: 57.5 us -> 47.3 us  [per_device(): pl.pallas_call(functools.partial(schur_kernel, factor), grid=(row_height...]
    pallas_call x1, Pallas kernels: 14.1 us -> 4.01 us  [gram_points(): pl.pallas_call(functools.partial(points_kernel, scale, center), out_shape...]
    pallas_call x1, Pallas kernels: 17 us -> 13.9 us  [per_device(): pl.pallas_call(functools.partial(head_kernel, factor), out_shape=(jax.Sha...]
  transfers between devices with their start and end apart: 7 -> 7, of which waited for: 0 -> 0; matrix products, arithmetic and copies ran while one was open for 4% -> 5% of each run, Pallas kernels for 10% -> 3%
where the time goes in v3:
time: 120 us; the launch traced here: 119 us
  Pallas kernels  96.1 us (80%)
  starting transfers between devices  16.5 us (14%)
  other arithmetic  4.61 us (4%)
  local copies, waits for them, and re-layouts  1.47 us (1%)
    pallas_call x1, Pallas kernels, per_device(): pl.pallas_call(functools.partial(schur_kernel, factor), grid=(row_height...  47.3 us
    pallas_call x1, Pallas kernels, per_device(): pl.pallas_call(factor_kernel, out_shape=(jax.ShapeDtypeStruct((NB, col_wi...  30.9 us
    ppermute x6, starting transfers between devices, from_first(): total = total + lax.ppermute(array, axis, [(0, target)])  15 us
    pallas_call x1, Pallas kernels, per_device(): pl.pallas_call(functools.partial(head_kernel, factor), out_shape=(jax.Sha...  13.9 us
    pallas_call x1, Pallas kernels, gram_points(): pl.pallas_call(functools.partial(points_kernel, scale, center), out_shape...  4.01 us
  transfers between devices with their start and end apart: 7, of which 0 were waited for; matrix products, arithmetic and copies ran while one was open for 5% of the time, Pallas kernels for 3%

profile of v3, /device:TPU:0, one launch (start us, length us, event | category | flops | bytes accessed | tf_op | source)
XLA Modules:
  0.0 119.4 jit_solution(14944761650961955488)
XLA Ops:
  0.6 4.3 %collective-permute-start.3 = (f32[1,512]{1,0:T(1,128)}, f32[1,512]{1,0:T(1,128)S(1)}, u32[]{:S(2)}, u32[]{:S(2)}) collective-permute-start(f32[1,512]{1,0:T(1,128)} %bitcast.17), channel_id=1, source_target_pairs={{0,3},{4,7},{8,11},{12,15},{16,19},{20,23},{24,27},{28,31}} | collective-permute-start | bytes 6152 | tf_op jit(solution)/shard_map/ppermute | solution.py:357
  4.9 1.3 %collective-permute-start.2 = (f32[1,512]{1,0:T(1,128)}, f32[1,512]{1,0:T(1,128)S(1)}, u32[]{:S(2)}, u32[]{:S(2)}) collective-permute-start(f32[1,512]{1,0:T(1,128)} %bitcast.18), channel_id=1, source_target_pairs={{0,2},{4,6},{8,10},{12,14},{16,18},{20,22},{24,26},{28,30}} | collective-permute-start | bytes 6152 | tf_op jit(solution)/shard_map/ppermute | solution.py:357
  6.2 1.3 %collective-permute-start.1 = (f32[1,512]{1,0:T(1,128)}, f32[1,512]{1,0:T(1,128)S(1)}, u32[]{:S(2)}, u32[]{:S(2)}) collective-permute-start(f32[1,512]{1,0:T(1,128)} %bitcast.19), channel_id=1, source_target_pairs={{0,1},{4,5},{8,9},{12,13},{16,17},{20,21},{24,25},{28,29}} | collective-permute-start | bytes 6152 | tf_op jit(solution)/shard_map/ppermute | solution.py:357
  7.5 0.7 log_multiply_fusion
  8.3 0.7 multiply_add_fusion
  9.0 1.6 %collective-permute-start = (f32[3,2048]{1,0:T(4,128)S(1)}, f32[3,2048]{1,0:T(4,128)S(1)}, u32[]{:S(2)}, u32[]{:S(2)}) collective-permute-start(f32[3,2048]{1,0:T(4,128)S(1)} %pad_maximum_fusion.1), channel_id=1, source_target_pairs={{0,16},{16,0},{1,17},{17,1},{2,18},{18,2},{3,19},{19,3},{4,20},{20... | collective-permute-start | bytes 73736 | tf_op jit(solution)/shard_map/ppermute | solution.py:346
  10.6 0.7 broadcast_select_fusion.3
  11.3 0.6 pad_add_fusion.offset_ref
  11.9 0.0 collective-permute-done.3
  11.9 0.0 collective-permute-done.2
  11.9 0.0 collective-permute-done.1
  11.9 5.5 %collective-permute-start.6 = (f32[1,512]{1,0:T(1,128)S(1)}, f32[1,512]{1,0:T(1,128)S(1)}, u32[]{:S(2)}, u32[]{:S(2)}) collective-permute-start(f32[1,512]{1,0:T(1,128)S(1)} %add_add_fusion), channel_id=1, source_target_pairs={{0,12},{1,13},{2,14},{3,15},{16,28},{17,29},{18,30},{19,31}} | collective-permute-start | bytes 6152 | tf_op jit(solution)/shard_map/ppermute | solution.py:357
  17.4 1.3 %collective-permute-start.5 = (f32[1,512]{1,0:T(1,128)S(1)}, f32[1,512]{1,0:T(1,128)S(1)}, u32[]{:S(2)}, u32[]{:S(2)}) collective-permute-start(f32[1,512]{1,0:T(1,128)S(1)} %add_add_fusion), channel_id=1, source_target_pairs={{0,8},{1,9},{2,10},{3,11},{16,24},{17,25},{18,26},{19,27}} | collective-permute-start | bytes 6152 | tf_op jit(solution)/shard_map/ppermute | solution.py:357
  18.7 1.3 %collective-permute-start.4 = (f32[1,512]{1,0:T(1,128)S(1)}, f32[1,512]{1,0:T(1,128)S(1)}, u32[]{:S(2)}, u32[]{:S(2)}) collective-permute-start(f32[1,512]{1,0:T(1,128)S(1)} %add_add_fusion), channel_id=1, source_target_pairs={{0,4},{1,5},{2,6},{3,7},{16,20},{17,21},{18,22},{19,23}} | collective-permute-start | bytes 6152 | tf_op jit(solution)/shard_map/ppermute | solution.py:357
  20.0 0.6 pad_add_fusion.1.starts_ref
  20.6 1.5 %copy.9 = f32[1,2,64,128]{3,2,1,0:T(8,128)} copy(f32[1,2,64,128]{3,1,2,0:T(2,128)} %bitcast.15) | data formatting | bytes 131072
  22.1 4.0 %points.1.points_ref = bf16[5120,32]{1,0:T(8,128)(2,1)} custom-call(s32[4]{0:T(128)} %pad_add_fusion.1.starts_ref, s32[64,128]{1,0:T(8,128)} %bitcast.16, f32[2,64,128]{2,1,0:T(8,128)} %bitcast.12), custom_call_target="tpu_custom_call" | custom-call | tf_op jit(solution)/shard_map/points/pallas_call | solution.py:116
  26.1 0.0 collective-permute-done.6
  26.1 0.0 collective-permute-done.5
  26.1 0.0 collective-permute-done.4
  26.1 0.6 fusion.2.first_prior_ref
  26.7 0.0 collective-permute-done
  26.7 0.6 pad_maximum_fusion.area_ref
  27.4 13.9 %head.1 = (bf16[512,4096]{1,0:T(8,128)(2,1)}, bf16[512,4096]{1,0:T(8,128)(2,1)}, f32[512,1024]{1,0:T(8,128)}, bf16[32,4096]{1,0:T(8,128)(2,1)}) custom-call(s32[2]{0:T(128)} %pad_add_fusion.offset_ref, bf16[5120,32]{1,0:T(8,128)(2,1)} %points.1.points_ref, f32[3,4096]{1,0:T(4,128)} %pad_maximum_fusion.area_ref, f32[1,512]{1,0:T(1,128)} %bitcast.20), custom_call_target="tpu_custom_call" | custom-call | tf_op jit(solution)/shard_map/head/pallas_call | solution.py:390
  41.3 30.9 %factor.1 = (f32[512,512]{1,0:T(8,128)}, f32[512,512]{1,0:T(8,128)}, f32[512,512]{1,0:T(8,128)}) custom-call(f32[512,1024]{1,0:T(8,128)} %get-tuple-element.9.system_ref, f32[1,512]{1,0:T(1,128)} %fusion.2.first_prior_ref), custom_call_target="tpu_custom_call" | custom-call | tf_op jit(solution)/shard_map/factor/pallas_call | solution.py:404
  72.2 47.3 %schur.1 = f32[4096,512]{1,0:T(8,128)} custom-call(s32[2]{0:T(128)} %pad_add_fusion.offset_ref, bf16[5120,32]{1,0:T(8,128)(2,1)} %points.1.points_ref, f32[3,4096]{1,0:T(4,128)} %pad_maximum_fusion.area_ref, bf16[32,4096]{1,0:T(8,128)(2,1)} %get-tuple-element.11.area_features_ref, f32[1,512]{1,0:T(1,128)} %bitcast.21, ...), custom_call_target="tpu_custom_call" | custom-call | tf_op jit(solution)/shard_map/schur/pallas_call | solution.py:417
  (3 shorter events, 0.1 us)
Async XLA Ops:
  0.6 11.3 %collective-permute-start.3 = (f32[1,512]{1,0:T(1,128)}, f32[1,512]{1,0:T(1,128)S(1)}, u32[]{:S(2)}, u32[]{:S(2)}) collective-permute-start(f32[1,512]{1,0:T(1,128)} %bitcast.17), channel_id=1, source_target_pairs={{0,3},{4,7},{8,11},{12,15},{16,19},{20,23},{24,27},{28,31}} | collective-permute-start | bytes 6152 | tf_op jit(solution)/shard_map/ppermute | solution.py:357
  4.9 6.9 %collective-permute-start.2 = (f32[1,512]{1,0:T(1,128)}, f32[1,512]{1,0:T(1,128)S(1)}, u32[]{:S(2)}, u32[]{:S(2)}) collective-permute-start(f32[1,512]{1,0:T(1,128)} %bitcast.18), channel_id=1, source_target_pairs={{0,2},{4,6},{8,10},{12,14},{16,18},{20,22},{24,26},{28,30}} | collective-permute-start | bytes 6152 | tf_op jit(solution)/shard_map/ppermute | solution.py:357
  6.2 5.6 %collective-permute-start.1 = (f32[1,512]{1,0:T(1,128)}, f32[1,512]{1,0:T(1,128)S(1)}, u32[]{:S(2)}, u32[]{:S(2)}) collective-permute-start(f32[1,512]{1,0:T(1,128)} %bitcast.19), channel_id=1, source_target_pairs={{0,1},{4,5},{8,9},{12,13},{16,17},{20,21},{24,25},{28,29}} | collective-permute-start | bytes 6152 | tf_op jit(solution)/shard_map/ppermute | solution.py:357
  9.0 17.7 %collective-permute-start = (f32[3,2048]{1,0:T(4,128)S(1)}, f32[3,2048]{1,0:T(4,128)S(1)}, u32[]{:S(2)}, u32[]{:S(2)}) collective-permute-start(f32[3,2048]{1,0:T(4,128)S(1)} %pad_maximum_fusion.1), channel_id=1, source_target_pairs={{0,16},{16,0},{1,17},{17,1},{2,18},{18,2},{3,19},{19,3},{4,20},{20... | collective-permute-start | bytes 73736 | tf_op jit(solution)/shard_map/ppermute | solution.py:346
  11.9 14.2 %collective-permute-start.6 = (f32[1,512]{1,0:T(1,128)S(1)}, f32[1,512]{1,0:T(1,128)S(1)}, u32[]{:S(2)}, u32[]{:S(2)}) collective-permute-start(f32[1,512]{1,0:T(1,128)S(1)} %add_add_fusion), channel_id=1, source_target_pairs={{0,12},{1,13},{2,14},{3,15},{16,28},{17,29},{18,30},{19,31}} | collective-permute-start | bytes 6152 | tf_op jit(solution)/shard_map/ppermute | solution.py:357
  17.4 8.7 %collective-permute-start.5 = (f32[1,512]{1,0:T(1,128)S(1)}, f32[1,512]{1,0:T(1,128)S(1)}, u32[]{:S(2)}, u32[]{:S(2)}) collective-permute-start(f32[1,512]{1,0:T(1,128)S(1)} %add_add_fusion), channel_id=1, source_target_pairs={{0,8},{1,9},{2,10},{3,11},{16,24},{17,25},{18,26},{19,27}} | collective-permute-start | bytes 6152 | tf_op jit(solution)/shard_map/ppermute | solution.py:357
  18.7 7.4 %collective-permute-start.4 = (f32[1,512]{1,0:T(1,128)S(1)}, f32[1,512]{1,0:T(1,128)S(1)}, u32[]{:S(2)}, u32[]{:S(2)}) collective-permute-start(f32[1,512]{1,0:T(1,128)S(1)} %add_add_fusion), channel_id=1, source_target_pairs={{0,4},{1,5},{2,6},{3,7},{16,20},{17,21},{18,22},{19,23}} | collective-permute-start | bytes 6152 | tf_op jit(solution)/shard_map/ppermute | solution.py:357

commit v4 on v3

v4 whole, which is shorter than its diff:
```python
import functools
import math

import jax
import jax.numpy as jnp
from jax import lax
from jax.experimental import pallas as pl
from jax.experimental.pallas import tpu as pltpu
from jax.sharding import PartitionSpec as P

NB = 512
LANES = 128
STRIP = 8
PANEL = 4
BLK = 128
CHUNK = 1024
SPAN = 512
VMEM_BYTES = 60 * 1024 * 1024
HIGH = lax.Precision.HIGHEST
F32 = jnp.float32
BF16 = jnp.bfloat16


def split_pieces(value):
    first = value.astype(BF16)
    rest = value - first.astype(F32)
    second = rest.astype(BF16)
    third = (rest - second.astype(F32)).astype(BF16)
    return first, second, third


def nt_dot(left, right, precision=None):
    return lax.dot_general(
        left, right, (((1,), (1,)), ((), ())), precision=precision, preferred_element_type=F32
    )


def tn_dot(left, right, precision=None):
    return lax.dot_general(
        left, right, (((0,), (0,)), ((), ())), precision=precision, preferred_element_type=F32
    )


def block_position():
    return lax.axis_index("row") * lax.axis_size("col") + lax.axis_index("col")


FEATURES = 32
PIECE_PAIRS = ((0, 0), (0, 1), (1, 0), (1, 1), (0, 2), (2, 0))


def write_features(dest, x_row, y_row, left):
    one = jnp.ones_like(x_row)
    norm = [piece.astype(F32) for piece in split_pieces(x_row * x_row + y_row * y_row)]
    rows = norm + [one] * 3 if left else [one] * 3 + norm
    for coordinate in (x_row, y_row):
        factor = 1.0 if left else -2.0
        pieces = [piece.astype(F32) * factor for piece in split_pieces(coordinate)]
        rows += [pieces[pair[0 if left else 1]] for pair in PIECE_PAIRS]
    for index, row in enumerate(rows):
        dest[index : index + 1, :] = row


def points_kernel(scale, center, starts_ref, order_ref, table_ref, features_ref, columns_ref, places, features):
    tables = table_ref[...]
    quotients = tables.shape[1]
    pieces_x = split_pieces(tables[0] * scale - center)
    pieces_y = split_pieces(tables[1] * scale - center)
    columns_ref[...] = jnp.concatenate(
        [jnp.concatenate(pieces_x, axis=0), jnp.concatenate(pieces_y, axis=0)], axis=1
    ).T
    quotient_ids = lax.broadcasted_iota(jnp.int32, (quotients, LANES), 0)
    lane_ids = lax.broadcasted_iota(jnp.int32, (LANES, LANES), 0)

    def one_block(step):
        row = jnp.where(
            step < starts_ref[0],
            step,
            jnp.where(
                step < starts_ref[1], starts_ref[2] + step - starts_ref[0], starts_ref[3] + step - starts_ref[1]
            ),
        )
        ids = order_ref[pl.ds(row, 1), :]
        hit = jnp.where(quotient_ids == lax.shift_right_logical(ids, 7), 1.0, 0.0).astype(BF16)
        values = jnp.dot(
            columns_ref[...], jnp.concatenate([hit, hit, hit], axis=0), preferred_element_type=F32
        )
        mine = lane_ids == lax.bitwise_and(ids, LANES - 1)
        return [
            jnp.sum(jnp.where(mine, values[k * LANES : (k + 1) * LANES], 0.0), axis=0, keepdims=True)
            for k in range(2)
        ]

    blocks = features_ref.shape[0] // LANES
    for step in range(blocks):
        x_row, y_row = one_block(step)
        places[0:1, step * LANES : (step + 1) * LANES] = x_row
        places[1:2, step * LANES : (step + 1) * LANES] = y_row
    features[...] = jnp.zeros_like(features)
    write_features(features, places[0:1, :], places[1:2, :], True)
    for step in range(blocks):
        mine = slice(step * LANES, (step + 1) * LANES)
        features_ref[mine, :] = features[:, mine].T.astype(BF16)


def gram_points(order, inducer_xy, scale, center, col_width, row_height):
    quotients = order.shape[0] // LANES
    starts = jnp.stack(
        [
            jnp.int32(NB // LANES),
            jnp.int32((NB + col_width) // LANES),
            block_position() * (col_width // LANES),
            lax.axis_index("area") * (row_height // LANES),
        ]
    ).astype(jnp.int32)
    count = NB + col_width + row_height
    return pl.pallas_call(
        functools.partial(points_kernel, scale, center),
        out_shape=jax.ShapeDtypeStruct((count, FEATURES), BF16),
        in_specs=[
            pl.BlockSpec(memory_space=pltpu.SMEM),
            pl.BlockSpec(memory_space=pltpu.VMEM),
            pl.BlockSpec(memory_space=pltpu.VMEM),
        ],
        out_specs=pl.BlockSpec(memory_space=pltpu.VMEM),
        scratch_shapes=[
            pltpu.VMEM((2 * LANES, 3 * quotients), BF16),
            pltpu.VMEM((2, count), F32),
            pltpu.VMEM((FEATURES, count), F32),
        ],
        compiler_params=pltpu.CompilerParams(vmem_limit_bytes=VMEM_BYTES),
        name="points",
    )(starts, order.reshape(quotients, LANES), inducer_xy.reshape(2, quotients, LANES))


def fill_kernel(dest, points, area_features, log_weights, first, count):
    for start in range(0, count, 256):
        lanes = pl.ds(first + start, 256)
        squares = jnp.dot(points, area_features[:, lanes], preferred_element_type=F32)
        weights = [
            jnp.broadcast_to(log_weights[2:3, pl.ds(first + start + half, LANES)], (16, LANES))
            for half in (0, LANES)
        ]
        for row in range(0, points.shape[0], 16):
            for half in range(2):
                square = jnp.maximum(
                    squares[row : row + 16, half * LANES : (half + 1) * LANES], 1e-30
                )
                value = jnp.exp2(weights[half] - square * lax.rsqrt(square))
                dest[row : row + 16, pl.ds(first + start + half * LANES, LANES)] = value.astype(BF16)


def whole_row(value, index):
    return jnp.broadcast_to(value[index : index + 1, :], (STRIP, LANES))


def whole_lane(value, index):
    return jnp.broadcast_to(value[:, index : index + 1], (STRIP, LANES))


def inverse_factor(block_ref, inverse_ref, beside):
    count = BLK // STRIP
    row_ids = lax.broadcasted_iota(jnp.int32, (STRIP, LANES), 0)
    lane_ids = lax.broadcasted_iota(jnp.int32, (STRIP, LANES), 1)
    tops = [block_ref[i * STRIP : (i + 1) * STRIP, :] for i in range(count)]
    units = [jnp.where(lane_ids == row_ids + i * STRIP, 1.0, 0.0).astype(F32) for i in range(count)]
    for p in range(count):
        panel_end = (p // PANEL + 1) * PANEL
        diag_cols = [whole_lane(tops[p], p * STRIP + j) for j in range(STRIP)]
        entry = {
            (i, j): whole_row(diag_cols[j], i) for j in range(STRIP) for i in range(j, STRIP)
        }
        top_rows = [whole_row(tops[p], j) for j in range(STRIP)]
        unit_rows = [whole_row(units[p], j) for j in range(STRIP)]
        roots = []
        for j in range(STRIP):
            root = lax.rsqrt(entry[j, j])
            roots.append(root)
            for i in range(j + 1, STRIP):
                entry[i, j] = entry[i, j] * root
            for k in range(j + 1, STRIP):
                for i in range(k, STRIP):
                    entry[i, k] = entry[i, k] - entry[i, j] * entry[k, j]
        for j in range(STRIP):
            for k in range(j):
                top_rows[j] = top_rows[j] - entry[j, k] * top_rows[k]
                unit_rows[j] = unit_rows[j] - entry[j, k] * unit_rows[k]
            top_rows[j] = top_rows[j] * roots[j]
            unit_rows[j] = unit_rows[j] * roots[j]
        for i in range(p + 1, panel_end):
            cols = [whole_lane(tops[i], p * STRIP + j) for j in range(STRIP)]
            top, unit = tops[i], units[i]
            for j in range(STRIP):
                for k in range(j):
                    cols[j] = cols[j] - cols[k] * entry[j, k]
                cols[j] = cols[j] * roots[j]
                top = top - cols[j] * top_rows[j]
                unit = unit - cols[j] * unit_rows[j]
            tops[i], units[i] = top, unit
        top, unit = top_rows[STRIP - 1], unit_rows[STRIP - 1]
        for j in range(STRIP - 1):
            top = jnp.where(row_ids == j, top_rows[j], top)
            unit = jnp.where(row_ids == j, unit_rows[j], unit)
        tops[p], units[p] = top, unit
        inverse_ref[p * STRIP : (p + 1) * STRIP, :] = unit
        beside(p)
        if p + 1 == panel_end and panel_end < count:
            panel = slice(panel_end - PANEL, panel_end)
            top = jnp.concatenate(tops[panel], axis=0)
            both = jnp.concatenate([top, jnp.concatenate(units[panel], axis=0)], axis=1)
            update = tn_dot(top, both, HIGH)
            for i in range(panel_end, count):
                mine = slice(i * STRIP, (i + 1) * STRIP)
                tops[i] = tops[i] - update[mine, :LANES]
                units[i] = units[i] - update[mine, LANES:]


def schur_kernel(
    factor,
    ahead,
    offset_ref,
    points_ref,
    area_ref,
    first_prior_ref,
    prior_ref,
    panel_ref,
    out_ref,
    head,
    cols,
    features,
    area_features,
    system,
    block,
    inverses,
    solved,
    weighted,
    residual,
    *lefts,
):
    tile = pl.program_id(0)
    col_width = cols.shape[0]
    total = area_ref.shape[1]
    first_points = NB + col_width
    tile_rows = out_ref.shape[0]
    tiles = (points_ref.shape[0] - first_points) // tile_rows

    def fill_left(index, first, count):
        start = first_points + index * tile_rows
        points = points_ref[start : start + tile_rows, :]
        fill_kernel(lefts[index % len(lefts)], points, area_features, area_ref, first, count)

    def products():
        features[...] = jnp.zeros_like(features)
        write_features(features, area_ref[0:1, :], area_ref[1:2, :], False)
        area_features[...] = features[...].astype(BF16)
        system[...] = jnp.zeros_like(system)
        group = min(4, total // CHUNK)

        def accumulate(first):
            here = pl.ds(first, CHUNK)
            left = head[:, here]
            system[:, :NB] += nt_dot(left, left)
            system[:, NB:] += nt_dot(left, cols[:, here])

        def step(index, carry):
            base = pl.multiple_of(index * (group * CHUNK), group * CHUNK)
            for part in range(group):
                first = base + part * CHUNK
                if part:
                    accumulate(first - CHUNK)
                fill_kernel(head, points_ref[:NB, :], area_features, area_ref, first, CHUNK)
                fill_kernel(
                    cols, points_ref[NB : NB + col_width, :], area_features, area_ref, first, CHUNK
                )
            accumulate(base + (group - 1) * CHUNK)
            return carry

        lax.fori_loop(0, total // (group * CHUNK), step, 0)

    def solve():
        rows = lax.broadcasted_iota(jnp.int32, (NB, NB), 0)
        lanes = lax.broadcasted_iota(jnp.int32, (NB, NB), 1)
        diagonal = jnp.where(rows == lanes, first_prior_ref[...], 0.0)
        system[:, :NB] = system[:, :NB] * factor + diagonal
        rows = lax.broadcasted_iota(jnp.int32, (NB, col_width), 0)
        lanes = lax.broadcasted_iota(jnp.int32, (NB, col_width), 1) + offset_ref[0]
        system[:, NB:] = system[:, NB:] * factor + jnp.where(rows == lanes, prior_ref[...], 0.0)
        weighted[...] = jnp.broadcast_to(jnp.sum(diagonal, axis=1, keepdims=True), weighted.shape)
        count = NB // BLK
        strips = BLK // STRIP
        quarter = total // count
        pieces = [(index, start) for index in range(ahead) for start in range(0, quarter, 256)]

        def eliminate(k, carry):
            mine = pl.ds(pl.multiple_of(k * BLK, BLK), BLK)
            block[...] = system[mine, mine]
            base = pl.multiple_of(k * quarter, quarter)

            def beside(p):
                for index, start in pieces[p * len(pieces) // strips : (p + 1) * len(pieces) // strips]:
                    fill_left(index, base + start, 256)

            inverse_factor(block, inverses.at[k], beside)
            row = jnp.dot(inverses[k], system[mine, :], precision=HIGH, preferred_element_type=F32)
            system[mine, :] = row
            for i in range(1, count):

                @pl.when(i > k)
                def _():
                    system[i * BLK : (i + 1) * BLK, :] -= tn_dot(row[:, i * BLK : (i + 1) * BLK], row, HIGH)

            return carry

        lax.fori_loop(0, count, eliminate, 0)
        for k in range(count - 1, -1, -1):
            mine = slice(k * BLK, (k + 1) * BLK)
            panel = system[mine, NB:]
            panel_ref[mine, :] = panel
            if k < count - 1:
                panel = panel - jnp.dot(
                    system[mine, (k + 1) * BLK : NB],
                    solved[(k + 1) * BLK :, :],
                    precision=HIGH,
                    preferred_element_type=F32,
                )
            solved[mine, :] = tn_dot(inverses[k], panel, HIGH)
        weighted[...] = weighted[...] * solved[...]

    def reduce_columns():
        high = solved[...].astype(BF16)
        low = (solved[...] - high.astype(F32)).astype(BF16)

        def step(index, carry):
            here = pl.ds(pl.multiple_of(index * CHUNK, CHUNK), CHUNK)
            right = head[:, here]
            removed = tn_dot(high, right) + tn_dot(low, right)
            residual[here, :] = (cols[:, here].astype(F32) - removed).astype(BF16).T
            return carry

        lax.fori_loop(0, total // CHUNK, step, 0)

    @pl.when(tile == 0)
    def _():
        products()
        solve()
        reduce_columns()

    def run(index):
        left = lefts[index % len(lefts)]
        for first in range(0, total, SPAN):
            here = slice(first, first + SPAN)
            part = jnp.dot(left[:, here], residual[here, :], preferred_element_type=F32)
            out_ref[...] = part if first == 0 else out_ref[...] + part
            if index + ahead < tiles:
                fill_left(index + ahead, first, SPAN)

    for index in range(tiles):
        pl.when(tile == index)(functools.partial(run, index))

    first_row = offset_ref[1] + tile * tile_rows
    rows = lax.broadcasted_iota(jnp.int32, (tile_rows, col_width), 0) + first_row
    lanes = lax.broadcasted_iota(jnp.int32, (tile_rows, col_width), 1) + offset_ref[0]
    out_ref[...] = out_ref[...] * factor + jnp.where(rows == lanes, prior_ref[...], 0.0)

    @pl.when(first_row < NB)
    def _():
        out_ref[...] -= weighted[pl.ds(pl.multiple_of(first_row, tile_rows), tile_rows), :]


def all_areas(array):
    axis = array.ndim - 1
    if lax.axis_size("area") == 2:
        other = lax.ppermute(array, "area", [(0, 1), (1, 0)])
        first = lax.axis_index("area") == 0
        return jnp.concatenate(
            [jnp.where(first, array, other), jnp.where(first, other, array)], axis=axis
        )
    return lax.all_gather(array, "area", axis=axis, tiled=True)


def first_block_prior(prior):
    if prior.shape[0] == NB:
        mine = jnp.where(block_position() == 0, prior, 0.0)
        return lax.psum(mine, ("row", "col")).reshape(1, NB)
    return lax.all_gather(prior, ("row", "col"), axis=0, tiled=True)[:NB].reshape(1, NB)


def per_device(area_xy, sampling_var, inducer_xy, order, prior):
    size_total = order.shape[0]
    length_scale = 2.0 / math.sqrt(size_total)
    scale = math.log2(math.e) / length_scale
    center = 6.0 / math.sqrt(size_total) * scale
    col_width = prior.shape[0]
    row_height = size_total // lax.axis_size("area")
    areas_total = area_xy.shape[1] * lax.axis_size("area")
    factor = size_total / areas_total

    own = jnp.concatenate([area_xy * scale - center, -0.5 * jnp.log2(0.5 + sampling_var)[None, :]], axis=0)
    areas = all_areas(own)
    first_prior = first_block_prior(prior)
    own_prior = prior.reshape(1, col_width)
    points = gram_points(order, inducer_xy, scale, center, col_width, row_height)
    offsets = jnp.stack(
        [block_position() * col_width, lax.axis_index("area") * row_height]
    ).astype(jnp.int32)

    small = areas_total <= 8192
    tile_rows = min(row_height, 512 if small else 256)
    tiles = row_height // tile_rows
    ahead = min(4 if small else 1, tiles)
    buffers = min(2 * ahead, tiles)
    smem = pl.BlockSpec(memory_space=pltpu.SMEM)
    vmem = pl.BlockSpec(memory_space=pltpu.VMEM)
    panel_rows, schur = pl.pallas_call(
        functools.partial(schur_kernel, factor, ahead),
        grid=(tiles,),
        out_shape=(
            jax.ShapeDtypeStruct((NB, col_width), F32),
            jax.ShapeDtypeStruct((row_height, col_width), F32),
        ),
        in_specs=[smem] + [vmem] * 4,
        out_specs=[vmem, pl.BlockSpec((tile_rows, col_width), lambda i: (i, 0))],
        scratch_shapes=[
            pltpu.VMEM((NB, areas_total), BF16),
            pltpu.VMEM((col_width, areas_total), BF16),
            pltpu.VMEM((FEATURES, areas_total), F32),
            pltpu.VMEM((FEATURES, areas_total), BF16),
            pltpu.VMEM((NB, NB + col_width), F32),
            pltpu.VMEM((BLK, BLK), F32),
            pltpu.VMEM((NB // BLK, BLK, BLK), F32),
            pltpu.VMEM((NB, col_width), F32),
            pltpu.VMEM((NB, col_width), F32),
            pltpu.VMEM((areas_total, col_width), BF16),
        ]
        + [pltpu.VMEM((tile_rows, areas_total), BF16)] * buffers,
        compiler_params=pltpu.CompilerParams(vmem_limit_bytes=VMEM_BYTES),
        name="schur",
    )(offsets, points, areas, first_prior, own_prior)
    return (panel_rows, schur)


def solution(mesh):
    in_specs = (P(None, "area"), P("area"), P(), P(), P(("row", "col")))
    out_specs = (P(None, ("row", "col")), P("area", ("row", "col")))
    return jax.shard_map(
        per_device, mesh=mesh, in_specs=in_specs, out_specs=out_specs, check_vma=False
    )
```

time: 120 us -> 147 us (1.23); the launches traced: 119 us -> 144 us
  blocking collectives: 0 us -> 33.1 us
  starting transfers between devices: 16.5 us -> 3 us
  Pallas kernels: 96.1 us -> 102 us
    psum x0 -> x1, blocking collectives: none -> 33.1 us  [first_block_prior(): return lax.psum(mine, ('row', 'col')).reshape(1, NB)]
    ppermute x6 -> x0, starting transfers between devices: 15 us -> none  [from_first(): total = total + lax.ppermute(array, axis, [(0, target)])]
    pallas_call x3 -> x1, Pallas kernels: 92.1 us -> 97.8 us  [per_device(): pl.pallas_call(functools.partial(schur_kernel, factor, ahead), grid=(tile...]
  transfers between devices with their start and end apart: 7 -> 1, of which waited for: 0 -> 0; matrix products, arithmetic and copies ran while one was open for 5% -> 2% of each run, Pallas kernels for 3% -> 3%
where the time goes in v4:
time: 147 us; the launch traced here: 144 us
  Pallas kernels  102 us (69%)
  blocking collectives  33.1 us (23%)
  other arithmetic  4.03 us (3%)
  starting transfers between devices  3 us (2%)
  local copies, waits for them, and re-layouts  1.47 us (1%)
    pallas_call x1, Pallas kernels, per_device(): pl.pallas_call(functools.partial(schur_kernel, factor, ahead), grid=(tile...  97.8 us
    psum x1, blocking collectives, first_block_prior(): return lax.psum(mine, ('row', 'col')).reshape(1, NB)  33.1 us
    pallas_call x1, Pallas kernels, gram_points(): pl.pallas_call(functools.partial(points_kernel, scale, center), out_shape...  3.91 us
    ppermute x1, starting transfers between devices, all_areas(): other = lax.ppermute(array, 'area', [(0, 1), (1, 0)])  3 us
  transfers between devices with their start and end apart: 1, of which 0 were waited for; matrix products, arithmetic and copies ran while one was open for 2% of the time, Pallas kernels for 3%

profile of v4, /device:TPU:0, one launch (start us, length us, event | category | flops | bytes accessed | tf_op | source)
XLA Modules:
  0.0 144.3 jit_solution(17450337949895551655)
XLA Ops:
  0.6 0.7 log_multiply_fusion
  1.3 0.7 multiply_add_fusion
  2.1 3.0 %collective-permute-start = (f32[3,2048]{1,0:T(4,128)S(1)}, f32[3,2048]{1,0:T(4,128)S(1)}, u32[]{:S(2)}, u32[]{:S(2)}) collective-permute-start(f32[3,2048]{1,0:T(4,128)S(1)} %pad_maximum_fusion.1), channel_id=1, source_target_pairs={{0,16},{16,0},{1,17},{17,1},{2,18},{18,2},{3,19},{19,3},{4,20},{20... | collective-permute-start | bytes 73736 | tf_op jit(solution)/shard_map/ppermute | solution.py:373
  5.1 0.7 pad_add_fusion.offset_ref
  5.8 0.7 broadcast_select_fusion.2
  6.4 0.6 pad_add_fusion.1.starts_ref
  7.0 1.5 %copy.9 = f32[1,2,64,128]{3,2,1,0:T(8,128)} copy(f32[1,2,64,128]{3,1,2,0:T(2,128)} %bitcast.15) | data formatting | bytes 131072
  8.5 3.9 %points.1.points_ref = bf16[5120,32]{1,0:T(8,128)(2,1)} custom-call(s32[4]{0:T(128)} %pad_add_fusion.1.starts_ref, s32[64,128]{1,0:T(8,128)} %bitcast.16, f32[2,64,128]{2,1,0:T(8,128)} %bitcast.12), custom_call_target="tpu_custom_call" | custom-call | tf_op jit(solution)/shard_map/points/pallas_call | solution.py:117
  12.4 33.1 %psum.7.first_prior_ref = f32[1,512]{1,0:T(1,128)} all-reduce(f32[1,512]{1,0:T(1,128)S(1)} %bitcast.18), channel_id=1, replica_groups=mesh['area'=2,'row'=4,'col'=4] {'row','col'}, use_global_device_ids=true, to_apply=%region_0.1 | all-reduce | flops 512 | bytes 4096 | tf_op jit(solution)/shard_map/psum | solution.py:384
  45.5 0.0 collective-permute-done
  45.5 0.6 pad_maximum_fusion.area_ref
  46.1 97.8 %schur.1 = (f32[512,512]{1,0:T(8,128)}, f32[4096,512]{1,0:T(8,128)}) custom-call(s32[2]{0:T(128)} %pad_add_fusion.offset_ref, bf16[5120,32]{1,0:T(8,128)(2,1)} %points.1.points_ref, f32[3,4096]{1,0:T(4,128)} %pad_maximum_fusion.area_ref, f32[1,512]{1,0:T(1,128)} %psum.7.first_prior_ref, f32[1,512]{1,0:T(1,128)} %bitcast.17), custom_call_target="tpu_custom_call" | custom-call | tf_op jit(solution)/shard_map/schur/pallas_call | solution.py:414
  (2 shorter events, 0.0 us)
Async XLA Ops:
  2.1 43.4 %collective-permute-start = (f32[3,2048]{1,0:T(4,128)S(1)}, f32[3,2048]{1,0:T(4,128)S(1)}, u32[]{:S(2)}, u32[]{:S(2)}) collective-permute-start(f32[3,2048]{1,0:T(4,128)S(1)} %pad_maximum_fusion.1), channel_id=1, source_target_pairs={{0,16},{16,0},{1,17},{17,1},{2,18},{18,2},{3,19},{19,3},{4,20},{20... | collective-permute-start | bytes 73736 | tf_op jit(solution)/shard_map/ppermute | solution.py:373

commit v5 on v3

--- a/solution.py
+++ b/solution.py
@@ -11,6 +11,7 @@
 NB = 512
 LANES = 128
 STRIP = 8
+PANEL = 4
 BLK = 128
 CHUNK = 1024
 SPAN = 512
@@ -60,9 +61,13 @@
         dest[index : index + 1, :] = row
 
 
-def points_kernel(scale, center, starts_ref, order_ref, table_ref, features_ref, columns_ref, places, features):
-    tables = table_ref[...]
-    quotients = tables.shape[1]
+def points_kernel(
+    scale, center, col_width, offset_ref, order_ref, table_ref, features_ref, columns_ref, places, features, tables
+):
+    quotients = order_ref.shape[0]
+    for q in range(quotients):
+        for k in range(2):
+            tables[k, q : q + 1, :] = table_ref[k : k + 1, q * LANES : (q + 1) * LANES]
     pieces_x = split_pieces(tables[0] * scale - center)
     pieces_y = split_pieces(tables[1] * scale - center)
     columns_ref[...] = jnp.concatenate(
@@ -72,13 +77,11 @@
     lane_ids = lax.broadcasted_iota(jnp.int32, (LANES, LANES), 0)
 
     def one_block(step):
-        row = jnp.where(
-            step < starts_ref[0],
-            step,
-            jnp.where(
-                step < starts_ref[1], starts_ref[2] + step - starts_ref[0], starts_ref[3] + step - starts_ref[1]
-            ),
-        )
+        row = step
+        if step >= (NB + col_width) // LANES:
+            row = offset_ref[1] // LANES + step - (NB + col_width) // LANES
+        elif step >= NB // LANES:
+            row = offset_ref[0] // LANES + step - NB // LANES
         ids = order_ref[pl.ds(row, 1), :]
         hit = jnp.where(quotient_ids == lax.shift_right_logical(ids, 7), 1.0, 0.0).astype(BF16)
         values = jnp.dot(
@@ -102,19 +105,11 @@
         features_ref[mine, :] = features[:, mine].T.astype(BF16)
 
 
-def gram_points(order, inducer_xy, scale, center, col_width, row_height):
+def gram_points(offsets, order, inducer_xy, scale, center, col_width, row_height):
     quotients = order.shape[0] // LANES
-    starts = jnp.stack(
-        [
-            jnp.int32(NB // LANES),
-            jnp.int32((NB + col_width) // LANES),
-            block_position() * (col_width // LANES),
-            lax.axis_index("area") * (row_height // LANES),
-        ]
-    ).astype(jnp.int32)
     count = NB + col_width + row_height
     return pl.pallas_call(
-        functools.partial(points_kernel, scale, center),
+        functools.partial(points_kernel, scale, center, col_width),
         out_shape=jax.ShapeDtypeStruct((count, FEATURES), BF16),
         in_specs=[
             pl.BlockSpec(memory_space=pltpu.SMEM),
@@ -126,10 +121,12 @@
             pltpu.VMEM((2 * LANES, 3 * quotients), BF16),
             pltpu.VMEM((2, count), F32),
             pltpu.VMEM((FEATURES, count), F32),
+            pltpu.VMEM((2, quotients, LANES), F32),
         ],
         compiler_params=pltpu.CompilerParams(vmem_limit_bytes=VMEM_BYTES),
+        cost_estimate=pl.CostEstimate(flops=5 * 10**9, bytes_accessed=2**20, transcendentals=0),
         name="points",
-    )(starts, order.reshape(quotients, LANES), inducer_xy.reshape(2, quotients, LANES))
+    )(offsets, order.reshape(quotients, LANES), inducer_xy)
 
 
 def fill_kernel(dest, points, area_features, log_weights, first, count):
@@ -137,7 +134,7 @@
         lanes = pl.ds(first + start, 256)
         squares = jnp.dot(points, area_features[:, lanes], preferred_element_type=F32)
         weights = [
-            jnp.broadcast_to(log_weights[2:3, pl.ds(first + start + half, LANES)], (16, LANES))
+            jnp.broadcast_to(log_weights[0:1, pl.ds(first + start + half, LANES)], (16, LANES))
             for half in (0, LANES)
         ]
         for row in range(0, points.shape[0], 16):
@@ -150,14 +147,27 @@
 
 
 def head_kernel(
-    factor, offset_ref, points_ref, area_ref, prior_ref, head_ref, cols_ref, system_ref, area_features_ref, features
+    factor,
+    scale,
+    center,
+    offset_ref,
+    points_ref,
+    *refs,
 ):
+    *area_refs, prior_ref, head_ref, cols_ref, system_ref, area_features_ref, log_weights, features = refs
     col_width = cols_ref.shape[0]
-    total = area_ref.shape[1]
+    total = area_features_ref.shape[1]
     features[...] = jnp.zeros_like(features)
-    write_features(features, area_ref[0:1, :], area_ref[1:2, :], False)
+    width = total // len(area_refs)
+    for index in range(len(area_refs)):
+        values = area_refs[index][...]
+        if len(area_refs) == 2:
+            values = jnp.where(offset_ref[2] == index, area_refs[0][...], area_refs[1][...])
+        lanes = slice(index * width, (index + 1) * width)
+        places = values[0:2] * scale - center
+        write_features(features.at[:, lanes], places[0:1], places[1:2], False)
+        log_weights[:, lanes] = -0.5 * jnp.log2(0.5 + values[2:3])
     area_features_ref[...] = features[...].astype(BF16)
-    log_weights = area_ref
     system_ref[...] = jnp.zeros_like(system_ref)
 
     def step(index, carry):
@@ -194,6 +204,7 @@
     tops = [block_ref[i * STRIP : (i + 1) * STRIP, :] for i in range(count)]
     units = [jnp.where(lane_ids == row_ids + i * STRIP, 1.0, 0.0).astype(F32) for i in range(count)]
     for p in range(count):
+        panel_end = (p // PANEL + 1) * PANEL
         diag_cols = [whole_lane(tops[p], p * STRIP + j) for j in range(STRIP)]
         entry = {
             (i, j): whole_row(diag_cols[j], i) for j in range(STRIP) for i in range(j, STRIP)
@@ -215,7 +226,7 @@
                 unit_rows[j] = unit_rows[j] - entry[j, k] * unit_rows[k]
             top_rows[j] = top_rows[j] * roots[j]
             unit_rows[j] = unit_rows[j] * roots[j]
-        for i in range(p + 1, count):
+        for i in range(p + 1, panel_end):
             cols = [whole_lane(tops[i], p * STRIP + j) for j in range(STRIP)]
             top, unit = tops[i], units[i]
             for j in range(STRIP):
@@ -225,10 +236,21 @@
                 top = top - cols[j] * top_rows[j]
                 unit = unit - cols[j] * unit_rows[j]
             tops[i], units[i] = top, unit
-        final = unit_rows[STRIP - 1]
+        top, unit = top_rows[STRIP - 1], unit_rows[STRIP - 1]
         for j in range(STRIP - 1):
-            final = jnp.where(row_ids == j, unit_rows[j], final)
-        inverse_ref[p * STRIP : (p + 1) * STRIP, :] = final
+            top = jnp.where(row_ids == j, top_rows[j], top)
+            unit = jnp.where(row_ids == j, unit_rows[j], unit)
+        tops[p], units[p] = top, unit
+        inverse_ref[p * STRIP : (p + 1) * STRIP, :] = unit
+        if p + 1 == panel_end and panel_end < count:
+            panel = slice(panel_end - PANEL, panel_end)
+            top = jnp.concatenate(tops[panel], axis=0)
+            both = jnp.concatenate([top, jnp.concatenate(units[panel], axis=0)], axis=1)
+            update = tn_dot(top, both, HIGH)
+            for i in range(panel_end, count):
+                mine = slice(i * STRIP, (i + 1) * STRIP)
+                tops[i] = tops[i] - update[mine, :LANES]
+                units[i] = units[i] - update[mine, LANES:]
 
 
 def factor_kernel(system_ref, first_prior_ref, panel_ref, solved_ref, weighted_ref, work, block, inverses):
@@ -273,7 +295,7 @@
     factor,
     offset_ref,
     points_ref,
-    area_ref,
+    log_weights,
     area_features_ref,
     prior_ref,
     head_ref,
@@ -288,11 +310,10 @@
     tile = pl.program_id(0)
     tiles = pl.num_programs(0)
     col_width = cols_ref.shape[0]
-    total = area_ref.shape[1]
+    total = log_weights.shape[1]
     steps = total // CHUNK
     first_points = NB + col_width
     tile_rows = out_ref.shape[0]
-    log_weights = area_ref
 
     @pl.when(tile == 0)
     def _():
@@ -315,12 +336,17 @@
         if dest is not None:
             next_row = pl.multiple_of(first_points + (tile + 1) * tile_rows, 16)
             points = points_ref[pl.ds(next_row, tile_rows), :]
-        for first in range(0, total, SPAN):
-            here = slice(first, first + SPAN)
-            part = jnp.dot(source[:, here], residual[here, :], preferred_element_type=F32)
-            out_ref[...] = part if first == 0 else out_ref[...] + part
+        out_ref[...] = jnp.zeros_like(out_ref)
+
+        def step(index, carry):
+            first = pl.multiple_of(index * SPAN, SPAN)
+            here = pl.ds(first, SPAN)
+            out_ref[...] += jnp.dot(source[:, here], residual[here, :], preferred_element_type=F32)
             if dest is not None:
                 fill_kernel(dest, points, area_features_ref, log_weights, first, SPAN)
+            return carry
+
+        lax.fori_loop(0, total // SPAN, step, 0)
 
     parity = lax.rem(tile, 2)
     more = tile < tiles - 1
@@ -341,14 +367,9 @@
 
 
 def all_areas(array):
-    axis = array.ndim - 1
     if lax.axis_size("area") == 2:
-        other = lax.ppermute(array, "area", [(0, 1), (1, 0)])
-        first = lax.axis_index("area") == 0
-        return jnp.concatenate(
-            [jnp.where(first, array, other), jnp.where(first, other, array)], axis=axis
-        )
-    return lax.all_gather(array, "area", axis=axis, tiled=True)
+        return [array, lax.ppermute(array, "area", [(0, 1), (1, 0)])]
+    return [lax.all_gather(array, "area", axis=array.ndim - 1, tiled=True)]
 
 
 def from_first(array, axis):
@@ -374,33 +395,35 @@
     areas_total = area_xy.shape[1] * lax.axis_size("area")
     factor = size_total / areas_total
 
-    own = jnp.concatenate([area_xy * scale - center, -0.5 * jnp.log2(0.5 + sampling_var)[None, :]], axis=0)
+    own = jnp.concatenate([area_xy, sampling_var[None, :]], axis=0)
     areas = all_areas(own)
     first_prior = first_block_prior(prior)
     own_prior = prior.reshape(1, col_width)
-    points = gram_points(order, inducer_xy, scale, center, col_width, row_height)
     offsets = jnp.stack(
-        [block_position() * col_width, lax.axis_index("area") * row_height]
+        [block_position() * col_width, lax.axis_index("area") * row_height, lax.axis_index("area")]
     ).astype(jnp.int32)
 
+    points = gram_points(offsets, order, inducer_xy, scale, center, col_width, row_height)
     tile_rows = min(row_height, 512 if areas_total <= 8192 else 256)
     smem = pl.BlockSpec(memory_space=pltpu.SMEM)
     vmem = pl.BlockSpec(memory_space=pltpu.VMEM)
     params = pltpu.CompilerParams(vmem_limit_bytes=VMEM_BYTES)
-    head, cols, system, area_features = pl.pallas_call(
-        functools.partial(head_kernel, factor),
+    head, cols, system, area_features, log_weights = pl.pallas_call(
+        functools.partial(head_kernel, factor, scale, center),
         out_shape=(
             jax.ShapeDtypeStruct((NB, areas_total), BF16),
             jax.ShapeDtypeStruct((col_width, areas_total), BF16),
             jax.ShapeDtypeStruct((NB, NB + col_width), F32),
             jax.ShapeDtypeStruct((FEATURES, areas_total), BF16),
+            jax.ShapeDtypeStruct((1, areas_total), F32),
         ),
-        in_specs=[smem] + [vmem] * 3,
-        out_specs=[vmem] * 4,
+        in_specs=[smem] + [vmem] * (2 + len(areas)),
+        out_specs=[vmem] * 5,
+        cost_estimate=pl.CostEstimate(flops=10**10, bytes_accessed=2**24, transcendentals=0),
         scratch_shapes=[pltpu.VMEM((FEATURES, areas_total), F32)],
         compiler_params=params,
         name="head",
-    )(offsets, points, areas, own_prior)
+    )(offsets, points, *areas, own_prior)
     panel_rows, solved, weighted = pl.pallas_call(
         factor_kernel,
         out_shape=(jax.ShapeDtypeStruct((NB, col_width), F32),) * 3,
@@ -427,7 +450,7 @@
         ],
         compiler_params=params,
         name="schur",
-    )(offsets, points, areas, area_features, own_prior, head, cols, solved, weighted)
+    )(offsets, points, log_weights, area_features, own_prior, head, cols, solved, weighted)
     return (panel_rows, schur)
 
 

time: 120 us -> 129 us (1.075)
  Pallas kernels: 96.1 us -> 108 us
  other arithmetic: 4.61 us -> 2.69 us
    pallas_call x1, Pallas kernels: 47.3 us -> 60.8 us  [per_device(): pl.pallas_call(functools.partial(schur_kernel, factor), grid=(row_height...]
    pallas_call x1, Pallas kernels: 30.9 us -> 29.3 us  [per_device(): pl.pallas_call(factor_kernel, out_shape=(jax.ShapeDtypeStruct((NB, col_wi...]
  transfers between devices with their start and end apart: 7 -> 7, of which waited for: 0 -> 0; matrix products, arithmetic and copies ran while one was open for 5% -> 2% of each run, Pallas kernels for 3% -> 3%
where the time goes in v5:
time: 129 us
  Pallas kernels  108 us (84%)
  starting transfers between devices  16.5 us (13%)
  other arithmetic  2.69 us (2%)
    pallas_call x1, Pallas kernels, per_device(): pl.pallas_call(functools.partial(schur_kernel, factor), grid=(row_height...  60.8 us
    pallas_call x1, Pallas kernels, per_device(): pl.pallas_call(factor_kernel, out_shape=(jax.ShapeDtypeStruct((NB, col_wi...  29.3 us
    ppermute x6, starting transfers between devices, from_first(): total = total + lax.ppermute(array, axis, [(0, target)])  15 us
    pallas_call x1, Pallas kernels, per_device(): pl.pallas_call(functools.partial(head_kernel, factor, scale, center), out...  13.9 us
    pallas_call x1, Pallas kernels, gram_points(): pl.pallas_call(functools.partial(points_kernel, scale, center, col_width)...  4.03 us
  transfers between devices with their start and end apart: 7, of which 0 were waited for; matrix products, arithmetic and copies ran while one was open for 2% of the time, Pallas kernels for 3%

profile of v5, /device:TPU:0, one launch (start us, length us, event | category | flops | bytes accessed | tf_op | source)
XLA Modules:
  0.0 128.6 jit_solution(8927747137866857595)
XLA Ops:
  0.6 4.3 %collective-permute-start.3 = (f32[1,512]{1,0:T(1,128)}, f32[1,512]{1,0:T(1,128)S(1)}, u32[]{:S(2)}, u32[]{:S(2)}) collective-permute-start(f32[1,512]{1,0:T(1,128)} %bitcast.9), channel_id=1, source_target_pairs={{0,3},{4,7},{8,11},{12,15},{16,19},{20,23},{24,27},{28,31}} | collective-permute-start | bytes 6152 | tf_op jit(solution)/shard_map/ppermute | solution.py:378
  4.9 1.3 %collective-permute-start.2 = (f32[1,512]{1,0:T(1,128)}, f32[1,512]{1,0:T(1,128)S(1)}, u32[]{:S(2)}, u32[]{:S(2)}) collective-permute-start(f32[1,512]{1,0:T(1,128)} %bitcast.10), channel_id=1, source_target_pairs={{0,2},{4,6},{8,10},{12,14},{16,18},{20,22},{24,26},{28,30}} | collective-permute-start | bytes 6152 | tf_op jit(solution)/shard_map/ppermute | solution.py:378
  6.2 1.3 %collective-permute-start.1 = (f32[1,512]{1,0:T(1,128)}, f32[1,512]{1,0:T(1,128)S(1)}, u32[]{:S(2)}, u32[]{:S(2)}) collective-permute-start(f32[1,512]{1,0:T(1,128)} %bitcast.11), channel_id=1, source_target_pairs={{0,1},{4,5},{8,9},{12,13},{16,17},{20,21},{24,25},{28,29}} | collective-permute-start | bytes 6152 | tf_op jit(solution)/shard_map/ppermute | solution.py:378
  7.5 0.8 pad_maximum_fusion.refs_0_
  8.3 0.0 copy-start
  8.3 1.6 %collective-permute-start = (f32[3,2048]{1,0:T(4,128)S(1)}, f32[3,2048]{1,0:T(4,128)S(1)}, u32[]{:S(2)}, u32[]{:S(2)}) collective-permute-start(f32[3,2048]{1,0:T(4,128)S(1)} %pad_maximum_fusion.refs_0_), channel_id=1, source_target_pairs={{0,16},{16,0},{1,17},{17,1},{2,18},{18,2},{3,19},{19,3},{4,20},{20... | collective-permute-start | bytes 73736 | tf_op jit(solution)/shard_map/ppermute | solution.py:371
  9.9 0.7 broadcast_select_fusion.1
  10.6 0.6 pad_add_fusion.offset_ref
  11.2 0.0 collective-permute-done.3
  11.2 0.0 collective-permute-done.2
  11.2 0.0 collective-permute-done.1
  11.2 5.5 %collective-permute-start.6 = (f32[1,512]{1,0:T(1,128)S(1)}, f32[1,512]{1,0:T(1,128)S(1)}, u32[]{:S(2)}, u32[]{:S(2)}) collective-permute-start(f32[1,512]{1,0:T(1,128)S(1)} %add_add_fusion), channel_id=1, source_target_pairs={{0,12},{1,13},{2,14},{3,15},{16,28},{17,29},{18,30},{19,31}} | collective-permute-start | bytes 6152 | tf_op jit(solution)/shard_map/ppermute | solution.py:378
  16.7 1.3 %collective-permute-start.5 = (f32[1,512]{1,0:T(1,128)S(1)}, f32[1,512]{1,0:T(1,128)S(1)}, u32[]{:S(2)}, u32[]{:S(2)}) collective-permute-start(f32[1,512]{1,0:T(1,128)S(1)} %add_add_fusion), channel_id=1, source_target_pairs={{0,8},{1,9},{2,10},{3,11},{16,24},{17,25},{18,26},{19,27}} | collective-permute-start | bytes 6152 | tf_op jit(solution)/shard_map/ppermute | solution.py:378
  18.0 1.3 %collective-permute-start.4 = (f32[1,512]{1,0:T(1,128)S(1)}, f32[1,512]{1,0:T(1,128)S(1)}, u32[]{:S(2)}, u32[]{:S(2)}) collective-permute-start(f32[1,512]{1,0:T(1,128)S(1)} %add_add_fusion), channel_id=1, source_target_pairs={{0,4},{1,5},{2,6},{3,7},{16,20},{17,21},{18,22},{19,23}} | collective-permute-start | bytes 6152 | tf_op jit(solution)/shard_map/ppermute | solution.py:378
  19.3 4.0 %points.1.points_ref = bf16[5120,32]{1,0:T(8,128)(2,1)} custom-call(s32[3]{0:T(128)} %pad_add_fusion.offset_ref, s32[64,128]{1,0:T(8,128)} %bitcast.14, f32[2,8192]{1,0:T(2,128)} %table_ref.1), custom_call_target="tpu_custom_call" | custom-call | flops 5000000000 | bytes 1048576 | tf_op jit(solution)/shard_map/points/pallas_call | solution.py:111
  23.4 0.0 copy-done
  23.4 0.0 collective-permute-done.6
  23.4 0.0 collective-permute-done.5
  23.4 0.0 collective-permute-done.4
  23.4 0.6 fusion.2.first_prior_ref
  24.0 0.0 collective-permute-done.refs_1_
  24.0 0.0 copy-start.1
  24.0 0.6 copy-done.1
  24.6 13.9 %head.1 = (bf16[512,4096]{1,0:T(8,128)(2,1)}, bf16[512,4096]{1,0:T(8,128)(2,1)}, f32[512,1024]{1,0:T(8,128)}, bf16[32,4096]{1,0:T(8,128)(2,1)}, f32[1,4096]{1,0:T(1,128)}) custom-call(s32[3]{0:T(128)} %pad_add_fusion.offset_ref, bf16[5120,32]{1,0:T(8,128)(2,1)} %points.1.points_ref, f32[3,2048]{1,0:T(4,128)} %copy-done, f32[3,2048]{1,0:T(4,128)} %copy-done.1, ...), custom_call_target="tpu_custom_call" | custom-call | flops 10000000000 | bytes 16777216 | tf_op jit(solution)/shard_map/head/pallas_call | solution.py:411
  38.5 29.3 %factor.1 = (f32[512,512]{1,0:T(8,128)}, f32[512,512]{1,0:T(8,128)}, f32[512,512]{1,0:T(8,128)}) custom-call(f32[512,1024]{1,0:T(8,128)} %get-tuple-element.10.system_ref, f32[1,512]{1,0:T(1,128)} %fusion.2.first_prior_ref), custom_call_target="tpu_custom_call" | custom-call | tf_op jit(solution)/shard_map/factor/pallas_call | solution.py:427
  67.8 60.8 %schur.1 = f32[4096,512]{1,0:T(8,128)} custom-call(s32[3]{0:T(128)} %pad_add_fusion.offset_ref, bf16[5120,32]{1,0:T(8,128)(2,1)} %points.1.points_ref, f32[1,4096]{1,0:T(1,128)} %get-tuple-element.12.log_weights, bf16[32,4096]{1,0:T(8,128)(2,1)} %get-tuple-element.13.area_features_ref, f32[1,512]{1,0:T(1,128)} %bitcast.13, ...), custom_call_target="tpu_custom_call" | custom-call | tf_op jit(solution)/shard_map/schur/pallas_call | solution.py:440
  (1 shorter events, 0.0 us)
Async XLA Ops:
  0.6 10.6 %collective-permute-start.3 = (f32[1,512]{1,0:T(1,128)}, f32[1,512]{1,0:T(1,128)S(1)}, u32[]{:S(2)}, u32[]{:S(2)}) collective-permute-start(f32[1,512]{1,0:T(1,128)} %bitcast.9), channel_id=1, source_target_pairs={{0,3},{4,7},{8,11},{12,15},{16,19},{20,23},{24,27},{28,31}} | collective-permute-start | bytes 6152 | tf_op jit(solution)/shard_map/ppermute | solution.py:378
  4.9 6.3 %collective-permute-start.2 = (f32[1,512]{1,0:T(1,128)}, f32[1,512]{1,0:T(1,128)S(1)}, u32[]{:S(2)}, u32[]{:S(2)}) collective-permute-start(f32[1,512]{1,0:T(1,128)} %bitcast.10), channel_id=1, source_target_pairs={{0,2},{4,6},{8,10},{12,14},{16,18},{20,22},{24,26},{28,30}} | collective-permute-start | bytes 6152 | tf_op jit(solution)/shard_map/ppermute | solution.py:378
  6.2 5.0 %collective-permute-start.1 = (f32[1,512]{1,0:T(1,128)}, f32[1,512]{1,0:T(1,128)S(1)}, u32[]{:S(2)}, u32[]{:S(2)}) collective-permute-start(f32[1,512]{1,0:T(1,128)} %bitcast.11), channel_id=1, source_target_pairs={{0,1},{4,5},{8,9},{12,13},{16,17},{20,21},{24,25},{28,29}} | collective-permute-start | bytes 6152 | tf_op jit(solution)/shard_map/ppermute | solution.py:378
  8.3 15.1 %copy-start = (f32[3,2048]{1,0:T(4,128)}, f32[3,2048]{1,0:T(4,128)S(1)}, u32[]{:S(2)}) copy-start(f32[3,2048]{1,0:T(4,128)S(1)} %pad_maximum_fusion.refs_0_) | copy-start | bytes 73732
  8.3 15.7 %collective-permute-start = (f32[3,2048]{1,0:T(4,128)S(1)}, f32[3,2048]{1,0:T(4,128)S(1)}, u32[]{:S(2)}, u32[]{:S(2)}) collective-permute-start(f32[3,2048]{1,0:T(4,128)S(1)} %pad_maximum_fusion.refs_0_), channel_id=1, source_target_pairs={{0,16},{16,0},{1,17},{17,1},{2,18},{18,2},{3,19},{19,3},{4,20},{20... | collective-permute-start | bytes 73736 | tf_op jit(solution)/shard_map/ppermute | solution.py:371
  11.2 12.1 %collective-permute-start.6 = (f32[1,512]{1,0:T(1,128)S(1)}, f32[1,512]{1,0:T(1,128)S(1)}, u32[]{:S(2)}, u32[]{:S(2)}) collective-permute-start(f32[1,512]{1,0:T(1,128)S(1)} %add_add_fusion), channel_id=1, source_target_pairs={{0,12},{1,13},{2,14},{3,15},{16,28},{17,29},{18,30},{19,31}} | collective-permute-start | bytes 6152 | tf_op jit(solution)/shard_map/ppermute | solution.py:378
  16.7 6.6 %collective-permute-start.5 = (f32[1,512]{1,0:T(1,128)S(1)}, f32[1,512]{1,0:T(1,128)S(1)}, u32[]{:S(2)}, u32[]{:S(2)}) collective-permute-start(f32[1,512]{1,0:T(1,128)S(1)} %add_add_fusion), channel_id=1, source_target_pairs={{0,8},{1,9},{2,10},{3,11},{16,24},{17,25},{18,26},{19,27}} | collective-permute-start | bytes 6152 | tf_op jit(solution)/shard_map/ppermute | solution.py:378
  18.0 5.3 %collective-permute-start.4 = (f32[1,512]{1,0:T(1,128)S(1)}, f32[1,512]{1,0:T(1,128)S(1)}, u32[]{:S(2)}, u32[]{:S(2)}) collective-permute-start(f32[1,512]{1,0:T(1,128)S(1)} %add_add_fusion), channel_id=1, source_target_pairs={{0,4},{1,5},{2,6},{3,7},{16,20},{17,21},{18,22},{19,23}} | collective-permute-start | bytes 6152 | tf_op jit(solution)/shard_map/ppermute | solution.py:378
  24.0 0.6 copy-start.1

commit v6 on v5

--- a/solution.py
+++ b/solution.py
@@ -11,10 +11,12 @@
 NB = 512
 LANES = 128
 STRIP = 8
+GROUP = 2
 PANEL = 4
 BLK = 128
 CHUNK = 1024
 SPAN = 512
+PIECE = 256
 VMEM_BYTES = 60 * 1024 * 1024
 HIGH = lax.Precision.HIGHEST
 F32 = jnp.float32
@@ -129,21 +131,32 @@
     )(offsets, order.reshape(quotients, LANES), inducer_xy)
 
 
-def fill_kernel(dest, points, area_features, log_weights, first, count):
-    for start in range(0, count, 256):
-        lanes = pl.ds(first + start, 256)
-        squares = jnp.dot(points, area_features[:, lanes], preferred_element_type=F32)
-        weights = [
-            jnp.broadcast_to(log_weights[0:1, pl.ds(first + start + half, LANES)], (16, LANES))
-            for half in (0, LANES)
-        ]
-        for row in range(0, points.shape[0], 16):
-            for half in range(2):
-                square = jnp.maximum(
-                    squares[row : row + 16, half * LANES : (half + 1) * LANES], 1e-30
-                )
-                value = jnp.exp2(weights[half] - square * lax.rsqrt(square))
-                dest[row : row + 16, pl.ds(first + start + half * LANES, LANES)] = value.astype(BF16)
+def rsqrt_root(square):
+    square = jnp.maximum(square, 1e-30)
+    return square * lax.rsqrt(square)
+
+
+def plain_root(square):
+    return jnp.sqrt(jnp.maximum(square, 0.0))
+
+
+def squared_distances(points, area_features, first):
+    return jnp.dot(points, area_features[:, pl.ds(first, PIECE)], preferred_element_type=F32)
+
+
+def kernel_values(dest, squares, log_weights, first, root):
+    for half in range(0, PIECE, LANES):
+        lanes = pl.ds(first + half, LANES)
+        weights = jnp.broadcast_to(log_weights[0:1, lanes], (16, LANES))
+        for row in range(0, squares.shape[0], 16):
+            distance = root(squares[row : row + 16, half : half + LANES])
+            dest[row : row + 16, lanes] = jnp.exp2(weights - distance).astype(BF16)
+
+
+def fill_kernel(dest, points, area_features, log_weights, first, count, root=rsqrt_root):
+    for start in range(0, count, PIECE):
+        squares = squared_distances(points, area_features, first + start)
+        kernel_values(dest, squares, log_weights, first + start, root)
 
 
 def head_kernel(
@@ -173,9 +186,9 @@
     def step(index, carry):
         first = pl.multiple_of(index * CHUNK, CHUNK)
         here = pl.ds(first, CHUNK)
-        fill_kernel(head_ref, points_ref[:NB, :], area_features_ref, log_weights, first, CHUNK)
+        fill_kernel(head_ref, points_ref[:NB, :], area_features_ref, log_weights, first, CHUNK, plain_root)
         fill_kernel(
-            cols_ref, points_ref[NB : NB + col_width, :], area_features_ref, log_weights, first, CHUNK
+            cols_ref, points_ref[NB : NB + col_width, :], area_features_ref, log_weights, first, CHUNK, plain_root
         )
         left = head_ref[:, here]
         system_ref[:, :NB] += nt_dot(left, left)
@@ -203,46 +216,57 @@
     lane_ids = lax.broadcasted_iota(jnp.int32, (STRIP, LANES), 1)
     tops = [block_ref[i * STRIP : (i + 1) * STRIP, :] for i in range(count)]
     units = [jnp.where(lane_ids == row_ids + i * STRIP, 1.0, 0.0).astype(F32) for i in range(count)]
-    for p in range(count):
-        panel_end = (p // PANEL + 1) * PANEL
-        diag_cols = [whole_lane(tops[p], p * STRIP + j) for j in range(STRIP)]
-        entry = {
-            (i, j): whole_row(diag_cols[j], i) for j in range(STRIP) for i in range(j, STRIP)
-        }
-        top_rows = [whole_row(tops[p], j) for j in range(STRIP)]
-        unit_rows = [whole_row(units[p], j) for j in range(STRIP)]
-        roots = []
-        for j in range(STRIP):
-            root = lax.rsqrt(entry[j, j])
-            roots.append(root)
-            for i in range(j + 1, STRIP):
+    width = GROUP * STRIP
+    for first in range(0, count, GROUP):
+        panel_end = (first // PANEL + 1) * PANEL
+        base = first * STRIP
+        entry, top_rows, unit_rows, roots = {}, [], [], []
+        for a in range(GROUP):
+            for j in range((a + 1) * STRIP):
+                column = whole_lane(tops[first + a], base + j)
+                for i in range(max(j, a * STRIP), (a + 1) * STRIP):
+                    entry[i, j] = whole_row(column, i - a * STRIP)
+            top_rows += [whole_row(tops[first + a], r) for r in range(STRIP)]
+            unit_rows += [whole_row(units[first + a], r) for r in range(STRIP)]
+        for j in range(0, width, 2):
+            corner, side, other = entry[j, j], entry[j + 1, j], entry[j + 1, j + 1]
+            root = lax.rsqrt(corner)
+            next_root = lax.rsqrt(corner * other - side * side) * (corner * root)
+            roots += [root, next_root]
+            side = side * root
+            entry[j + 1, j] = side
+            for i in range(j + 2, width):
                 entry[i, j] = entry[i, j] * root
-            for k in range(j + 1, STRIP):
-                for i in range(k, STRIP):
-                    entry[i, k] = entry[i, k] - entry[i, j] * entry[k, j]
-        for j in range(STRIP):
+                entry[i, j + 1] = (entry[i, j + 1] - entry[i, j] * side) * next_root
+            for k in range(j + 2, width):
+                for i in range(k, width):
+                    entry[i, k] = entry[i, k] - (
+                        entry[i, j] * entry[k, j] + entry[i, j + 1] * entry[k, j + 1]
+                    )
+        for j in range(width):
             for k in range(j):
                 top_rows[j] = top_rows[j] - entry[j, k] * top_rows[k]
                 unit_rows[j] = unit_rows[j] - entry[j, k] * unit_rows[k]
             top_rows[j] = top_rows[j] * roots[j]
             unit_rows[j] = unit_rows[j] * roots[j]
-        for i in range(p + 1, panel_end):
-            cols = [whole_lane(tops[i], p * STRIP + j) for j in range(STRIP)]
+        for i in range(first + GROUP, panel_end):
+            cols = [whole_lane(tops[i], base + j) for j in range(width)]
             top, unit = tops[i], units[i]
-            for j in range(STRIP):
+            for j in range(width):
                 for k in range(j):
                     cols[j] = cols[j] - cols[k] * entry[j, k]
                 cols[j] = cols[j] * roots[j]
                 top = top - cols[j] * top_rows[j]
                 unit = unit - cols[j] * unit_rows[j]
             tops[i], units[i] = top, unit
-        top, unit = top_rows[STRIP - 1], unit_rows[STRIP - 1]
-        for j in range(STRIP - 1):
-            top = jnp.where(row_ids == j, top_rows[j], top)
-            unit = jnp.where(row_ids == j, unit_rows[j], unit)
-        tops[p], units[p] = top, unit
-        inverse_ref[p * STRIP : (p + 1) * STRIP, :] = unit
-        if p + 1 == panel_end and panel_end < count:
+        for a in range(GROUP):
+            top, unit = top_rows[(a + 1) * STRIP - 1], unit_rows[(a + 1) * STRIP - 1]
+            for r in range(STRIP - 1):
+                top = jnp.where(row_ids == r, top_rows[a * STRIP + r], top)
+                unit = jnp.where(row_ids == r, unit_rows[a * STRIP + r], unit)
+            tops[first + a], units[first + a] = top, unit
+            inverse_ref[(first + a) * STRIP : (first + a + 1) * STRIP, :] = unit
+        if first + GROUP == panel_end and panel_end < count:
             panel = slice(panel_end - PANEL, panel_end)
             top = jnp.concatenate(tops[panel], axis=0)
             both = jnp.concatenate([top, jnp.concatenate(units[panel], axis=0)], axis=1)
@@ -336,17 +360,32 @@
         if dest is not None:
             next_row = pl.multiple_of(first_points + (tile + 1) * tile_rows, 16)
             points = points_ref[pl.ds(next_row, tile_rows), :]
-        out_ref[...] = jnp.zeros_like(out_ref)
-
-        def step(index, carry):
-            first = pl.multiple_of(index * SPAN, SPAN)
-            here = pl.ds(first, SPAN)
-            out_ref[...] += jnp.dot(source[:, here], residual[here, :], preferred_element_type=F32)
+        halves = max(1, col_width // 256)
+        wide = col_width // halves
+        pieces = [(first, half * wide) for first in range(0, total, SPAN) for half in range(halves)]
+        stride = total // len(pieces)
+        squares = None
+        if dest is not None:
+            squares = [squared_distances(points, area_features_ref, start) for start in range(0, stride, PIECE)]
+        for index, (first, column) in enumerate(pieces):
+            start = index * stride
+            later = None
+            if dest is not None and index + 1 < len(pieces):
+                later = [
+                    squared_distances(points, area_features_ref, start + stride + more)
+                    for more in range(0, stride, PIECE)
+                ]
+            lanes = slice(column, column + wide)
+            part = jnp.dot(
+                source[:, first : first + SPAN],
+                residual[first : first + SPAN, lanes],
+                preferred_element_type=F32,
+            )
+            out_ref[:, lanes] = part if first == 0 else out_ref[:, lanes] + part
             if dest is not None:
-                fill_kernel(dest, points, area_features_ref, log_weights, first, SPAN)
-            return carry
-
-        lax.fori_loop(0, total // SPAN, step, 0)
+                for more in range(0, stride, PIECE):
+                    kernel_values(dest, squares[more // PIECE], log_weights, start + more, rsqrt_root)
+            squares = later
 
     parity = lax.rem(tile, 2)
     more = tile < tiles - 1

time: 129 us -> 117 us (0.907)
  Pallas kernels: 108 us -> 95.8 us
    pallas_call x1, Pallas kernels: 60.8 us -> 42.7 us  [per_device(): pl.pallas_call(functools.partial(schur_kernel, factor), grid=(row_height...]
    pallas_call x1, Pallas kernels: 13.9 us -> 17.3 us  [per_device(): pl.pallas_call(functools.partial(head_kernel, factor, scale, center), out...]
    pallas_call x1, Pallas kernels: 29.3 us -> 31.8 us  [per_device(): pl.pallas_call(factor_kernel, out_shape=(jax.ShapeDtypeStruct((NB, col_wi...]
where the time goes in v6:
time: 117 us; the launch traced here: 116 us
  Pallas kernels  95.8 us (82%)
  starting transfers between devices  16.5 us (14%)
  other arithmetic  2.69 us (2%)
    pallas_call x1, Pallas kernels, per_device(): pl.pallas_call(functools.partial(schur_kernel, factor), grid=(row_height...  42.7 us
    pallas_call x1, Pallas kernels, per_device(): pl.pallas_call(factor_kernel, out_shape=(jax.ShapeDtypeStruct((NB, col_wi...  31.8 us
    pallas_call x1, Pallas kernels, per_device(): pl.pallas_call(functools.partial(head_kernel, factor, scale, center), out...  17.3 us
    ppermute x6, starting transfers between devices, from_first(): total = total + lax.ppermute(array, axis, [(0, target)])  15 us
    pallas_call x1, Pallas kernels, gram_points(): pl.pallas_call(functools.partial(points_kernel, scale, center, col_width)...  4.03 us
  transfers between devices with their start and end apart: 7, of which 0 were waited for; matrix products, arithmetic and copies ran while one was open for 2% of the time, Pallas kernels for 3%

profile of v6, /device:TPU:0, one launch (start us, length us, event | category | flops | bytes accessed | tf_op | source)
XLA Modules:
  0.0 116.4 jit_solution(11032691798990270829)
XLA Ops:
  0.6 4.3 %collective-permute-start.3 = (f32[1,512]{1,0:T(1,128)}, f32[1,512]{1,0:T(1,128)S(1)}, u32[]{:S(2)}, u32[]{:S(2)}) collective-permute-start(f32[1,512]{1,0:T(1,128)} %bitcast.9), channel_id=1, source_target_pairs={{0,3},{4,7},{8,11},{12,15},{16,19},{20,23},{24,27},{28,31}} | collective-permute-start | bytes 6152 | tf_op jit(solution)/shard_map/ppermute | solution.py:417
  4.9 1.3 %collective-permute-start.2 = (f32[1,512]{1,0:T(1,128)}, f32[1,512]{1,0:T(1,128)S(1)}, u32[]{:S(2)}, u32[]{:S(2)}) collective-permute-start(f32[1,512]{1,0:T(1,128)} %bitcast.10), channel_id=1, source_target_pairs={{0,2},{4,6},{8,10},{12,14},{16,18},{20,22},{24,26},{28,30}} | collective-permute-start | bytes 6152 | tf_op jit(solution)/shard_map/ppermute | solution.py:417
  6.2 1.3 %collective-permute-start.1 = (f32[1,512]{1,0:T(1,128)}, f32[1,512]{1,0:T(1,128)S(1)}, u32[]{:S(2)}, u32[]{:S(2)}) collective-permute-start(f32[1,512]{1,0:T(1,128)} %bitcast.11), channel_id=1, source_target_pairs={{0,1},{4,5},{8,9},{12,13},{16,17},{20,21},{24,25},{28,29}} | collective-permute-start | bytes 6152 | tf_op jit(solution)/shard_map/ppermute | solution.py:417
  7.5 0.8 pad_maximum_fusion.refs_0_
  8.3 0.0 copy-start
  8.3 1.6 %collective-permute-start = (f32[3,2048]{1,0:T(4,128)S(1)}, f32[3,2048]{1,0:T(4,128)S(1)}, u32[]{:S(2)}, u32[]{:S(2)}) collective-permute-start(f32[3,2048]{1,0:T(4,128)S(1)} %pad_maximum_fusion.refs_0_), channel_id=1, source_target_pairs={{0,16},{16,0},{1,17},{17,1},{2,18},{18,2},{3,19},{19,3},{4,20},{20... | collective-permute-start | bytes 73736 | tf_op jit(solution)/shard_map/ppermute | solution.py:410
  9.9 0.7 broadcast_select_fusion.1
  10.6 0.6 pad_add_fusion.offset_ref
  11.2 0.0 collective-permute-done.3
  11.2 0.0 collective-permute-done.2
  11.2 0.0 collective-permute-done.1
  11.2 5.5 %collective-permute-start.6 = (f32[1,512]{1,0:T(1,128)S(1)}, f32[1,512]{1,0:T(1,128)S(1)}, u32[]{:S(2)}, u32[]{:S(2)}) collective-permute-start(f32[1,512]{1,0:T(1,128)S(1)} %add_add_fusion), channel_id=1, source_target_pairs={{0,12},{1,13},{2,14},{3,15},{16,28},{17,29},{18,30},{19,31}} | collective-permute-start | bytes 6152 | tf_op jit(solution)/shard_map/ppermute | solution.py:417
  16.7 1.3 %collective-permute-start.5 = (f32[1,512]{1,0:T(1,128)S(1)}, f32[1,512]{1,0:T(1,128)S(1)}, u32[]{:S(2)}, u32[]{:S(2)}) collective-permute-start(f32[1,512]{1,0:T(1,128)S(1)} %add_add_fusion), channel_id=1, source_target_pairs={{0,8},{1,9},{2,10},{3,11},{16,24},{17,25},{18,26},{19,27}} | collective-permute-start | bytes 6152 | tf_op jit(solution)/shard_map/ppermute | solution.py:417
  18.0 1.3 %collective-permute-start.4 = (f32[1,512]{1,0:T(1,128)S(1)}, f32[1,512]{1,0:T(1,128)S(1)}, u32[]{:S(2)}, u32[]{:S(2)}) collective-permute-start(f32[1,512]{1,0:T(1,128)S(1)} %add_add_fusion), channel_id=1, source_target_pairs={{0,4},{1,5},{2,6},{3,7},{16,20},{17,21},{18,22},{19,23}} | collective-permute-start | bytes 6152 | tf_op jit(solution)/shard_map/ppermute | solution.py:417
  19.3 4.0 %points.1.points_ref = bf16[5120,32]{1,0:T(8,128)(2,1)} custom-call(s32[3]{0:T(128)} %pad_add_fusion.offset_ref, s32[64,128]{1,0:T(8,128)} %bitcast.14, f32[2,8192]{1,0:T(2,128)} %table_ref.1), custom_call_target="tpu_custom_call" | custom-call | flops 5000000000 | bytes 1048576 | tf_op jit(solution)/shard_map/points/pallas_call | solution.py:113
  23.4 0.0 copy-done
  23.4 0.0 collective-permute-done.6
  23.4 0.0 collective-permute-done.5
  23.4 0.0 collective-permute-done.4
  23.4 0.6 fusion.2.first_prior_ref
  24.0 0.0 collective-permute-done.refs_1_
  24.0 0.0 copy-start.1
  24.0 0.6 copy-done.1
  24.6 17.3 %head.1 = (bf16[512,4096]{1,0:T(8,128)(2,1)}, bf16[512,4096]{1,0:T(8,128)(2,1)}, f32[512,1024]{1,0:T(8,128)}, bf16[32,4096]{1,0:T(8,128)(2,1)}, f32[1,4096]{1,0:T(1,128)}) custom-call(s32[3]{0:T(128)} %pad_add_fusion.offset_ref, bf16[5120,32]{1,0:T(8,128)(2,1)} %points.1.points_ref, f32[3,2048]{1,0:T(4,128)} %copy-done, f32[3,2048]{1,0:T(4,128)} %copy-done.1, ...), custom_call_target="tpu_custom_call" | custom-call | flops 10000000000 | bytes 16777216 | tf_op jit(solution)/shard_map/head/pallas_call | solution.py:450
  41.9 31.8 %factor.1 = (f32[512,512]{1,0:T(8,128)}, f32[512,512]{1,0:T(8,128)}, f32[512,512]{1,0:T(8,128)}) custom-call(f32[512,1024]{1,0:T(8,128)} %get-tuple-element.10.system_ref, f32[1,512]{1,0:T(1,128)} %fusion.2.first_prior_ref), custom_call_target="tpu_custom_call" | custom-call | tf_op jit(solution)/shard_map/factor/pallas_call | solution.py:466
  73.7 42.7 %schur.1 = f32[4096,512]{1,0:T(8,128)} custom-call(s32[3]{0:T(128)} %pad_add_fusion.offset_ref, bf16[5120,32]{1,0:T(8,128)(2,1)} %points.1.points_ref, f32[1,4096]{1,0:T(1,128)} %get-tuple-element.12.log_weights, bf16[32,4096]{1,0:T(8,128)(2,1)} %get-tuple-element.13.area_features_ref, f32[1,512]{1,0:T(1,128)} %bitcast.13, ...), custom_call_target="tpu_custom_call" | custom-call | tf_op jit(solution)/shard_map/schur/pallas_call | solution.py:479
  (1 shorter events, 0.0 us)
Async XLA Ops:
  0.6 10.6 %collective-permute-start.3 = (f32[1,512]{1,0:T(1,128)}, f32[1,512]{1,0:T(1,128)S(1)}, u32[]{:S(2)}, u32[]{:S(2)}) collective-permute-start(f32[1,512]{1,0:T(1,128)} %bitcast.9), channel_id=1, source_target_pairs={{0,3},{4,7},{8,11},{12,15},{16,19},{20,23},{24,27},{28,31}} | collective-permute-start | bytes 6152 | tf_op jit(solution)/shard_map/ppermute | solution.py:417
  4.9 6.3 %collective-permute-start.2 = (f32[1,512]{1,0:T(1,128)}, f32[1,512]{1,0:T(1,128)S(1)}, u32[]{:S(2)}, u32[]{:S(2)}) collective-permute-start(f32[1,512]{1,0:T(1,128)} %bitcast.10), channel_id=1, source_target_pairs={{0,2},{4,6},{8,10},{12,14},{16,18},{20,22},{24,26},{28,30}} | collective-permute-start | bytes 6152 | tf_op jit(solution)/shard_map/ppermute | solution.py:417
  6.2 5.0 %collective-permute-start.1 = (f32[1,512]{1,0:T(1,128)}, f32[1,512]{1,0:T(1,128)S(1)}, u32[]{:S(2)}, u32[]{:S(2)}) collective-permute-start(f32[1,512]{1,0:T(1,128)} %bitcast.11), channel_id=1, source_target_pairs={{0,1},{4,5},{8,9},{12,13},{16,17},{20,21},{24,25},{28,29}} | collective-permute-start | bytes 6152 | tf_op jit(solution)/shard_map/ppermute | solution.py:417
  8.3 15.1 %copy-start = (f32[3,2048]{1,0:T(4,128)}, f32[3,2048]{1,0:T(4,128)S(1)}, u32[]{:S(2)}) copy-start(f32[3,2048]{1,0:T(4,128)S(1)} %pad_maximum_fusion.refs_0_) | copy-start | bytes 73732
  8.3 15.7 %collective-permute-start = (f32[3,2048]{1,0:T(4,128)S(1)}, f32[3,2048]{1,0:T(4,128)S(1)}, u32[]{:S(2)}, u32[]{:S(2)}) collective-permute-start(f32[3,2048]{1,0:T(4,128)S(1)} %pad_maximum_fusion.refs_0_), channel_id=1, source_target_pairs={{0,16},{16,0},{1,17},{17,1},{2,18},{18,2},{3,19},{19,3},{4,20},{20... | collective-permute-start | bytes 73736 | tf_op jit(solution)/shard_map/ppermute | solution.py:410
  11.2 12.1 %collective-permute-start.6 = (f32[1,512]{1,0:T(1,128)S(1)}, f32[1,512]{1,0:T(1,128)S(1)}, u32[]{:S(2)}, u32[]{:S(2)}) collective-permute-start(f32[1,512]{1,0:T(1,128)S(1)} %add_add_fusion), channel_id=1, source_target_pairs={{0,12},{1,13},{2,14},{3,15},{16,28},{17,29},{18,30},{19,31}} | collective-permute-start | bytes 6152 | tf_op jit(solution)/shard_map/ppermute | solution.py:417
  16.7 6.6 %collective-permute-start.5 = (f32[1,512]{1,0:T(1,128)S(1)}, f32[1,512]{1,0:T(1,128)S(1)}, u32[]{:S(2)}, u32[]{:S(2)}) collective-permute-start(f32[1,512]{1,0:T(1,128)S(1)} %add_add_fusion), channel_id=1, source_target_pairs={{0,8},{1,9},{2,10},{3,11},{16,24},{17,25},{18,26},{19,27}} | collective-permute-start | bytes 6152 | tf_op jit(solution)/shard_map/ppermute | solution.py:417
  18.0 5.3 %collective-permute-start.4 = (f32[1,512]{1,0:T(1,128)S(1)}, f32[1,512]{1,0:T(1,128)S(1)}, u32[]{:S(2)}, u32[]{:S(2)}) collective-permute-start(f32[1,512]{1,0:T(1,128)S(1)} %add_add_fusion), channel_id=1, source_target_pairs={{0,4},{1,5},{2,6},{3,7},{16,20},{17,21},{18,22},{19,23}} | collective-permute-start | bytes 6152 | tf_op jit(solution)/shard_map/ppermute | solution.py:417
  24.0 0.6 copy-start.1

commit v7 on v6

--- a/solution.py
+++ b/solution.py
@@ -11,11 +11,11 @@
 NB = 512
 LANES = 128
 STRIP = 8
-GROUP = 2
+GROUP = 1
 PANEL = 4
 BLK = 128
 CHUNK = 1024
-SPAN = 512
+SPAN = 1024
 PIECE = 256
 VMEM_BYTES = 60 * 1024 * 1024
 HIGH = lax.Precision.HIGHEST
@@ -41,6 +41,16 @@
     return lax.dot_general(
         left, right, (((0,), (0,)), ((), ())), precision=precision, preferred_element_type=F32
     )
+
+
+def stack_left(value, axis):
+    a, b, c = split_pieces(value)
+    return jnp.concatenate([a, a, b, b, a, c], axis=axis)
+
+
+def stack_right(value):
+    a, b, c = split_pieces(value)
+    return jnp.concatenate([a, b, a, b, c, a], axis=0)
 
 
 def block_position():
@@ -131,20 +141,16 @@
     )(offsets, order.reshape(quotients, LANES), inducer_xy)
 
 
-def rsqrt_root(square):
+def root(square):
     square = jnp.maximum(square, 1e-30)
     return square * lax.rsqrt(square)
 
 
-def plain_root(square):
-    return jnp.sqrt(jnp.maximum(square, 0.0))
-
-
 def squared_distances(points, area_features, first):
     return jnp.dot(points, area_features[:, pl.ds(first, PIECE)], preferred_element_type=F32)
 
 
-def kernel_values(dest, squares, log_weights, first, root):
+def kernel_values(dest, squares, log_weights, first):
     for half in range(0, PIECE, LANES):
         lanes = pl.ds(first + half, LANES)
         weights = jnp.broadcast_to(log_weights[0:1, lanes], (16, LANES))
@@ -153,10 +159,10 @@
             dest[row : row + 16, lanes] = jnp.exp2(weights - distance).astype(BF16)
 
 
-def fill_kernel(dest, points, area_features, log_weights, first, count, root=rsqrt_root):
+def fill_kernel(dest, points, area_features, log_weights, first, count):
     for start in range(0, count, PIECE):
         squares = squared_distances(points, area_features, first + start)
-        kernel_values(dest, squares, log_weights, first + start, root)
+        kernel_values(dest, squares, log_weights, first + start)
 
 
 def head_kernel(
@@ -182,20 +188,33 @@
         log_weights[:, lanes] = -0.5 * jnp.log2(0.5 + values[2:3])
     area_features_ref[...] = features[...].astype(BF16)
     system_ref[...] = jnp.zeros_like(system_ref)
+    group = min(4096, total)
 
     def step(index, carry):
-        first = pl.multiple_of(index * CHUNK, CHUNK)
-        here = pl.ds(first, CHUNK)
-        fill_kernel(head_ref, points_ref[:NB, :], area_features_ref, log_weights, first, CHUNK, plain_root)
-        fill_kernel(
-            cols_ref, points_ref[NB : NB + col_width, :], area_features_ref, log_weights, first, CHUNK, plain_root
-        )
-        left = head_ref[:, here]
-        system_ref[:, :NB] += nt_dot(left, left)
-        system_ref[:, NB:] += nt_dot(left, cols_ref[:, here])
+        base = pl.multiple_of(index * group, group)
+        targets = [(head_ref, points_ref[:NB, :]), (cols_ref, points_ref[NB : NB + col_width, :])]
+
+        def distances(start):
+            return [squared_distances(points, area_features_ref, base + start) for _, points in targets]
+
+        def accumulate(start):
+            here = pl.ds(base + start, CHUNK)
+            left = head_ref[:, here]
+            system_ref[:, :NB] += nt_dot(left, left)
+            system_ref[:, NB:] += nt_dot(left, cols_ref[:, here])
+
+        squares = distances(0)
+        for start in range(0, group, PIECE):
+            later = distances(start + PIECE) if start + PIECE < group else None
+            if start and start % CHUNK == 0:
+                accumulate(start - CHUNK)
+            for (dest, _), square in zip(targets, squares):
+                kernel_values(dest, square, log_weights, base + start)
+            squares = later
+        accumulate(group - CHUNK)
         return carry
 
-    lax.fori_loop(0, total // CHUNK, step, 0)
+    lax.fori_loop(0, total // group, step, 0)
     system_ref[:, :NB] = system_ref[:, :NB] * factor
     rows = lax.broadcasted_iota(jnp.int32, (NB, col_width), 0)
     cols = lax.broadcasted_iota(jnp.int32, (NB, col_width), 1) + offset_ref[0]
@@ -277,7 +296,7 @@
                 units[i] = units[i] - update[mine, LANES:]
 
 
-def factor_kernel(system_ref, first_prior_ref, panel_ref, solved_ref, weighted_ref, work, block, inverses):
+def factor_kernel(system_ref, first_prior_ref, panel_ref, solved_ref, weighted_ref, work, block, inverses, right):
     count = NB // BLK
     rows = lax.broadcasted_iota(jnp.int32, (NB, NB), 0)
     cols = lax.broadcasted_iota(jnp.int32, (NB, NB), 1)
@@ -288,13 +307,17 @@
     def eliminate(k, carry):
         block[...] = work[k, :, pl.ds(pl.multiple_of(k * BLK, BLK), BLK)]
         inverse_factor(block, inverses.at[k])
-        row = jnp.dot(inverses[k], work[k], precision=HIGH, preferred_element_type=F32)
+        row = jnp.dot(
+            stack_left(inverses[k], 1), stack_right(work[k]), preferred_element_type=F32
+        )
         work[k] = row
+        right[...] = stack_right(row)
         for i in range(1, count):
 
             @pl.when(i > k)
             def _():
-                work[i] -= tn_dot(row[:, i * BLK : (i + 1) * BLK], row, HIGH)
+                left = stack_left(row[:, i * BLK : (i + 1) * BLK].T, 1)
+                work[i] -= jnp.dot(left, right[...], preferred_element_type=F32)
 
         return carry
 
@@ -305,12 +328,13 @@
         panel_ref[mine, :] = panel
         if k < count - 1:
             panel = panel - jnp.dot(
-                work[k, :, (k + 1) * BLK : NB],
-                solved_ref[(k + 1) * BLK :, :],
-                precision=HIGH,
+                stack_left(work[k, :, (k + 1) * BLK : NB], 1),
+                stack_right(solved_ref[(k + 1) * BLK :, :]),
                 preferred_element_type=F32,
             )
-        solved_ref[mine, :] = tn_dot(inverses[k], panel, HIGH)
+        solved_ref[mine, :] = jnp.dot(
+            stack_left(inverses[k].T, 1), stack_right(panel), preferred_element_type=F32
+        )
     column = jnp.sum(diagonal, axis=1, keepdims=True)
     weighted_ref[...] = solved_ref[...] * column
 
@@ -342,14 +366,16 @@
     @pl.when(tile == 0)
     def _():
         points = points_ref[first_points : first_points + tile_rows, :]
-        high = solved_ref[...].astype(BF16)
-        low = (solved_ref[...] - high.astype(F32)).astype(BF16)
+        transposed = solved_ref[...].T
+        high = transposed.astype(BF16)
+        low = (transposed - high.astype(F32)).astype(BF16)
 
         def step(index, carry):
             first = pl.multiple_of(index * CHUNK, CHUNK)
             here = pl.ds(first, CHUNK)
             right = head_ref[:, here]
-            removed = tn_dot(high, right) + tn_dot(low, right)
+            removed = jnp.dot(high, right, preferred_element_type=F32)
+            removed += jnp.dot(low, right, preferred_element_type=F32)
             residual[here, :] = (cols_ref[:, here].astype(F32) - removed).astype(BF16).T
             fill_kernel(left_even, points, area_features_ref, log_weights, first, CHUNK)
             return carry
@@ -384,7 +410,7 @@
             out_ref[:, lanes] = part if first == 0 else out_ref[:, lanes] + part
             if dest is not None:
                 for more in range(0, stride, PIECE):
-                    kernel_values(dest, squares[more // PIECE], log_weights, start + more, rsqrt_root)
+                    kernel_values(dest, squares[more // PIECE], log_weights, start + more)
             squares = later
 
     parity = lax.rem(tile, 2)
@@ -472,6 +498,7 @@
             pltpu.VMEM((NB // BLK, BLK, NB + col_width), F32),
             pltpu.VMEM((BLK, BLK), F32),
             pltpu.VMEM((NB // BLK, BLK, BLK), F32),
+            pltpu.VMEM((6 * BLK, NB + col_width), BF16),
         ],
         compiler_params=params,
         name="factor",

time: 117 us -> 108 us (0.923)
  Pallas kernels: 95.8 us -> 87.2 us
    pallas_call x1, Pallas kernels: 31.8 us -> 26.6 us  [per_device(): pl.pallas_call(factor_kernel, out_shape=(jax.ShapeDtypeStruct((NB, col_wi...]
    pallas_call x1, Pallas kernels: 17.3 us -> 12.8 us  [per_device(): pl.pallas_call(functools.partial(head_kernel, factor, scale, center), out...]
  transfers between devices with their start and end apart: 7 -> 7, of which waited for: 0 -> 0; matrix products, arithmetic and copies ran while one was open for 2% -> 2% of each run, Pallas kernels for 3% -> 4%
where the time goes in v7:
time: 108 us
  Pallas kernels  87.2 us (81%)
  starting transfers between devices  16.5 us (15%)
  other arithmetic  2.69 us (2%)
    pallas_call x1, Pallas kernels, per_device(): pl.pallas_call(functools.partial(schur_kernel, factor), grid=(row_height...  43.7 us
    pallas_call x1, Pallas kernels, per_device(): pl.pallas_call(factor_kernel, out_shape=(jax.ShapeDtypeStruct((NB, col_wi...  26.6 us
    ppermute x6, starting transfers between devices, from_first(): total = total + lax.ppermute(array, axis, [(0, target)])  15 us
    pallas_call x1, Pallas kernels, per_device(): pl.pallas_call(functools.partial(head_kernel, factor, scale, center), out...  12.8 us
    pallas_call x1, Pallas kernels, gram_points(): pl.pallas_call(functools.partial(points_kernel, scale, center, col_width)...  4.03 us
  transfers between devices with their start and end apart: 7, of which 0 were waited for; matrix products, arithmetic and copies ran while one was open for 2% of the time, Pallas kernels for 4%

profile of v7, /device:TPU:0, one launch (start us, length us, event | category | flops | bytes accessed | tf_op | source)
XLA Modules:
  0.0 107.8 jit_solution(8910307124177889862)
XLA Ops:
  0.6 4.3 %collective-permute-start.3 = (f32[1,512]{1,0:T(1,128)}, f32[1,512]{1,0:T(1,128)S(1)}, u32[]{:S(2)}, u32[]{:S(2)}) collective-permute-start(f32[1,512]{1,0:T(1,128)} %bitcast.9), channel_id=1, source_target_pairs={{0,3},{4,7},{8,11},{12,15},{16,19},{20,23},{24,27},{28,31}} | collective-permute-start | bytes 6152 | tf_op jit(solution)/shard_map/ppermute | solution.py:443
  4.9 1.3 %collective-permute-start.2 = (f32[1,512]{1,0:T(1,128)}, f32[1,512]{1,0:T(1,128)S(1)}, u32[]{:S(2)}, u32[]{:S(2)}) collective-permute-start(f32[1,512]{1,0:T(1,128)} %bitcast.10), channel_id=1, source_target_pairs={{0,2},{4,6},{8,10},{12,14},{16,18},{20,22},{24,26},{28,30}} | collective-permute-start | bytes 6152 | tf_op jit(solution)/shard_map/ppermute | solution.py:443
  6.2 1.3 %collective-permute-start.1 = (f32[1,512]{1,0:T(1,128)}, f32[1,512]{1,0:T(1,128)S(1)}, u32[]{:S(2)}, u32[]{:S(2)}) collective-permute-start(f32[1,512]{1,0:T(1,128)} %bitcast.11), channel_id=1, source_target_pairs={{0,1},{4,5},{8,9},{12,13},{16,17},{20,21},{24,25},{28,29}} | collective-permute-start | bytes 6152 | tf_op jit(solution)/shard_map/ppermute | solution.py:443
  7.5 0.8 pad_maximum_fusion.refs_0_
  8.3 0.0 copy-start
  8.3 1.6 %collective-permute-start = (f32[3,2048]{1,0:T(4,128)S(1)}, f32[3,2048]{1,0:T(4,128)S(1)}, u32[]{:S(2)}, u32[]{:S(2)}) collective-permute-start(f32[3,2048]{1,0:T(4,128)S(1)} %pad_maximum_fusion.refs_0_), channel_id=1, source_target_pairs={{0,16},{16,0},{1,17},{17,1},{2,18},{18,2},{3,19},{19,3},{4,20},{20... | collective-permute-start | bytes 73736 | tf_op jit(solution)/shard_map/ppermute | solution.py:436
  9.9 0.7 broadcast_select_fusion.1
  10.6 0.6 pad_add_fusion.offset_ref
  11.2 0.0 collective-permute-done.3
  11.2 0.0 collective-permute-done.2
  11.2 0.0 collective-permute-done.1
  11.2 5.5 %collective-permute-start.6 = (f32[1,512]{1,0:T(1,128)S(1)}, f32[1,512]{1,0:T(1,128)S(1)}, u32[]{:S(2)}, u32[]{:S(2)}) collective-permute-start(f32[1,512]{1,0:T(1,128)S(1)} %add_add_fusion), channel_id=1, source_target_pairs={{0,12},{1,13},{2,14},{3,15},{16,28},{17,29},{18,30},{19,31}} | collective-permute-start | bytes 6152 | tf_op jit(solution)/shard_map/ppermute | solution.py:443
  16.7 1.3 %collective-permute-start.5 = (f32[1,512]{1,0:T(1,128)S(1)}, f32[1,512]{1,0:T(1,128)S(1)}, u32[]{:S(2)}, u32[]{:S(2)}) collective-permute-start(f32[1,512]{1,0:T(1,128)S(1)} %add_add_fusion), channel_id=1, source_target_pairs={{0,8},{1,9},{2,10},{3,11},{16,24},{17,25},{18,26},{19,27}} | collective-permute-start | bytes 6152 | tf_op jit(solution)/shard_map/ppermute | solution.py:443
  18.0 1.3 %collective-permute-start.4 = (f32[1,512]{1,0:T(1,128)S(1)}, f32[1,512]{1,0:T(1,128)S(1)}, u32[]{:S(2)}, u32[]{:S(2)}) collective-permute-start(f32[1,512]{1,0:T(1,128)S(1)} %add_add_fusion), channel_id=1, source_target_pairs={{0,4},{1,5},{2,6},{3,7},{16,20},{17,21},{18,22},{19,23}} | collective-permute-start | bytes 6152 | tf_op jit(solution)/shard_map/ppermute | solution.py:443
  19.3 4.0 %points.1.points_ref = bf16[5120,32]{1,0:T(8,128)(2,1)} custom-call(s32[3]{0:T(128)} %pad_add_fusion.offset_ref, s32[64,128]{1,0:T(8,128)} %bitcast.14, f32[2,8192]{1,0:T(2,128)} %table_ref.1), custom_call_target="tpu_custom_call" | custom-call | flops 5000000000 | bytes 1048576 | tf_op jit(solution)/shard_map/points/pallas_call | solution.py:123
  23.4 0.0 copy-done
  23.4 0.0 collective-permute-done.6
  23.4 0.0 collective-permute-done.5
  23.4 0.0 collective-permute-done.4
  23.4 0.6 fusion.2.first_prior_ref
  24.0 0.0 collective-permute-done.refs_1_
  24.0 0.0 copy-start.1
  24.0 0.6 copy-done.1
  24.6 12.8 %head.1 = (bf16[512,4096]{1,0:T(8,128)(2,1)}, bf16[512,4096]{1,0:T(8,128)(2,1)}, f32[512,1024]{1,0:T(8,128)}, bf16[32,4096]{1,0:T(8,128)(2,1)}, f32[1,4096]{1,0:T(1,128)}) custom-call(s32[3]{0:T(128)} %pad_add_fusion.offset_ref, bf16[5120,32]{1,0:T(8,128)(2,1)} %points.1.points_ref, f32[3,2048]{1,0:T(4,128)} %copy-done, f32[3,2048]{1,0:T(4,128)} %copy-done.1, ...), custom_call_target="tpu_custom_call" | custom-call | flops 10000000000 | bytes 16777216 | tf_op jit(solution)/shard_map/head/pallas_call | solution.py:476
  37.5 26.6 %factor.1 = (f32[512,512]{1,0:T(8,128)}, f32[512,512]{1,0:T(8,128)}, f32[512,512]{1,0:T(8,128)}) custom-call(f32[512,1024]{1,0:T(8,128)} %get-tuple-element.10.system_ref, f32[1,512]{1,0:T(1,128)} %fusion.2.first_prior_ref), custom_call_target="tpu_custom_call" | custom-call | tf_op jit(solution)/shard_map/factor/pallas_call | solution.py:492
  64.1 43.7 %schur.1 = f32[4096,512]{1,0:T(8,128)} custom-call(s32[3]{0:T(128)} %pad_add_fusion.offset_ref, bf16[5120,32]{1,0:T(8,128)(2,1)} %points.1.points_ref, f32[1,4096]{1,0:T(1,128)} %get-tuple-element.12.log_weights, bf16[32,4096]{1,0:T(8,128)(2,1)} %get-tuple-element.13.area_features_ref, f32[1,512]{1,0:T(1,128)} %bitcast.13, ...), custom_call_target="tpu_custom_call" | custom-call | tf_op jit(solution)/shard_map/schur/pallas_call | solution.py:506
  (1 shorter events, 0.0 us)
Async XLA Ops:
  0.6 10.6 %collective-permute-start.3 = (f32[1,512]{1,0:T(1,128)}, f32[1,512]{1,0:T(1,128)S(1)}, u32[]{:S(2)}, u32[]{:S(2)}) collective-permute-start(f32[1,512]{1,0:T(1,128)} %bitcast.9), channel_id=1, source_target_pairs={{0,3},{4,7},{8,11},{12,15},{16,19},{20,23},{24,27},{28,31}} | collective-permute-start | bytes 6152 | tf_op jit(solution)/shard_map/ppermute | solution.py:443
  4.9 6.3 %collective-permute-start.2 = (f32[1,512]{1,0:T(1,128)}, f32[1,512]{1,0:T(1,128)S(1)}, u32[]{:S(2)}, u32[]{:S(2)}) collective-permute-start(f32[1,512]{1,0:T(1,128)} %bitcast.10), channel_id=1, source_target_pairs={{0,2},{4,6},{8,10},{12,14},{16,18},{20,22},{24,26},{28,30}} | collective-permute-start | bytes 6152 | tf_op jit(solution)/shard_map/ppermute | solution.py:443
  6.2 5.0 %collective-permute-start.1 = (f32[1,512]{1,0:T(1,128)}, f32[1,512]{1,0:T(1,128)S(1)}, u32[]{:S(2)}, u32[]{:S(2)}) collective-permute-start(f32[1,512]{1,0:T(1,128)} %bitcast.11), channel_id=1, source_target_pairs={{0,1},{4,5},{8,9},{12,13},{16,17},{20,21},{24,25},{28,29}} | collective-permute-start | bytes 6152 | tf_op jit(solution)/shard_map/ppermute | solution.py:443
  8.3 15.1 %copy-start = (f32[3,2048]{1,0:T(4,128)}, f32[3,2048]{1,0:T(4,128)S(1)}, u32[]{:S(2)}) copy-start(f32[3,2048]{1,0:T(4,128)S(1)} %pad_maximum_fusion.refs_0_) | copy-start | bytes 73732
  8.3 15.7 %collective-permute-start = (f32[3,2048]{1,0:T(4,128)S(1)}, f32[3,2048]{1,0:T(4,128)S(1)}, u32[]{:S(2)}, u32[]{:S(2)}) collective-permute-start(f32[3,2048]{1,0:T(4,128)S(1)} %pad_maximum_fusion.refs_0_), channel_id=1, source_target_pairs={{0,16},{16,0},{1,17},{17,1},{2,18},{18,2},{3,19},{19,3},{4,20},{20... | collective-permute-start | bytes 73736 | tf_op jit(solution)/shard_map/ppermute | solution.py:436
  11.2 12.1 %collective-permute-start.6 = (f32[1,512]{1,0:T(1,128)S(1)}, f32[1,512]{1,0:T(1,128)S(1)}, u32[]{:S(2)}, u32[]{:S(2)}) collective-permute-start(f32[1,512]{1,0:T(1,128)S(1)} %add_add_fusion), channel_id=1, source_target_pairs={{0,12},{1,13},{2,14},{3,15},{16,28},{17,29},{18,30},{19,31}} | collective-permute-start | bytes 6152 | tf_op jit(solution)/shard_map/ppermute | solution.py:443
  16.7 6.6 %collective-permute-start.5 = (f32[1,512]{1,0:T(1,128)S(1)}, f32[1,512]{1,0:T(1,128)S(1)}, u32[]{:S(2)}, u32[]{:S(2)}) collective-permute-start(f32[1,512]{1,0:T(1,128)S(1)} %add_add_fusion), channel_id=1, source_target_pairs={{0,8},{1,9},{2,10},{3,11},{16,24},{17,25},{18,26},{19,27}} | collective-permute-start | bytes 6152 | tf_op jit(solution)/shard_map/ppermute | solution.py:443
  18.0 5.3 %collective-permute-start.4 = (f32[1,512]{1,0:T(1,128)S(1)}, f32[1,512]{1,0:T(1,128)S(1)}, u32[]{:S(2)}, u32[]{:S(2)}) collective-permute-start(f32[1,512]{1,0:T(1,128)S(1)} %add_add_fusion), channel_id=1, source_target_pairs={{0,4},{1,5},{2,6},{3,7},{16,20},{17,21},{18,22},{19,23}} | collective-permute-start | bytes 6152 | tf_op jit(solution)/shard_map/ppermute | solution.py:443
  24.0 0.6 copy-start.1

commit v8 on v7

--- a/solution.py
+++ b/solution.py
@@ -15,7 +15,7 @@
 PANEL = 4
 BLK = 128
 CHUNK = 1024
-SPAN = 1024
+SPAN = 512
 PIECE = 256
 VMEM_BYTES = 60 * 1024 * 1024
 HIGH = lax.Precision.HIGHEST
@@ -296,39 +296,41 @@
                 units[i] = units[i] - update[mine, LANES:]
 
 
-def factor_kernel(system_ref, first_prior_ref, panel_ref, solved_ref, weighted_ref, work, block, inverses, right):
+def factor_kernel(system_ref, first_prior_ref, panel_ref, solved_ref, weighted_ref, block, inverses, right):
     count = NB // BLK
     rows = lax.broadcasted_iota(jnp.int32, (NB, NB), 0)
     cols = lax.broadcasted_iota(jnp.int32, (NB, NB), 1)
     diagonal = jnp.where(rows == cols, first_prior_ref[...], 0.0)
-    work[:, :, :NB] = (system_ref[:, :NB] + diagonal).reshape(count, BLK, NB)
-    work[:, :, NB:] = system_ref[:, NB:].reshape(count, BLK, panel_ref.shape[1])
+    system_ref[:, :NB] = system_ref[:, :NB] + diagonal
 
     def eliminate(k, carry):
-        block[...] = work[k, :, pl.ds(pl.multiple_of(k * BLK, BLK), BLK)]
+        mine = pl.ds(pl.multiple_of(k * BLK, BLK), BLK)
+        block[...] = system_ref[mine, mine]
         inverse_factor(block, inverses.at[k])
         row = jnp.dot(
-            stack_left(inverses[k], 1), stack_right(work[k]), preferred_element_type=F32
+            stack_left(inverses[k], 1), stack_right(system_ref[mine, :]), preferred_element_type=F32
         )
-        work[k] = row
+        system_ref[mine, :] = row
         right[...] = stack_right(row)
         for i in range(1, count):
 
             @pl.when(i > k)
             def _():
                 left = stack_left(row[:, i * BLK : (i + 1) * BLK].T, 1)
-                work[i] -= jnp.dot(left, right[...], preferred_element_type=F32)
+                system_ref[i * BLK : (i + 1) * BLK, :] -= jnp.dot(
+                    left, right[...], preferred_element_type=F32
+                )
 
         return carry
 
     lax.fori_loop(0, count, eliminate, 0)
     for k in range(count - 1, -1, -1):
         mine = pl.ds(k * BLK, BLK)
-        panel = work[k, :, NB:]
+        panel = system_ref[mine, NB:]
         panel_ref[mine, :] = panel
         if k < count - 1:
             panel = panel - jnp.dot(
-                stack_left(work[k, :, (k + 1) * BLK : NB], 1),
+                stack_left(system_ref[mine, (k + 1) * BLK : NB], 1),
                 stack_right(solved_ref[(k + 1) * BLK :, :]),
                 preferred_element_type=F32,
             )
@@ -359,7 +361,6 @@
     tiles = pl.num_programs(0)
     col_width = cols_ref.shape[0]
     total = log_weights.shape[1]
-    steps = total // CHUNK
     first_points = NB + col_width
     tile_rows = out_ref.shape[0]
 
@@ -370,17 +371,26 @@
         high = transposed.astype(BF16)
         low = (transposed - high.astype(F32)).astype(BF16)
 
+        group = min(4096, total)
+
         def step(index, carry):
-            first = pl.multiple_of(index * CHUNK, CHUNK)
-            here = pl.ds(first, CHUNK)
-            right = head_ref[:, here]
-            removed = jnp.dot(high, right, preferred_element_type=F32)
-            removed += jnp.dot(low, right, preferred_element_type=F32)
-            residual[here, :] = (cols_ref[:, here].astype(F32) - removed).astype(BF16).T
-            fill_kernel(left_even, points, area_features_ref, log_weights, first, CHUNK)
+            base = pl.multiple_of(index * group, group)
+            squares = squared_distances(points, area_features_ref, base)
+            for start in range(0, group, PIECE):
+                later = None
+                if start + PIECE < group:
+                    later = squared_distances(points, area_features_ref, base + start + PIECE)
+                if start % SPAN == 0:
+                    here = pl.ds(base + start, SPAN)
+                    right = head_ref[:, here]
+                    removed = jnp.dot(high, right, preferred_element_type=F32)
+                    removed += jnp.dot(low, right, preferred_element_type=F32)
+                    residual[here, :] = (cols_ref[:, here].astype(F32) - removed).astype(BF16).T
+                kernel_values(left_even, squares, log_weights, base + start)
+                squares = later
             return carry
 
-        lax.fori_loop(0, steps, step, 0)
+        lax.fori_loop(0, total // group, step, 0)
 
     def run(source, dest):
         if dest is not None:
@@ -431,6 +441,26 @@
         out_ref[...] -= weighted_ref[pl.ds(pl.multiple_of(first_row, tile_rows), tile_rows), :]
 
 
+def whole_kernel(factor, scale, center, offset_ref, points_ref, *refs):
+    areas, rest = refs[:-18], refs[-18:]
+    prior_ref, first_prior_ref, panel_ref, out_ref = rest[:4]
+    head, cols, system, area_features, log_weights, features = rest[4:10]
+    block, inverses, right, solved, weighted = rest[10:15]
+
+    @pl.when(pl.program_id(0) == 0)
+    def _():
+        head_kernel(
+            factor, scale, center, offset_ref, points_ref, *areas, prior_ref,
+            head, cols, system, area_features, log_weights, features,
+        )
+        factor_kernel(system, first_prior_ref, panel_ref, solved, weighted, block, inverses, right)
+
+    schur_kernel(
+        factor, offset_ref, points_ref, log_weights, area_features, prior_ref,
+        head, cols, solved, weighted, out_ref, *rest[15:],
+    )
+
+
 def all_areas(array):
     if lax.axis_size("area") == 2:
         return [array, lax.ppermute(array, "area", [(0, 1), (1, 0)])]
@@ -469,54 +499,39 @@
     ).astype(jnp.int32)
 
     points = gram_points(offsets, order, inducer_xy, scale, center, col_width, row_height)
-    tile_rows = min(row_height, 512 if areas_total <= 8192 else 256)
+    tile_rows = min(row_height, 512 if areas_total <= 8192 else 128)
     smem = pl.BlockSpec(memory_space=pltpu.SMEM)
     vmem = pl.BlockSpec(memory_space=pltpu.VMEM)
     params = pltpu.CompilerParams(vmem_limit_bytes=VMEM_BYTES)
-    head, cols, system, area_features, log_weights = pl.pallas_call(
-        functools.partial(head_kernel, factor, scale, center),
+    panel_rows, schur = pl.pallas_call(
+        functools.partial(whole_kernel, factor, scale, center),
+        grid=(row_height // tile_rows,),
         out_shape=(
-            jax.ShapeDtypeStruct((NB, areas_total), BF16),
-            jax.ShapeDtypeStruct((col_width, areas_total), BF16),
-            jax.ShapeDtypeStruct((NB, NB + col_width), F32),
-            jax.ShapeDtypeStruct((FEATURES, areas_total), BF16),
-            jax.ShapeDtypeStruct((1, areas_total), F32),
+            jax.ShapeDtypeStruct((NB, col_width), F32),
+            jax.ShapeDtypeStruct((row_height, col_width), F32),
         ),
-        in_specs=[smem] + [vmem] * (2 + len(areas)),
-        out_specs=[vmem] * 5,
-        cost_estimate=pl.CostEstimate(flops=10**10, bytes_accessed=2**24, transcendentals=0),
-        scratch_shapes=[pltpu.VMEM((FEATURES, areas_total), F32)],
-        compiler_params=params,
-        name="head",
-    )(offsets, points, *areas, own_prior)
-    panel_rows, solved, weighted = pl.pallas_call(
-        factor_kernel,
-        out_shape=(jax.ShapeDtypeStruct((NB, col_width), F32),) * 3,
-        in_specs=[vmem] * 2,
-        out_specs=[vmem] * 3,
+        in_specs=[smem] + [vmem] * (3 + len(areas)),
+        out_specs=[vmem, pl.BlockSpec((tile_rows, col_width), lambda i: (i, 0))],
         scratch_shapes=[
-            pltpu.VMEM((NB // BLK, BLK, NB + col_width), F32),
+            pltpu.VMEM((NB, areas_total), BF16),
+            pltpu.VMEM((col_width, areas_total), BF16),
+            pltpu.VMEM((NB, NB + col_width), F32),
+            pltpu.VMEM((FEATURES, areas_total), BF16),
+            pltpu.VMEM((1, areas_total), F32),
+            pltpu.VMEM((FEATURES, areas_total), F32),
             pltpu.VMEM((BLK, BLK), F32),
             pltpu.VMEM((NB // BLK, BLK, BLK), F32),
             pltpu.VMEM((6 * BLK, NB + col_width), BF16),
-        ],
-        compiler_params=params,
-        name="factor",
-    )(system, first_prior)
-    schur = pl.pallas_call(
-        functools.partial(schur_kernel, factor),
-        grid=(row_height // tile_rows,),
-        out_shape=jax.ShapeDtypeStruct((row_height, col_width), F32),
-        in_specs=[smem] + [vmem] * 8,
-        out_specs=pl.BlockSpec((tile_rows, col_width), lambda i: (i, 0)),
-        scratch_shapes=[
+            pltpu.VMEM((NB, col_width), F32),
+            pltpu.VMEM((NB, col_width), F32),
             pltpu.VMEM((tile_rows, areas_total), BF16),
             pltpu.VMEM((tile_rows, areas_total), BF16),
             pltpu.VMEM((areas_total, col_width), BF16),
         ],
         compiler_params=params,
+        cost_estimate=pl.CostEstimate(flops=5 * 10**10, bytes_accessed=2**24, transcendentals=0),
         name="schur",
-    )(offsets, points, log_weights, area_features, own_prior, head, cols, solved, weighted)
+    )(offsets, points, *areas, own_prior, first_prior)
     return (panel_rows, schur)
 
 

time: 108 us -> 94.6 us (0.88)
  Pallas kernels: 87.2 us -> 73.7 us
    pallas_call x3 -> x1, Pallas kernels: 83.1 us -> 69.8 us  [per_device(): pl.pallas_call(functools.partial(whole_kernel, factor, scale, center), gr...]
  transfers between devices with their start and end apart: 7 -> 7, of which waited for: 0 -> 0; matrix products, arithmetic and copies ran while one was open for 2% -> 3% of each run, Pallas kernels for 4% -> 4%
where the time goes in v8:
time: 94.6 us; the launch traced here: 94.2 us
  Pallas kernels  73.7 us (78%)
  starting transfers between devices  16.5 us (17%)
  other arithmetic  2.61 us (3%)
    pallas_call x1, Pallas kernels, per_device(): pl.pallas_call(functools.partial(whole_kernel, factor, scale, center), gr...  69.8 us
    ppermute x6, starting transfers between devices, from_first(): total = total + lax.ppermute(array, axis, [(0, target)])  15 us
    pallas_call x1, Pallas kernels, gram_points(): pl.pallas_call(functools.partial(points_kernel, scale, center, col_width)...  3.94 us
  transfers between devices with their start and end apart: 7, of which 0 were waited for; matrix products, arithmetic and copies ran while one was open for 3% of the time, Pallas kernels for 4%

profile of v8, /device:TPU:0, one launch (start us, length us, event | category | flops | bytes accessed | tf_op | source)
XLA Modules:
  0.0 94.2 jit_solution(11989668830072369547)
XLA Ops:
  0.6 4.3 %collective-permute-start.3 = (f32[1,512]{1,0:T(1,128)}, f32[1,512]{1,0:T(1,128)S(1)}, u32[]{:S(2)}, u32[]{:S(2)}) collective-permute-start(f32[1,512]{1,0:T(1,128)} %bitcast.9), channel_id=1, source_target_pairs={{0,3},{4,7},{8,11},{12,15},{16,19},{20,23},{24,27},{28,31}} | collective-permute-start | bytes 6152 | tf_op jit(solution)/shard_map/ppermute | solution.py:473
  4.9 1.3 %collective-permute-start.2 = (f32[1,512]{1,0:T(1,128)}, f32[1,512]{1,0:T(1,128)S(1)}, u32[]{:S(2)}, u32[]{:S(2)}) collective-permute-start(f32[1,512]{1,0:T(1,128)} %bitcast.10), channel_id=1, source_target_pairs={{0,2},{4,6},{8,10},{12,14},{16,18},{20,22},{24,26},{28,30}} | collective-permute-start | bytes 6152 | tf_op jit(solution)/shard_map/ppermute | solution.py:473
  6.2 1.3 %collective-permute-start.1 = (f32[1,512]{1,0:T(1,128)}, f32[1,512]{1,0:T(1,128)S(1)}, u32[]{:S(2)}, u32[]{:S(2)}) collective-permute-start(f32[1,512]{1,0:T(1,128)} %bitcast.11), channel_id=1, source_target_pairs={{0,1},{4,5},{8,9},{12,13},{16,17},{20,21},{24,25},{28,29}} | collective-permute-start | bytes 6152 | tf_op jit(solution)/shard_map/ppermute | solution.py:473
  7.5 0.8 pad_maximum_fusion.refs_0_
  8.3 0.0 copy-start
  8.3 1.6 %collective-permute-start = (f32[3,2048]{1,0:T(4,128)S(1)}, f32[3,2048]{1,0:T(4,128)S(1)}, u32[]{:S(2)}, u32[]{:S(2)}) collective-permute-start(f32[3,2048]{1,0:T(4,128)S(1)} %pad_maximum_fusion.refs_0_), channel_id=1, source_target_pairs={{0,16},{16,0},{1,17},{17,1},{2,18},{18,2},{3,19},{19,3},{4,20},{20... | collective-permute-start | bytes 73736 | tf_op jit(solution)/shard_map/ppermute | solution.py:466
  9.9 0.7 broadcast_select_fusion.1
  10.6 0.6 pad_add_fusion.offset_ref
  11.1 0.0 collective-permute-done.3
  11.1 0.0 collective-permute-done.2
  11.2 0.0 collective-permute-done.1
  11.2 5.5 %collective-permute-start.6 = (f32[1,512]{1,0:T(1,128)S(1)}, f32[1,512]{1,0:T(1,128)S(1)}, u32[]{:S(2)}, u32[]{:S(2)}) collective-permute-start(f32[1,512]{1,0:T(1,128)S(1)} %add_add_fusion), channel_id=1, source_target_pairs={{0,12},{1,13},{2,14},{3,15},{16,28},{17,29},{18,30},{19,31}} | collective-permute-start | bytes 6152 | tf_op jit(solution)/shard_map/ppermute | solution.py:473
  16.7 1.3 %collective-permute-start.5 = (f32[1,512]{1,0:T(1,128)S(1)}, f32[1,512]{1,0:T(1,128)S(1)}, u32[]{:S(2)}, u32[]{:S(2)}) collective-permute-start(f32[1,512]{1,0:T(1,128)S(1)} %add_add_fusion), channel_id=1, source_target_pairs={{0,8},{1,9},{2,10},{3,11},{16,24},{17,25},{18,26},{19,27}} | collective-permute-start | bytes 6152 | tf_op jit(solution)/shard_map/ppermute | solution.py:473
  18.0 1.3 %collective-permute-start.4 = (f32[1,512]{1,0:T(1,128)S(1)}, f32[1,512]{1,0:T(1,128)S(1)}, u32[]{:S(2)}, u32[]{:S(2)}) collective-permute-start(f32[1,512]{1,0:T(1,128)S(1)} %add_add_fusion), channel_id=1, source_target_pairs={{0,4},{1,5},{2,6},{3,7},{16,20},{17,21},{18,22},{19,23}} | collective-permute-start | bytes 6152 | tf_op jit(solution)/shard_map/ppermute | solution.py:473
  19.3 3.9 %points.1.points_ref = bf16[5120,32]{1,0:T(8,128)(2,1)} custom-call(s32[3]{0:T(128)} %pad_add_fusion.offset_ref, s32[64,128]{1,0:T(8,128)} %bitcast.13, f32[2,8192]{1,0:T(2,128)} %table_ref.1), custom_call_target="tpu_custom_call" | custom-call | flops 5000000000 | bytes 1048576 | tf_op jit(solution)/shard_map/points/pallas_call | solution.py:123
  23.2 0.0 copy-done
  23.2 0.0 collective-permute-done.6
  23.2 0.0 collective-permute-done.5
  23.2 0.0 collective-permute-done.4
  23.2 0.6 fusion.2.refs_3_
  23.8 0.0 collective-permute-done.refs_1_
  23.8 0.0 copy-start.1
  23.8 0.6 copy-done.1
  24.4 69.8 %schur.1 = (f32[512,512]{1,0:T(8,128)}, f32[4096,512]{1,0:T(8,128)}) custom-call(s32[3]{0:T(128)} %pad_add_fusion.offset_ref, bf16[5120,32]{1,0:T(8,128)(2,1)} %points.1.points_ref, f32[3,2048]{1,0:T(4,128)} %copy-done, f32[3,2048]{1,0:T(4,128)} %copy-done.1, f32[1,512]{1,0:T(1,128)} %bitcast.12, f32[1,512]{1,0:T(1,128)} %fusion.2.refs_3_), custom_call_target="tpu_custom_call" | custom-call | flops 49999998976 | bytes 16777216 | tf_op jit(solution)/shard_map/schur/pallas_call | solution.py:506
  (1 shorter events, 0.0 us)
Async XLA Ops:
  0.6 10.5 %collective-permute-start.3 = (f32[1,512]{1,0:T(1,128)}, f32[1,512]{1,0:T(1,128)S(1)}, u32[]{:S(2)}, u32[]{:S(2)}) collective-permute-start(f32[1,512]{1,0:T(1,128)} %bitcast.9), channel_id=1, source_target_pairs={{0,3},{4,7},{8,11},{12,15},{16,19},{20,23},{24,27},{28,31}} | collective-permute-start | bytes 6152 | tf_op jit(solution)/shard_map/ppermute | solution.py:473
  4.9 6.2 %collective-permute-start.2 = (f32[1,512]{1,0:T(1,128)}, f32[1,512]{1,0:T(1,128)S(1)}, u32[]{:S(2)}, u32[]{:S(2)}) collective-permute-start(f32[1,512]{1,0:T(1,128)} %bitcast.10), channel_id=1, source_target_pairs={{0,2},{4,6},{8,10},{12,14},{16,18},{20,22},{24,26},{28,30}} | collective-permute-start | bytes 6152 | tf_op jit(solution)/shard_map/ppermute | solution.py:473
  6.2 4.9 %collective-permute-start.1 = (f32[1,512]{1,0:T(1,128)}, f32[1,512]{1,0:T(1,128)S(1)}, u32[]{:S(2)}, u32[]{:S(2)}) collective-permute-start(f32[1,512]{1,0:T(1,128)} %bitcast.11), channel_id=1, source_target_pairs={{0,1},{4,5},{8,9},{12,13},{16,17},{20,21},{24,25},{28,29}} | collective-permute-start | bytes 6152 | tf_op jit(solution)/shard_map/ppermute | solution.py:473
  8.3 14.9 %copy-start = (f32[3,2048]{1,0:T(4,128)}, f32[3,2048]{1,0:T(4,128)S(1)}, u32[]{:S(2)}) copy-start(f32[3,2048]{1,0:T(4,128)S(1)} %pad_maximum_fusion.refs_0_) | copy-start | bytes 73732
  8.3 15.5 %collective-permute-start = (f32[3,2048]{1,0:T(4,128)S(1)}, f32[3,2048]{1,0:T(4,128)S(1)}, u32[]{:S(2)}, u32[]{:S(2)}) collective-permute-start(f32[3,2048]{1,0:T(4,128)S(1)} %pad_maximum_fusion.refs_0_), channel_id=1, source_target_pairs={{0,16},{16,0},{1,17},{17,1},{2,18},{18,2},{3,19},{19,3},{4,20},{20... | collective-permute-start | bytes 73736 | tf_op jit(solution)/shard_map/ppermute | solution.py:466
  11.2 12.1 %collective-permute-start.6 = (f32[1,512]{1,0:T(1,128)S(1)}, f32[1,512]{1,0:T(1,128)S(1)}, u32[]{:S(2)}, u32[]{:S(2)}) collective-permute-start(f32[1,512]{1,0:T(1,128)S(1)} %add_add_fusion), channel_id=1, source_target_pairs={{0,12},{1,13},{2,14},{3,15},{16,28},{17,29},{18,30},{19,31}} | collective-permute-start | bytes 6152 | tf_op jit(solution)/shard_map/ppermute | solution.py:473
  16.7 6.5 %collective-permute-start.5 = (f32[1,512]{1,0:T(1,128)S(1)}, f32[1,512]{1,0:T(1,128)S(1)}, u32[]{:S(2)}, u32[]{:S(2)}) collective-permute-start(f32[1,512]{1,0:T(1,128)S(1)} %add_add_fusion), channel_id=1, source_target_pairs={{0,8},{1,9},{2,10},{3,11},{16,24},{17,25},{18,26},{19,27}} | collective-permute-start | bytes 6152 | tf_op jit(solution)/shard_map/ppermute | solution.py:473
  18.0 5.2 %collective-permute-start.4 = (f32[1,512]{1,0:T(1,128)S(1)}, f32[1,512]{1,0:T(1,128)S(1)}, u32[]{:S(2)}, u32[]{:S(2)}) collective-permute-start(f32[1,512]{1,0:T(1,128)S(1)} %add_add_fusion), channel_id=1, source_target_pairs={{0,4},{1,5},{2,6},{3,7},{16,20},{17,21},{18,22},{19,23}} | collective-permute-start | bytes 6152 | tf_op jit(solution)/shard_map/ppermute | solution.py:473
  23.8 0.6 copy-start.1

commit v9 on v8

--- a/solution.py
+++ b/solution.py
@@ -3,6 +3,7 @@
 
 import jax
 import jax.numpy as jnp
+import numpy as np
 from jax import lax
 from jax.experimental import pallas as pl
 from jax.experimental.pallas import tpu as pltpu
@@ -17,6 +18,11 @@
 CHUNK = 1024
 SPAN = 512
 PIECE = 256
+POWER_EVERY = 3
+LOWEST = -0.5 * math.log2(128.5) - 6 * math.sqrt(2) * math.log2(math.e)
+HIGHEST = -0.5 * math.log2(8.5)
+MIDDLE = (LOWEST + HIGHEST) / 2
+REACH = (HIGHEST - LOWEST) / 2 + 0.01
 VMEM_BYTES = 60 * 1024 * 1024
 HIGH = lax.Precision.HIGHEST
 F32 = jnp.float32
@@ -146,6 +152,22 @@
     return square * lax.rsqrt(square)
 
 
+def power_coefficients():
+    nodes = np.cos((np.arange(64) + 0.5) * np.pi / 64) * REACH
+    fit = np.polynomial.Chebyshev.fit(nodes, np.exp2((MIDDLE + nodes) / 16), 5, domain=[-REACH, REACH])
+    return [float(value) for value in fit.convert(kind=np.polynomial.Polynomial).coef]
+
+
+def power_of_two(offset):
+    coefficients = power_coefficients()
+    value = coefficients[-1] * offset + coefficients[-2]
+    for coefficient in coefficients[-3::-1]:
+        value = value * offset + coefficient
+    for _ in range(4):
+        value = value * value
+    return value
+
+
 def squared_distances(points, area_features, first):
     return jnp.dot(points, area_features[:, pl.ds(first, PIECE)], preferred_element_type=F32)
 
@@ -154,9 +176,14 @@
     for half in range(0, PIECE, LANES):
         lanes = pl.ds(first + half, LANES)
         weights = jnp.broadcast_to(log_weights[0:1, lanes], (16, LANES))
+        shifted = weights - MIDDLE
         for row in range(0, squares.shape[0], 16):
             distance = root(squares[row : row + 16, half : half + LANES])
-            dest[row : row + 16, lanes] = jnp.exp2(weights - distance).astype(BF16)
+            if row // 16 % POWER_EVERY == POWER_EVERY - 1:
+                value = power_of_two(shifted - distance)
+            else:
+                value = jnp.exp2(weights - distance)
+            dest[row : row + 16, lanes] = value.astype(BF16)
 
 
 def fill_kernel(dest, points, area_features, log_weights, first, count):

time: 94.6 us -> 106 us (1.12)
  Pallas kernels: 73.7 us -> 84.8 us
    pallas_call x1, Pallas kernels: 69.8 us -> 80.8 us  [per_device(): pl.pallas_call(functools.partial(whole_kernel, factor, scale, center), gr...]
  transfers between devices with their start and end apart: 7 -> 7, of which waited for: 0 -> 0; matrix products, arithmetic and copies ran while one was open for 3% -> 2% of each run, Pallas kernels for 4% -> 4%
where the time goes in v9:
time: 106 us; the launch traced here: 105 us
  Pallas kernels  84.8 us (80%)
  starting transfers between devices  16.5 us (16%)
  other arithmetic  2.61 us (2%)
    pallas_call x1, Pallas kernels, per_device(): pl.pallas_call(functools.partial(whole_kernel, factor, scale, center), gr...  80.8 us
    ppermute x6, starting transfers between devices, from_first(): total = total + lax.ppermute(array, axis, [(0, target)])  15 us
    pallas_call x1, Pallas kernels, gram_points(): pl.pallas_call(functools.partial(points_kernel, scale, center, col_width)...  3.94 us
  transfers between devices with their start and end apart: 7, of which 0 were waited for; matrix products, arithmetic and copies ran while one was open for 2% of the time, Pallas kernels for 4%

profile of v9, /device:TPU:0, one launch (start us, length us, event | category | flops | bytes accessed | tf_op | source)
XLA Modules:
  0.0 105.3 jit_solution(6089412796887537687)
XLA Ops:
  0.6 4.3 %collective-permute-start.3 = (f32[1,512]{1,0:T(1,128)}, f32[1,512]{1,0:T(1,128)S(1)}, u32[]{:S(2)}, u32[]{:S(2)}) collective-permute-start(f32[1,512]{1,0:T(1,128)} %bitcast.9), channel_id=1, source_target_pairs={{0,3},{4,7},{8,11},{12,15},{16,19},{20,23},{24,27},{28,31}} | collective-permute-start | bytes 6152 | tf_op jit(solution)/shard_map/ppermute | solution.py:500
  4.9 1.3 %collective-permute-start.2 = (f32[1,512]{1,0:T(1,128)}, f32[1,512]{1,0:T(1,128)S(1)}, u32[]{:S(2)}, u32[]{:S(2)}) collective-permute-start(f32[1,512]{1,0:T(1,128)} %bitcast.10), channel_id=1, source_target_pairs={{0,2},{4,6},{8,10},{12,14},{16,18},{20,22},{24,26},{28,30}} | collective-permute-start | bytes 6152 | tf_op jit(solution)/shard_map/ppermute | solution.py:500
  6.2 1.3 %collective-permute-start.1 = (f32[1,512]{1,0:T(1,128)}, f32[1,512]{1,0:T(1,128)S(1)}, u32[]{:S(2)}, u32[]{:S(2)}) collective-permute-start(f32[1,512]{1,0:T(1,128)} %bitcast.11), channel_id=1, source_target_pairs={{0,1},{4,5},{8,9},{12,13},{16,17},{20,21},{24,25},{28,29}} | collective-permute-start | bytes 6152 | tf_op jit(solution)/shard_map/ppermute | solution.py:500
  7.5 0.8 pad_maximum_fusion.refs_0_
  8.3 0.0 copy-start
  8.3 1.6 %collective-permute-start = (f32[3,2048]{1,0:T(4,128)S(1)}, f32[3,2048]{1,0:T(4,128)S(1)}, u32[]{:S(2)}, u32[]{:S(2)}) collective-permute-start(f32[3,2048]{1,0:T(4,128)S(1)} %pad_maximum_fusion.refs_0_), channel_id=1, source_target_pairs={{0,16},{16,0},{1,17},{17,1},{2,18},{18,2},{3,19},{19,3},{4,20},{20... | collective-permute-start | bytes 73736 | tf_op jit(solution)/shard_map/ppermute | solution.py:493
  9.9 0.7 broadcast_select_fusion.1
  10.6 0.6 pad_add_fusion.offset_ref
  11.1 0.0 collective-permute-done.3
  11.1 0.0 collective-permute-done.2
  11.2 0.0 collective-permute-done.1
  11.2 5.5 %collective-permute-start.6 = (f32[1,512]{1,0:T(1,128)S(1)}, f32[1,512]{1,0:T(1,128)S(1)}, u32[]{:S(2)}, u32[]{:S(2)}) collective-permute-start(f32[1,512]{1,0:T(1,128)S(1)} %add_add_fusion), channel_id=1, source_target_pairs={{0,12},{1,13},{2,14},{3,15},{16,28},{17,29},{18,30},{19,31}} | collective-permute-start | bytes 6152 | tf_op jit(solution)/shard_map/ppermute | solution.py:500
  16.7 1.3 %collective-permute-start.5 = (f32[1,512]{1,0:T(1,128)S(1)}, f32[1,512]{1,0:T(1,128)S(1)}, u32[]{:S(2)}, u32[]{:S(2)}) collective-permute-start(f32[1,512]{1,0:T(1,128)S(1)} %add_add_fusion), channel_id=1, source_target_pairs={{0,8},{1,9},{2,10},{3,11},{16,24},{17,25},{18,26},{19,27}} | collective-permute-start | bytes 6152 | tf_op jit(solution)/shard_map/ppermute | solution.py:500
  18.0 1.3 %collective-permute-start.4 = (f32[1,512]{1,0:T(1,128)S(1)}, f32[1,512]{1,0:T(1,128)S(1)}, u32[]{:S(2)}, u32[]{:S(2)}) collective-permute-start(f32[1,512]{1,0:T(1,128)S(1)} %add_add_fusion), channel_id=1, source_target_pairs={{0,4},{1,5},{2,6},{3,7},{16,20},{17,21},{18,22},{19,23}} | collective-permute-start | bytes 6152 | tf_op jit(solution)/shard_map/ppermute | solution.py:500
  19.3 3.9 %points.1.points_ref = bf16[5120,32]{1,0:T(8,128)(2,1)} custom-call(s32[3]{0:T(128)} %pad_add_fusion.offset_ref, s32[64,128]{1,0:T(8,128)} %bitcast.13, f32[2,8192]{1,0:T(2,128)} %table_ref.1), custom_call_target="tpu_custom_call" | custom-call | flops 5000000000 | bytes 1048576 | tf_op jit(solution)/shard_map/points/pallas_call | solution.py:129
  23.2 0.0 copy-done
  23.2 0.0 collective-permute-done.6
  23.2 0.0 collective-permute-done.5
  23.2 0.0 collective-permute-done.4
  23.2 0.6 fusion.2.refs_3_
  23.8 0.0 collective-permute-done.refs_1_
  23.8 0.0 copy-start.1
  23.8 0.6 copy-done.1
  24.4 80.8 %schur.1 = (f32[512,512]{1,0:T(8,128)}, f32[4096,512]{1,0:T(8,128)}) custom-call(s32[3]{0:T(128)} %pad_add_fusion.offset_ref, bf16[5120,32]{1,0:T(8,128)(2,1)} %points.1.points_ref, f32[3,2048]{1,0:T(4,128)} %copy-done, f32[3,2048]{1,0:T(4,128)} %copy-done.1, f32[1,512]{1,0:T(1,128)} %bitcast.12, f32[1,512]{1,0:T(1,128)} %fusion.2.refs_3_), custom_call_target="tpu_custom_call" | custom-call | flops 49999998976 | bytes 16777216 | tf_op jit(solution)/shard_map/schur/pallas_call | solution.py:533
  (1 shorter events, 0.0 us)
Async XLA Ops:
  0.6 10.5 %collective-permute-start.3 = (f32[1,512]{1,0:T(1,128)}, f32[1,512]{1,0:T(1,128)S(1)}, u32[]{:S(2)}, u32[]{:S(2)}) collective-permute-start(f32[1,512]{1,0:T(1,128)} %bitcast.9), channel_id=1, source_target_pairs={{0,3},{4,7},{8,11},{12,15},{16,19},{20,23},{24,27},{28,31}} | collective-permute-start | bytes 6152 | tf_op jit(solution)/shard_map/ppermute | solution.py:500
  4.9 6.2 %collective-permute-start.2 = (f32[1,512]{1,0:T(1,128)}, f32[1,512]{1,0:T(1,128)S(1)}, u32[]{:S(2)}, u32[]{:S(2)}) collective-permute-start(f32[1,512]{1,0:T(1,128)} %bitcast.10), channel_id=1, source_target_pairs={{0,2},{4,6},{8,10},{12,14},{16,18},{20,22},{24,26},{28,30}} | collective-permute-start | bytes 6152 | tf_op jit(solution)/shard_map/ppermute | solution.py:500
  6.2 4.9 %collective-permute-start.1 = (f32[1,512]{1,0:T(1,128)}, f32[1,512]{1,0:T(1,128)S(1)}, u32[]{:S(2)}, u32[]{:S(2)}) collective-permute-start(f32[1,512]{1,0:T(1,128)} %bitcast.11), channel_id=1, source_target_pairs={{0,1},{4,5},{8,9},{12,13},{16,17},{20,21},{24,25},{28,29}} | collective-permute-start | bytes 6152 | tf_op jit(solution)/shard_map/ppermute | solution.py:500
  8.3 14.9 %copy-start = (f32[3,2048]{1,0:T(4,128)}, f32[3,2048]{1,0:T(4,128)S(1)}, u32[]{:S(2)}) copy-start(f32[3,2048]{1,0:T(4,128)S(1)} %pad_maximum_fusion.refs_0_) | copy-start | bytes 73732
  8.3 15.5 %collective-permute-start = (f32[3,2048]{1,0:T(4,128)S(1)}, f32[3,2048]{1,0:T(4,128)S(1)}, u32[]{:S(2)}, u32[]{:S(2)}) collective-permute-start(f32[3,2048]{1,0:T(4,128)S(1)} %pad_maximum_fusion.refs_0_), channel_id=1, source_target_pairs={{0,16},{16,0},{1,17},{17,1},{2,18},{18,2},{3,19},{19,3},{4,20},{20... | collective-permute-start | bytes 73736 | tf_op jit(solution)/shard_map/ppermute | solution.py:493
  11.2 12.1 %collective-permute-start.6 = (f32[1,512]{1,0:T(1,128)S(1)}, f32[1,512]{1,0:T(1,128)S(1)}, u32[]{:S(2)}, u32[]{:S(2)}) collective-permute-start(f32[1,512]{1,0:T(1,128)S(1)} %add_add_fusion), channel_id=1, source_target_pairs={{0,12},{1,13},{2,14},{3,15},{16,28},{17,29},{18,30},{19,31}} | collective-permute-start | bytes 6152 | tf_op jit(solution)/shard_map/ppermute | solution.py:500
  16.7 6.5 %collective-permute-start.5 = (f32[1,512]{1,0:T(1,128)S(1)}, f32[1,512]{1,0:T(1,128)S(1)}, u32[]{:S(2)}, u32[]{:S(2)}) collective-permute-start(f32[1,512]{1,0:T(1,128)S(1)} %add_add_fusion), channel_id=1, source_target_pairs={{0,8},{1,9},{2,10},{3,11},{16,24},{17,25},{18,26},{19,27}} | collective-permute-start | bytes 6152 | tf_op jit(solution)/shard_map/ppermute | solution.py:500
  18.0 5.2 %collective-permute-start.4 = (f32[1,512]{1,0:T(1,128)S(1)}, f32[1,512]{1,0:T(1,128)S(1)}, u32[]{:S(2)}, u32[]{:S(2)}) collective-permute-start(f32[1,512]{1,0:T(1,128)S(1)} %add_add_fusion), channel_id=1, source_target_pairs={{0,4},{1,5},{2,6},{3,7},{16,20},{17,21},{18,22},{19,23}} | collective-permute-start | bytes 6152 | tf_op jit(solution)/shard_map/ppermute | solution.py:500
  23.8 0.6 copy-start.1

commit v10 on v8

--- a/solution.py
+++ b/solution.py
@@ -385,7 +385,8 @@
                     right = head_ref[:, here]
                     removed = jnp.dot(high, right, preferred_element_type=F32)
                     removed += jnp.dot(low, right, preferred_element_type=F32)
-                    residual[here, :] = (cols_ref[:, here].astype(F32) - removed).astype(BF16).T
+                    left = cols_ref[:, here].astype(F32) - removed
+                    residual[here, :] = (left * factor).astype(BF16).T
                 kernel_values(left_even, squares, log_weights, base + start)
                 squares = later
             return carry
@@ -430,11 +431,14 @@
     pl.when(jnp.logical_and(jnp.logical_not(more), parity == 0))(lambda: run(left_even, None))
     pl.when(jnp.logical_and(jnp.logical_not(more), parity == 1))(lambda: run(left_odd, None))
 
-    rows = lax.broadcasted_iota(jnp.int32, (tile_rows, col_width), 0) + (offset_ref[1] + tile * tile_rows)
-    cols = lax.broadcasted_iota(jnp.int32, (tile_rows, col_width), 1) + offset_ref[0]
-    out_ref[...] = out_ref[...] * factor + jnp.where(rows == cols, prior_ref[...], 0.0)
-
     first_row = offset_ref[1] + tile * tile_rows
+    first_col = offset_ref[0]
+
+    @pl.when(jnp.logical_and(first_row < first_col + col_width, first_col < first_row + tile_rows))
+    def _():
+        rows = lax.broadcasted_iota(jnp.int32, (tile_rows, col_width), 0) + first_row
+        cols = lax.broadcasted_iota(jnp.int32, (tile_rows, col_width), 1) + first_col
+        out_ref[...] += jnp.where(rows == cols, prior_ref[...], 0.0)
 
     @pl.when(first_row < NB)
     def _():

time: 94.6 us -> 93.6 us (0.989)
  Pallas kernels: 73.7 us -> 72.7 us
    pallas_call x1, Pallas kernels: 69.8 us -> 68.8 us  [per_device(): pl.pallas_call(functools.partial(whole_kernel, factor, scale, center), gr...]
where the time goes in v10:
time: 93.6 us; the launch traced here: 93.2 us
  Pallas kernels  72.7 us (78%)
  starting transfers between devices  16.5 us (18%)
  other arithmetic  2.61 us (3%)
    pallas_call x1, Pallas kernels, per_device(): pl.pallas_call(functools.partial(whole_kernel, factor, scale, center), gr...  68.8 us
    ppermute x6, starting transfers between devices, from_first(): total = total + lax.ppermute(array, axis, [(0, target)])  15 us
    pallas_call x1, Pallas kernels, gram_points(): pl.pallas_call(functools.partial(points_kernel, scale, center, col_width)...  3.94 us
  transfers between devices with their start and end apart: 7, of which 0 were waited for; matrix products, arithmetic and copies ran while one was open for 3% of the time, Pallas kernels for 4%

profile of v10, /device:TPU:0, one launch (start us, length us, event | category | flops | bytes accessed | tf_op | source)
XLA Modules:
  0.0 93.2 jit_solution(9460924951629300419)
XLA Ops:
  0.6 4.3 %collective-permute-start.3 = (f32[1,512]{1,0:T(1,128)}, f32[1,512]{1,0:T(1,128)S(1)}, u32[]{:S(2)}, u32[]{:S(2)}) collective-permute-start(f32[1,512]{1,0:T(1,128)} %bitcast.9), channel_id=1, source_target_pairs={{0,3},{4,7},{8,11},{12,15},{16,19},{20,23},{24,27},{28,31}} | collective-permute-start | bytes 6152 | tf_op jit(solution)/shard_map/ppermute | solution.py:477
  4.9 1.3 %collective-permute-start.2 = (f32[1,512]{1,0:T(1,128)}, f32[1,512]{1,0:T(1,128)S(1)}, u32[]{:S(2)}, u32[]{:S(2)}) collective-permute-start(f32[1,512]{1,0:T(1,128)} %bitcast.10), channel_id=1, source_target_pairs={{0,2},{4,6},{8,10},{12,14},{16,18},{20,22},{24,26},{28,30}} | collective-permute-start | bytes 6152 | tf_op jit(solution)/shard_map/ppermute | solution.py:477
  6.2 1.3 %collective-permute-start.1 = (f32[1,512]{1,0:T(1,128)}, f32[1,512]{1,0:T(1,128)S(1)}, u32[]{:S(2)}, u32[]{:S(2)}) collective-permute-start(f32[1,512]{1,0:T(1,128)} %bitcast.11), channel_id=1, source_target_pairs={{0,1},{4,5},{8,9},{12,13},{16,17},{20,21},{24,25},{28,29}} | collective-permute-start | bytes 6152 | tf_op jit(solution)/shard_map/ppermute | solution.py:477
  7.5 0.8 pad_maximum_fusion.refs_0_
  8.3 0.0 copy-start
  8.3 1.6 %collective-permute-start = (f32[3,2048]{1,0:T(4,128)S(1)}, f32[3,2048]{1,0:T(4,128)S(1)}, u32[]{:S(2)}, u32[]{:S(2)}) collective-permute-start(f32[3,2048]{1,0:T(4,128)S(1)} %pad_maximum_fusion.refs_0_), channel_id=1, source_target_pairs={{0,16},{16,0},{1,17},{17,1},{2,18},{18,2},{3,19},{19,3},{4,20},{20... | collective-permute-start | bytes 73736 | tf_op jit(solution)/shard_map/ppermute | solution.py:470
  9.9 0.7 broadcast_select_fusion.1
  10.6 0.6 pad_add_fusion.offset_ref
  11.1 0.0 collective-permute-done.3
  11.1 0.0 collective-permute-done.2
  11.2 0.0 collective-permute-done.1
  11.2 5.5 %collective-permute-start.6 = (f32[1,512]{1,0:T(1,128)S(1)}, f32[1,512]{1,0:T(1,128)S(1)}, u32[]{:S(2)}, u32[]{:S(2)}) collective-permute-start(f32[1,512]{1,0:T(1,128)S(1)} %add_add_fusion), channel_id=1, source_target_pairs={{0,12},{1,13},{2,14},{3,15},{16,28},{17,29},{18,30},{19,31}} | collective-permute-start | bytes 6152 | tf_op jit(solution)/shard_map/ppermute | solution.py:477
  16.7 1.3 %collective-permute-start.5 = (f32[1,512]{1,0:T(1,128)S(1)}, f32[1,512]{1,0:T(1,128)S(1)}, u32[]{:S(2)}, u32[]{:S(2)}) collective-permute-start(f32[1,512]{1,0:T(1,128)S(1)} %add_add_fusion), channel_id=1, source_target_pairs={{0,8},{1,9},{2,10},{3,11},{16,24},{17,25},{18,26},{19,27}} | collective-permute-start | bytes 6152 | tf_op jit(solution)/shard_map/ppermute | solution.py:477
  18.0 1.3 %collective-permute-start.4 = (f32[1,512]{1,0:T(1,128)S(1)}, f32[1,512]{1,0:T(1,128)S(1)}, u32[]{:S(2)}, u32[]{:S(2)}) collective-permute-start(f32[1,512]{1,0:T(1,128)S(1)} %add_add_fusion), channel_id=1, source_target_pairs={{0,4},{1,5},{2,6},{3,7},{16,20},{17,21},{18,22},{19,23}} | collective-permute-start | bytes 6152 | tf_op jit(solution)/shard_map/ppermute | solution.py:477
  19.3 3.9 %points.1.points_ref = bf16[5120,32]{1,0:T(8,128)(2,1)} custom-call(s32[3]{0:T(128)} %pad_add_fusion.offset_ref, s32[64,128]{1,0:T(8,128)} %bitcast.13, f32[2,8192]{1,0:T(2,128)} %table_ref.1), custom_call_target="tpu_custom_call" | custom-call | flops 5000000000 | bytes 1048576 | tf_op jit(solution)/shard_map/points/pallas_call | solution.py:123
  23.2 0.0 copy-done
  23.2 0.0 collective-permute-done.6
  23.2 0.0 collective-permute-done.5
  23.2 0.0 collective-permute-done.4
  23.2 0.6 fusion.2.refs_3_
  23.8 0.0 collective-permute-done.refs_1_
  23.8 0.0 copy-start.1
  23.8 0.6 copy-done.1
  24.4 68.8 %schur.1 = (f32[512,512]{1,0:T(8,128)}, f32[4096,512]{1,0:T(8,128)}) custom-call(s32[3]{0:T(128)} %pad_add_fusion.offset_ref, bf16[5120,32]{1,0:T(8,128)(2,1)} %points.1.points_ref, f32[3,2048]{1,0:T(4,128)} %copy-done, f32[3,2048]{1,0:T(4,128)} %copy-done.1, f32[1,512]{1,0:T(1,128)} %bitcast.12, f32[1,512]{1,0:T(1,128)} %fusion.2.refs_3_), custom_call_target="tpu_custom_call" | custom-call | flops 49999998976 | bytes 16777216 | tf_op jit(solution)/shard_map/schur/pallas_call | solution.py:510
  (1 shorter events, 0.0 us)
Async XLA Ops:
  0.6 10.5 %collective-permute-start.3 = (f32[1,512]{1,0:T(1,128)}, f32[1,512]{1,0:T(1,128)S(1)}, u32[]{:S(2)}, u32[]{:S(2)}) collective-permute-start(f32[1,512]{1,0:T(1,128)} %bitcast.9), channel_id=1, source_target_pairs={{0,3},{4,7},{8,11},{12,15},{16,19},{20,23},{24,27},{28,31}} | collective-permute-start | bytes 6152 | tf_op jit(solution)/shard_map/ppermute | solution.py:477
  4.9 6.2 %collective-permute-start.2 = (f32[1,512]{1,0:T(1,128)}, f32[1,512]{1,0:T(1,128)S(1)}, u32[]{:S(2)}, u32[]{:S(2)}) collective-permute-start(f32[1,512]{1,0:T(1,128)} %bitcast.10), channel_id=1, source_target_pairs={{0,2},{4,6},{8,10},{12,14},{16,18},{20,22},{24,26},{28,30}} | collective-permute-start | bytes 6152 | tf_op jit(solution)/shard_map/ppermute | solution.py:477
  6.2 4.9 %collective-permute-start.1 = (f32[1,512]{1,0:T(1,128)}, f32[1,512]{1,0:T(1,128)S(1)}, u32[]{:S(2)}, u32[]{:S(2)}) collective-permute-start(f32[1,512]{1,0:T(1,128)} %bitcast.11), channel_id=1, source_target_pairs={{0,1},{4,5},{8,9},{12,13},{16,17},{20,21},{24,25},{28,29}} | collective-permute-start | bytes 6152 | tf_op jit(solution)/shard_map/ppermute | solution.py:477
  8.3 14.9 %copy-start = (f32[3,2048]{1,0:T(4,128)}, f32[3,2048]{1,0:T(4,128)S(1)}, u32[]{:S(2)}) copy-start(f32[3,2048]{1,0:T(4,128)S(1)} %pad_maximum_fusion.refs_0_) | copy-start | bytes 73732
  8.3 15.5 %collective-permute-start = (f32[3,2048]{1,0:T(4,128)S(1)}, f32[3,2048]{1,0:T(4,128)S(1)}, u32[]{:S(2)}, u32[]{:S(2)}) collective-permute-start(f32[3,2048]{1,0:T(4,128)S(1)} %pad_maximum_fusion.refs_0_), channel_id=1, source_target_pairs={{0,16},{16,0},{1,17},{17,1},{2,18},{18,2},{3,19},{19,3},{4,20},{20... | collective-permute-start | bytes 73736 | tf_op jit(solution)/shard_map/ppermute | solution.py:470
  11.2 12.1 %collective-permute-start.6 = (f32[1,512]{1,0:T(1,128)S(1)}, f32[1,512]{1,0:T(1,128)S(1)}, u32[]{:S(2)}, u32[]{:S(2)}) collective-permute-start(f32[1,512]{1,0:T(1,128)S(1)} %add_add_fusion), channel_id=1, source_target_pairs={{0,12},{1,13},{2,14},{3,15},{16,28},{17,29},{18,30},{19,31}} | collective-permute-start | bytes 6152 | tf_op jit(solution)/shard_map/ppermute | solution.py:477
  16.7 6.5 %collective-permute-start.5 = (f32[1,512]{1,0:T(1,128)S(1)}, f32[1,512]{1,0:T(1,128)S(1)}, u32[]{:S(2)}, u32[]{:S(2)}) collective-permute-start(f32[1,512]{1,0:T(1,128)S(1)} %add_add_fusion), channel_id=1, source_target_pairs={{0,8},{1,9},{2,10},{3,11},{16,24},{17,25},{18,26},{19,27}} | collective-permute-start | bytes 6152 | tf_op jit(solution)/shard_map/ppermute | solution.py:477
  18.0 5.2 %collective-permute-start.4 = (f32[1,512]{1,0:T(1,128)S(1)}, f32[1,512]{1,0:T(1,128)S(1)}, u32[]{:S(2)}, u32[]{:S(2)}) collective-permute-start(f32[1,512]{1,0:T(1,128)S(1)} %add_add_fusion), channel_id=1, source_target_pairs={{0,4},{1,5},{2,6},{3,7},{16,20},{17,21},{18,22},{19,23}} | collective-permute-start | bytes 6152 | tf_op jit(solution)/shard_map/ppermute | solution.py:477
  23.8 0.6 copy-start.1
